TPU v7x, 32 devices: a whole 2x2x4 slice. The times are simulated.
32 devices in a mesh: pair: 2 (over y), rows: 16 (over z, x, core).
Axes of the slice: x: 2, y: 2, z: 4, core: 2. Of those that a mesh axis runs over, the one named last changes fastest.
Arguments:
- inputs: bfloat16 [2, 16, 2, 256, 1024], P(None, 'rows', 'pair'), may hold values from -6 to 6
- cotangent: bfloat16 [2, 16, 2, 256, 1024], P(None, 'rows', 'pair'), may hold values from -6 to 6
- phone_len: int32 [2, 16, 2], P(None, 'rows'), may hold values from 1 to 96, as said below
- prompt_len: int32 [2, 16, 2], P(None, 'rows'), may hold values from 32 to 191, as said below
- target_len: int32 [2, 16, 2], P(None, 'rows'), may hold values from 64 to 192, as said below
- ln1_gain: bfloat16 [1024], P(('pair', 'rows')), may hold values from 0.5 to 1.5
- ln1_bias: bfloat16 [1024], P(('pair', 'rows')), may hold values from -3 to 3
- w_qkv: bfloat16 [1024, 3072], P(('pair', 'rows')), may hold values from -0.1875 to 0.1875
- w_out: bfloat16 [1024, 1024], P(('pair', 'rows')), may hold values from -0.5 to 0.5
- ln2_gain: bfloat16 [1024], P(('pair', 'rows')), may hold values from 0.5 to 1.5
- ln2_bias: bfloat16 [1024], P(('pair', 'rows')), may hold values from -3 to 3
- w_up: bfloat16 [1024, 4096], P(('pair', 'rows')), may hold values from -0.1875 to 0.1875
- up_bias: bfloat16 [4096], P(('pair', 'rows')), may hold values from -3 to 3
- w_down: bfloat16 [4096, 1024], P(('pair', 'rows')), may hold values from -0.09375 to 0.09375
Outputs:
- outputs: bfloat16 [2, 16, 2, 256, 1024], P(None, 'rows', 'pair')
- input_grad: float32 [2, 16, 2, 256, 1024], P(None, 'rows', 'pair')
- grad_ln1_gain: float32 [1024], P(('pair', 'rows'))
- grad_ln1_bias: float32 [1024], P(('pair', 'rows'))
- grad_qkv: float32 [1024, 3072], P(('pair', 'rows'))
- grad_out: float32 [1024, 1024], P(('pair', 'rows'))
- grad_ln2_gain: float32 [1024], P(('pair', 'rows'))
- grad_ln2_bias: float32 [1024], P(('pair', 'rows'))
- grad_up: float32 [1024, 4096], P(('pair', 'rows'))
- grad_up_bias: float32 [4096], P(('pair', 'rows'))
- grad_down: float32 [4096, 1024], P(('pair', 'rows'))
Inputs may be any that keep to these rules, and one draw needn't show every extreme that they name: In each packed row, phone_len plus prompt_len summed over its 2 utterances is exactly 256, each utterance's phone_len plus prompt_len lies between 64 and 192, and phone_len is at most half of phone_len plus prompt_len. `prompt_len`: see phone_len for the row sums. `target_len`: in each packed row the target lengths of its 2 utterances sum to exactly 256.
All inputs are finite; a program needn't handle non-finite values.
Results may differ from a plain program's by a relative error of at most 0.011.
Values may be sent and summed in bfloat16 or wider, within the bound.
No kernel may reach another device: no remote copies, remote signals or barrier semaphores. Data moves between devices by JAX's collectives and lax.ppermute only.
A program may use at most 256 MiB of HBM per device.

v0:
```python
import jax
import jax.numpy as jnp
from jax import lax
from jax.sharding import PartitionSpec as P

D = 1024
HEADS = 16
HEAD = 64
ROW = 256
MICRO = 2


def passed_along(block, axis, distance):
    devices = range(lax.axis_size(axis))
    route = [(i - distance, i) for i in devices if i - distance in devices]
    return lax.ppermute(block, axis, route)


def times_transposed(left, right):
    return lax.dot_general(
        left, right, (((1,), (1,)), ((), ())), preferred_element_type=jnp.float32
    )


def transposed_times(left, right):
    return lax.dot_general(
        left, right, (((0,), (0,)), ((), ())), preferred_element_type=jnp.float32
    )


def layer_norm(values, gain, bias):
    center = values - jnp.mean(values, -1, keepdims=True)
    spread = jnp.mean(center * center, -1, keepdims=True)
    return center * lax.rsqrt(spread + 1e-05) * gain + bias


def locate(lengths, slot_ids):
    seg_ends = jnp.cumsum(lengths, dtype=jnp.int32)
    seg_ids = jnp.sum(
        (slot_ids[:, None] >= seg_ends[None, :]).astype(jnp.int32), 1, dtype=jnp.int32
    )
    one_hot = (seg_ids[:, None] == jnp.arange(lengths.shape[0], dtype=jnp.int32)[None, :]).astype(
        jnp.int32
    )
    seg_start = jnp.sum(one_hot * (seg_ends - lengths)[None, :], 1, dtype=jnp.int32)
    return (seg_ids, one_hot, slot_ids - seg_start)


def frame_meta(phone_lens, prompt_lens, target_lens, slot_count):
    slot_ids = jnp.arange(slot_count, dtype=jnp.int32)
    pre_seg, pre_hot, pre_off = locate(phone_lens + prompt_lens, slot_ids)
    pre_phone = jnp.sum(pre_hot * phone_lens[None, :], 1, dtype=jnp.int32)
    prefix = (pre_seg, pre_off < pre_phone, pre_off - pre_phone)
    tgt_seg, tgt_hot, tgt_off = locate(target_lens, slot_ids)
    tgt_pos = jnp.sum(tgt_hot * prompt_lens[None, :], 1, dtype=jnp.int32) + tgt_off
    targets = (tgt_seg, tgt_off < 0, tgt_pos)
    return (prefix, targets)


def allowed(query_meta, key_meta):
    same_seg = query_meta[0][:, None] == key_meta[0][None, :]
    audio_ok = key_meta[1][None, :] | (key_meta[2][None, :] <= query_meta[2][:, None])
    return same_seg & jnp.where(query_meta[1][:, None], key_meta[1][None, :], audio_ok)


def masked_scores(queries, key_rows, allowed_mask, score_scale):
    scores = (
        jnp.einsum("qhd,khd->hqk", queries, key_rows, preferred_element_type=jnp.float32)
        * score_scale
    )
    return jnp.where(allowed_mask[None], scores, -1e30)


def attention_forward(queries, key_rows, value_rows, allowed_mask, score_scale):
    scores = masked_scores(queries, key_rows, allowed_mask, score_scale)
    peak = jnp.max(scores, -1, keepdims=True)
    exp_scores = jnp.exp(scores - peak)
    row_total = jnp.sum(exp_scores, -1, keepdims=True)
    probs = (exp_scores / row_total).astype(jnp.bfloat16)
    mixed = jnp.einsum("hqk,khd->qhd", probs, value_rows, preferred_element_type=jnp.float32)
    return (mixed.astype(jnp.bfloat16), peak + jnp.log(row_total))


def attention_backward(
    queries, key_rows, value_rows, allowed_mask, log_total, grad_mixed, score_scale
):
    scores = masked_scores(queries, key_rows, allowed_mask, score_scale)
    probs = jnp.where(allowed_mask[None], jnp.exp(scores - log_total), 0.0)
    grad_probs = jnp.einsum(
        "qhd,khd->hqk", grad_mixed, value_rows, preferred_element_type=jnp.float32
    )
    grad_values = jnp.einsum(
        "hqk,qhd->khd", probs.astype(jnp.bfloat16), grad_mixed, preferred_element_type=jnp.float32
    )
    inner = jnp.sum(grad_probs * probs, -1, keepdims=True)
    grad_scores = (probs * (grad_probs - inner)).astype(jnp.bfloat16)
    grad_queries = (
        jnp.einsum("hqk,khd->qhd", grad_scores, key_rows, preferred_element_type=jnp.float32)
        * score_scale
    )
    grad_keys = (
        jnp.einsum("hqk,qhd->khd", grad_scores, queries, preferred_element_type=jnp.float32)
        * score_scale
    )
    return (grad_queries, grad_keys, grad_values)


def add_up(summed, fresh):
    if summed is None:
        return fresh
    return jax.tree.map(lambda summed_part, fresh_part: summed_part + fresh_part, summed, fresh)


def fetch_forward(params):
    return (
        lax.all_gather(params[0], ("pair", "rows"), axis=0, tiled=True),
        lax.all_gather(params[1], ("pair", "rows"), axis=0, tiled=True),
        lax.all_gather(params[2], ("pair", "rows"), axis=0, tiled=True),
        lax.all_gather(params[3], ("pair", "rows"), axis=0, tiled=True),
        lax.all_gather(params[4], ("pair", "rows"), axis=0, tiled=True),
        lax.all_gather(params[5], ("pair", "rows"), axis=0, tiled=True),
        lax.all_gather(params[6], ("pair", "rows"), axis=0, tiled=True),
        lax.all_gather(params[7], ("pair", "rows"), axis=0, tiled=True),
        lax.all_gather(params[8], ("pair", "rows"), axis=0, tiled=True),
    )


def shards(
    inputs,
    cotangent,
    phone_len,
    prompt_len,
    target_len,
    ln1_gain,
    ln1_bias,
    w_qkv,
    w_out,
    ln2_gain,
    ln2_bias,
    w_up,
    up_bias,
    w_down,
):
    half_index = lax.axis_index("pair")
    score_scale = HEAD ** (-0.5)
    params = (ln1_gain, ln1_bias, w_qkv, w_out, ln2_gain, ln2_bias, w_up, up_bias, w_down)
    out_blocks = []
    grad_blocks = []
    summed = None
    for batch_index in range(MICRO):
        gathered = fetch_forward(params)
        (
            gain_one,
            bias_one,
            qkv_weight,
            out_weight,
            gain_two,
            bias_two,
            up_weight,
            up_shift,
            down_weight,
        ) = gathered
        gain_one_f = gain_one.astype(jnp.float32)
        bias_one_f = bias_one.astype(jnp.float32)
        gain_two_f = gain_two.astype(jnp.float32)
        bias_two_f = bias_two.astype(jnp.float32)
        prefix, targets = frame_meta(
            phone_len[batch_index, 0], prompt_len[batch_index, 0], target_len[batch_index, 0], ROW
        )
        query_meta = tuple(
            (
                jnp.where(half_index == 0, pre_field, tgt_field)
                for pre_field, tgt_field in zip(prefix, targets)
            )
        )
        remote_mask = allowed(query_meta, prefix) & (half_index == 1)
        allowed_mask = jnp.concatenate([remote_mask, allowed(query_meta, query_meta)], 1)
        resident = inputs[batch_index, 0, 0].astype(jnp.float32)
        normed = layer_norm(resident, gain_one_f, bias_one_f).astype(jnp.bfloat16)
        qkv_rows = jnp.dot(normed, qkv_weight, preferred_element_type=jnp.float32).astype(
            jnp.bfloat16
        )
        own_kv = qkv_rows[:, D:]
        remote_kv = passed_along(own_kv, "pair", 1)
        queries = qkv_rows[:, :D].reshape(ROW, HEADS, HEAD)
        key_rows = jnp.concatenate([remote_kv[:, :D], own_kv[:, :D]], 0).reshape(
            2 * ROW, HEADS, HEAD
        )
        value_rows = jnp.concatenate([remote_kv[:, D:], own_kv[:, D:]], 0).reshape(
            2 * ROW, HEADS, HEAD
        )
        mixed, log_total = attention_forward(
            queries, key_rows, value_rows, allowed_mask, score_scale
        )
        mixed_flat = mixed.reshape(ROW, D)
        hidden_res = resident + jnp.dot(mixed_flat, out_weight, preferred_element_type=jnp.float32)
        normed_two = layer_norm(hidden_res, gain_two_f, bias_two_f).astype(jnp.bfloat16)
        pre_act = jnp.dot(
            normed_two, up_weight, preferred_element_type=jnp.float32
        ) + up_shift.astype(jnp.float32)
        activ = jax.nn.gelu(pre_act, approximate=True).astype(jnp.bfloat16)
        result = hidden_res + jnp.dot(activ, down_weight, preferred_element_type=jnp.float32)
        out_blocks.append(result.astype(jnp.bfloat16))
        gathered = (
            lax.all_gather(params[0], ("pair", "rows"), axis=0, tiled=True),
            lax.all_gather(params[1], ("pair", "rows"), axis=0, tiled=True),
            lax.all_gather(params[2], ("pair", "rows"), axis=0, tiled=True),
            lax.all_gather(params[3], ("pair", "rows"), axis=0, tiled=True),
            lax.all_gather(params[4], ("pair", "rows"), axis=0, tiled=True),
            lax.all_gather(params[5], ("pair", "rows"), axis=0, tiled=True),
            lax.all_gather(params[6], ("pair", "rows"), axis=0, tiled=True),
            lax.all_gather(params[7], ("pair", "rows"), axis=0, tiled=True),
            lax.all_gather(params[8], ("pair", "rows"), axis=0, tiled=True),
        )
        (
            gain_one,
            bias_one,
            qkv_weight,
            out_weight,
            gain_two,
            bias_two,
            up_weight,
            up_shift,
            down_weight,
        ) = gathered
        gain_one_f = gain_one.astype(jnp.float32)
        bias_one_f = bias_one.astype(jnp.float32)
        gain_two_f = gain_two.astype(jnp.float32)
        bias_two_f = bias_two.astype(jnp.float32)
        grad_result = cotangent[batch_index, 0, 0]
        grad_down = transposed_times(activ, grad_result)
        grad_activ = times_transposed(grad_result, down_weight)
        _, gelu_back = jax.vjp(lambda pre_value: jax.nn.gelu(pre_value, approximate=True), pre_act)
        grad_pre = gelu_back(grad_activ)[0].astype(jnp.bfloat16)
        grad_up = transposed_times(normed_two, grad_pre)
        grad_up_bias = jnp.sum(grad_pre.astype(jnp.float32), 0)
        grad_normed_two = times_transposed(grad_pre, up_weight)
        _, norm_back_two = jax.vjp(layer_norm, hidden_res, gain_two_f, bias_two_f)
        grad_hidden_ln, grad_gain_two, grad_bias_two = norm_back_two(grad_normed_two)
        grad_hidden = grad_result.astype(jnp.float32) + grad_hidden_ln
        grad_hidden_low = grad_hidden.astype(jnp.bfloat16)
        grad_out_w = transposed_times(mixed_flat, grad_hidden_low)
        grad_mixed = (
            times_transposed(grad_hidden_low, out_weight)
            .astype(jnp.bfloat16)
            .reshape(ROW, HEADS, HEAD)
        )
        grad_queries, grad_keys, grad_values = attention_backward(
            queries, key_rows, value_rows, allowed_mask, log_total, grad_mixed, score_scale
        )
        remote_grads = jnp.concatenate(
            [grad_keys[:ROW].reshape(ROW, D), grad_values[:ROW].reshape(ROW, D)], 1
        )
        returned = passed_along(remote_grads.astype(jnp.bfloat16), "pair", -1).astype(
            remote_grads.dtype
        )
        grad_qkv_rows = jnp.concatenate(
            [
                grad_queries.reshape(ROW, D),
                grad_keys[ROW:].reshape(ROW, D) + returned[:, :D],
                grad_values[ROW:].reshape(ROW, D) + returned[:, D:],
            ],
            1,
        ).astype(jnp.bfloat16)
        grad_qkv_w = transposed_times(normed, grad_qkv_rows)
        grad_normed = times_transposed(grad_qkv_rows, qkv_weight)
        _, norm_back_one = jax.vjp(layer_norm, resident, gain_one_f, bias_one_f)
        grad_resident_ln, grad_gain_one, grad_bias_one = norm_back_one(grad_normed)
        grad_blocks.append(grad_hidden + grad_resident_ln)
        local_grads = (
            grad_gain_one,
            grad_bias_one,
            grad_qkv_w,
            grad_out_w,
            grad_gain_two,
            grad_bias_two,
            grad_up,
            grad_up_bias,
            grad_down,
        )
        shard_part = (
            lax.psum_scatter(local_grads[0], ("pair", "rows"), scatter_dimension=0, tiled=True),
            lax.psum_scatter(local_grads[1], ("pair", "rows"), scatter_dimension=0, tiled=True),
            lax.psum_scatter(local_grads[2], ("pair", "rows"), scatter_dimension=0, tiled=True),
            lax.psum_scatter(local_grads[3], ("pair", "rows"), scatter_dimension=0, tiled=True),
            lax.psum_scatter(local_grads[4], ("pair", "rows"), scatter_dimension=0, tiled=True),
            lax.psum_scatter(local_grads[5], ("pair", "rows"), scatter_dimension=0, tiled=True),
            lax.psum_scatter(local_grads[6], ("pair", "rows"), scatter_dimension=0, tiled=True),
            lax.psum_scatter(local_grads[7], ("pair", "rows"), scatter_dimension=0, tiled=True),
            lax.psum_scatter(local_grads[8], ("pair", "rows"), scatter_dimension=0, tiled=True),
        )
        summed = add_up(summed, shard_part)
    block_shape = (MICRO, 1, 1, ROW, D)
    out_stack = jnp.stack(out_blocks, 0).reshape(block_shape)
    grad_stack = jnp.stack(grad_blocks, 0).reshape(block_shape)
    return (
        out_stack,
        grad_stack,
        summed[0],
        summed[1],
        summed[2],
        summed[3],
        summed[4],
        summed[5],
        summed[6],
        summed[7],
        summed[8],
    )


def solution(mesh):
    return jax.shard_map(
        shards,
        mesh=mesh,
        in_specs=(
            P(None, "rows", "pair", None, None),
            P(None, "rows", "pair", None, None),
            P(None, "rows", None),
            P(None, "rows", None),
            P(None, "rows", None),
            P(("pair", "rows")),
            P(("pair", "rows")),
            P(("pair", "rows"), None),
            P(("pair", "rows"), None),
            P(("pair", "rows")),
            P(("pair", "rows")),
            P(("pair", "rows"), None),
            P(("pair", "rows")),
            P(("pair", "rows"), None),
        ),
        out_specs=(
            P(None, "rows", "pair", None, None),
            P(None, "rows", "pair", None, None),
            P(("pair", "rows")),
            P(("pair", "rows")),
            P(("pair", "rows"), None),
            P(("pair", "rows"), None),
            P(("pair", "rows")),
            P(("pair", "rows")),
            P(("pair", "rows"), None),
            P(("pair", "rows")),
            P(("pair", "rows"), None),
        ),
        check_vma=False,
    )
```

profile of v0, /device:TPU:0, one launch (start us, length us, event | category | flops | bytes accessed | tf_op | source)
XLA Modules:
  0.0 1027.0 jit_solution(1516417270811962957)
XLA Ops:
  14.4 42.2 %all-reduce.10 = (bf16[1024]{0:T(1024)(128)(2,1)S(1)}, bf16[1024]{0:T(1024)(128)(2,1)S(1)}, bf16[1024]{0:T(1024)(128)(2,1)S(1)}, bf16[1024]{0:T(1024)(128)(2,1)S(1)}) all-reduce(bf16[1024]{0:T(1024)(128)(2,1)S(1)} %dynamic-update-slice.1, bf16[1024]{0:T(1024)(128)(2,1)S(1)} %dynamic-update-slice, ...), channel_id=1, replica_groups=mesh['pair'=2,'rows'=16] {'pair','rows'}, use_global_device_ids=true, to_apply=%add.1 | all-reduce | flops 4096 | bytes 16384
  57.7 40.5 %all-gather = bf16[32,1,128]{2,1,0:T(2,128)(2,1)S(1)} all-gather(bf16[1,1,128]{2,1,0:T(2,128)(2,1)} %bitcast.270), channel_id=1, replica_groups=mesh['pair'=2,'rows'=16] {'pair','rows'}, dimensions={0}, use_global_device_ids=true | all-gather | bytes 8448 | tf_op jit(solution)/shard_map/all_gather | solution.py:123
  105.0 5.0 convolution_convert_fusion
  111.1 4.3 collective-permute-start.1
  125.7 16.1 %collective-permute-done.1 = bf16[256,2048]{1,0:T(8,128)(2,1)} collective-permute-done((bf16[256,2048]{1,0:T(8,128)(2,1)}, bf16[256,2048]{1,0:T(8,128)(2,1)}, u32[]{:S(2)}, u32[]{:S(2)}) %collective-permute-start.1) | collective-permute-done | bytes 1048608 | tf_op jit(solution)/shard_map/ppermute | solution.py:16
  152.4 13.2 %collective-permute-done = bf16[256,2048]{1,0:T(8,128)(2,1)} collective-permute-done((bf16[256,2048]{1,0:T(8,128)(2,1)}, bf16[256,2048]{1,0:T(8,128)(2,1)}, u32[]{:S(2)}, u32[]{:S(2)}) %collective-permute-start) | collective-permute-done | bytes 1048608 | tf_op jit(solution)/shard_map/ppermute | solution.py:16
  200.6 24.0 %all-gather.10.cloned.1.call-done = bf16[1024,4096]{1,0:T(8,128)(2,1)} async-done(((bf16[32,4096]{1,0:T(8,128)(2,1)}), bf16[1024,4096]{1,0:T(8,128)(2,1)}) %all-gather.10.cloned.1.call-update) | async-done | bytes 8388624 | tf_op jit(solution)/shard_map/all_gather | solution.py:122
  224.6 8.2 convolution_add_fusion.4
  232.8 4.5 convolution_add_fusion.3
  237.4 66.1 %all-gather.12.cloned.1.call-done = bf16[4096,1024]{1,0:T(8,128)(2,1)} async-done(((bf16[128,1024]{1,0:T(8,128)(2,1)}), bf16[4096,1024]{1,0:T(8,128)(2,1)}) %all-gather.12.cloned.1.call-update) | async-done | bytes 8388624 | tf_op jit(solution)/shard_map/all_gather | solution.py:124
  303.5 8.5 convert_reduce_fusion.1
  312.2 5.6 convert_reduce_fusion
  317.9 6.8 fusion.131
  324.7 7.2 multiply_reduce_fusion.3
  345.7 5.3 convolution_add_fusion.5
  351.0 5.9 fusion.27
  357.0 5.7 fusion.24
  363.9 5.7 multiply_reduce_fusion.1
  369.7 5.0 multiply_convert_fusion.1
  390.5 18.7 %collective-permute-done.2 = bf16[256,2048]{0,1:T(8,128)(2,1)} collective-permute-done((bf16[256,2048]{0,1:T(8,128)(2,1)}, bf16[256,2048]{0,1:T(8,128)(2,1)}, u32[]{:S(2)}, u32[]{:S(2)}) %collective-permute-start.2) | collective-permute-done | bytes 1048608 | tf_op jit(solution)/shard_map/ppermute | solution.py:16
  410.6 24.5 %collective-permute-done.3 = bf16[256,2048]{0,1:T(8,128)(2,1)S(1)} collective-permute-done((bf16[256,2048]{0,1:T(8,128)(2,1)S(1)}, bf16[256,2048]{0,1:T(8,128)(2,1)S(1)}, u32[]{:S(2)}, u32[]{:S(2)}) %collective-permute-start.3) | collective-permute-done | bytes 1048608 | tf_op jit(solution)/shard_map/ppermute | solution.py:16
  438.4 6.6 convolution_add_fusion.2
  445.1 11.0 %fusion.76 = f32[4096,1024]{1,0:T(8,128)} fusion(bf16[2,1,1,256,1024]{4,3,2,1,0:T(8,128)(2,1)} %param.15, f32[256,4096]{1,0:T(8,128)} %convolution_add_fusion.4), kind=kOutput, calls=%fused_computation.146 | convolution fusion | flops 2156920832 | bytes 21495808 | tf_op jit(solution)/shard_map/dot_general | solution.py:26
  456.0 11.1 %convolution_add_fusion = f32[4096,1024]{1,0:T(8,128)} fusion(f32[4096,1024]{1,0:T(8,128)} %fusion.76, bf16[2,1,1,256,1024]{4,3,2,1,0:T(8,128)(2,1)S(1)} %copy-done.9, f32[256,4096]{1,0:T(8,128)S(1)} %copy-done.6), kind=kOutput, calls=%fused_computation | convolution fusion | flops 2161115136 | bytes 38273024 | tf_op jit(solution)/shard_map/dot_general | solution.py:26
  467.6 4.5 fusion.118
  472.1 10.0 convolution_add_fusion.1
  482.9 7.7 fusion.47
  490.7 6.4 fusion.46
  503.8 37.7 %all-reduce.9 = (f32[1024]{0:T(1024)S(1)}, f32[1024]{0:T(1024)S(1)}, f32[1024]{0:T(1024)S(1)}, f32[1024]{0:T(1024)S(1)}, f32[4096]{0:T(1024)S(1)}) all-reduce(f32[1024]{0:T(1024)S(1)} %add.327, f32[1024]{0:T(1024)S(1)} %add.328, f32[1024]{0:T(1024)S(1)} %add.331, ...), channel_id=11, replica_groups=mesh['pair'=2,'rows'=16] {'pair','rows'}, use_global_device_ids=true, to_apply=%region_39.40.clone | all-reduce | flops 8192 | bytes 65536
  548.6 101.1 %reduce-scatter.5.cloned.1.call-done = f32[32,3072]{1,0:T(8,128)} async-done(((f32[1024,3072]{1,0:T(8,128)}), f32[32,3072]{1,0:T(8,128)}) %reduce-scatter.5.cloned.1.call-update) | async-done | bytes 393232 | tf_op jit(solution)/shard_map/reduce_scatter | solution.py:284
  649.7 183.1 %reduce-scatter.11.cloned.1.call-done = f32[128,1024]{1,0:T(8,128)} async-done(((f32[4096,1024]{1,0:T(8,128)}), f32[128,1024]{1,0:T(8,128)}) %reduce-scatter.11.cloned.1.call-update) | async-done | bytes 524304 | tf_op jit(solution)/shard_map/reduce_scatter | solution.py:290
  832.8 187.1 %reduce-scatter.9.cloned.1.call-done = f32[32,4096]{1,0:T(8,128)} async-done(((f32[1024,4096]{1,0:T(8,128)}), f32[32,4096]{1,0:T(8,128)}) %reduce-scatter.9.cloned.1.call-update) | async-done | bytes 524304 | tf_op jit(solution)/shard_map/reduce_scatter | solution.py:288
  (327 shorter events, 121.7 us)
Async XLA Ops:
  7.2 97.8 %all-gather.6.cloned.1.call-start = ((), (), s32[]{:S(2)}) async-start(), calls=%async_computation.4 | async-start | bytes 6488064 | tf_op jit(solution)/shard_map/all_gather | solution.py:118
  7.9 178.6 %all-gather.8.cloned.1.call-start = ((), (), s32[]{:S(2)}) async-start(), calls=%async_computation.5 | async-start | bytes 2162688 | tf_op jit(solution)/shard_map/all_gather | solution.py:119
  8.7 215.9 %all-gather.10.cloned.1.call-start = ((), (), s32[]{:S(2)}) async-start(), calls=%async_computation.6 | async-start | bytes 8650752 | tf_op jit(solution)/shard_map/all_gather | solution.py:122
  9.4 294.0 %all-gather.12.cloned.1.call-start = ((), (), s32[]{:S(2)}) async-start(), calls=%async_computation.7 | async-start | bytes 8650752 | tf_op jit(solution)/shard_map/all_gather | solution.py:124
  10.0 538.6 %reduce-scatter.7.cloned.1.call-start = ((), (), s32[]{:S(2)}) async-start(), calls=%async_computation.9 | async-start | bytes 4325376 | tf_op jit(solution)/shard_map/reduce_scatter | solution.py:285
  56.6 58.8 %copy-start.47 = (f32[1024]{0:T(1024)}, f32[1024]{0:T(1024)S(1)}, u32[]{:S(2)}) copy-start(f32[1024]{0:T(1024)S(1)} %convert_element_type.155) | copy-start | bytes 12292
  57.7 57.7 %copy-start.43 = (f32[1024]{0:T(1024)}, f32[1024]{0:T(1024)S(1)}, u32[]{:S(2)}) copy-start(f32[1024]{0:T(1024)S(1)} %convert_element_type.154) | copy-start | bytes 12292
  111.1 30.7 %collective-permute-start.1 = (bf16[256,2048]{1,0:T(8,128)(2,1)}, bf16[256,2048]{1,0:T(8,128)(2,1)}, u32[]{:S(2)}, u32[]{:S(2)}) collective-permute-start(bf16[256,2048]{1,0:T(8,128)(2,1)} %slice.150), channel_id=1, source_target_pairs={{0,16},{1,17},{2,18},{3,19},{4,20},{5,21},{6,22},{7,23},{8,24},{9,... | collective-permute-start | bytes 3145736 | tf_op jit(solution)/shard_map/ppermute | solution.py:16
  118.4 47.1 %collective-permute-start = (bf16[256,2048]{1,0:T(8,128)(2,1)}, bf16[256,2048]{1,0:T(8,128)(2,1)}, u32[]{:S(2)}, u32[]{:S(2)}) collective-permute-start(bf16[256,2048]{1,0:T(8,128)(2,1)} %slice.144), channel_id=1, source_target_pairs={{0,16},{1,17},{2,18},{3,19},{4,20},{5,21},{6,22},{7,23},{8,24},{9,... | collective-permute-start | bytes 3145736 | tf_op jit(solution)/shard_map/ppermute | solution.py:16
  147.5 42.6 %copy-start.11 = (bf16[512,1024]{0,1:T(8,128)(2,1)}, bf16[512,1024]{0,1:T(8,128)(2,1)S(1)}, u32[]{:S(2)}) copy-start(bf16[512,1024]{0,1:T(8,128)(2,1)S(1)} %copy.68) | copy-start | bytes 3145732
  189.1 142.8 %copy-start.55 = (f32[256]{0:T(256)}, f32[256]{0:T(256)S(1)}, u32[]{:S(2)}) copy-start(f32[256]{0:T(256)S(1)} %broadcast_multiply_fusion.2) | copy-start | bytes 3076
  199.4 25.2 %copy-start.63 = (f32[32,1,128]{2,1,0:T(1,128)S(1)}, f32[32,1,128]{2,1,0:T(1,128)}, u32[]{:S(2)}) copy-start(f32[32,1,128]{2,1,0:T(1,128)} %convert_element_type.197) | copy-start | bytes 49156
  200.3 131.6 %copy-start.59 = (f32[256]{0:T(256)}, f32[256]{0:T(256)S(1)}, u32[]{:S(2)}) copy-start(f32[256]{0:T(256)S(1)} %broadcast_multiply_fusion) | copy-start | bytes 3076
  200.5 131.4 %copy-start.60 = (f32[256]{0:T(256)}, f32[256]{0:T(256)S(1)}, u32[]{:S(2)}) copy-start(f32[256]{0:T(256)S(1)} %fusion.95) | copy-start | bytes 3076
  200.6 131.4 %copy-start.64 = (f32[256]{0:T(256)}, f32[256]{0:T(256)S(1)}, u32[]{:S(2)}) copy-start(f32[256]{0:T(256)S(1)} %fusion.97) | copy-start | bytes 3076
  351.0 298.7 %reduce-scatter.5.cloned.1.call-start = ((), (), s32[]{:S(2)}) async-start(), calls=%async_computation.8 | async-start | bytes 12976128 | tf_op jit(solution)/shard_map/reduce_scatter | solution.py:284
  351.0 12.9 %slice-start.2 = ((s8[8388608]{0:T(1024)(128)(4,1)}), s8[4194304]{0:T(1024)(128)(4,1)S(1)}, s32[]{:S(2)}) async-start(s8[8388608]{0:T(1024)(128)(4,1)} %bitcast.238), calls=%async_computation.14 | async-start | bytes 8388608
  363.9 14.2 %slice-start = ((s8[8388608]{0:T(1024)(128)(4,1)}), s8[4194304]{0:T(1024)(128)(4,1)S(1)}, s32[]{:S(2)}) async-start(s8[8388608]{0:T(1024)(128)(4,1)} %bitcast.236), calls=%async_computation.12 | async-start | bytes 8388608
  376.8 32.4 %collective-permute-start.2 = (bf16[256,2048]{0,1:T(8,128)(2,1)}, bf16[256,2048]{0,1:T(8,128)(2,1)}, u32[]{:S(2)}, u32[]{:S(2)}) collective-permute-start(bf16[256,2048]{0,1:T(8,128)(2,1)} %pad_maximum_fusion.6), channel_id=1, source_target_pairs={{16,0},{17,1},{18,2},{19,3},{20,4},{21,5},{22,6},{23,7},{24,8},{25... | collective-permute-start | bytes 3145736 | tf_op jit(solution)/shard_map/ppermute | solution.py:16
  385.9 49.3 %collective-permute-start.3 = (bf16[256,2048]{0,1:T(8,128)(2,1)S(1)}, bf16[256,2048]{0,1:T(8,128)(2,1)S(1)}, u32[]{:S(2)}, u32[]{:S(2)}) collective-permute-start(bf16[256,2048]{0,1:T(8,128)(2,1)S(1)} %pad_maximum_fusion.7), channel_id=1, source_target_pairs={{16,0},{17,1},{18,2},{19,3},{20,4},{21,5},{22,6},{23,7},{24,8},{25... | collective-permute-start | bytes 3145736 | tf_op jit(solution)/shard_map/ppermute | solution.py:16
  389.1 47.1 %copy-start.36 = (bf16[16,64,256]{2,1,0:T(8,128)(2,1)}, bf16[16,64,256]{2,1,0:T(8,128)(2,1)S(1)}, u32[]{:S(2)}) copy-start(bf16[16,64,256]{2,1,0:T(8,128)(2,1)S(1)} %fusion.44) | copy-start | bytes 1572868
  390.5 47.9 %copy-start.27 = (bf16[16,64,256]{2,1,0:T(8,128)(2,1)}, bf16[16,64,256]{2,1,0:T(8,128)(2,1)S(1)}, u32[]{:S(2)}) copy-start(bf16[16,64,256]{2,1,0:T(8,128)(2,1)S(1)} %fusion.45) | copy-start | bytes 1572868
  390.5 44.9 %slice-start.4 = ((f32[512,16,64]{0,2,1:T(8,128)}), f32[256,16,64]{0,2,1:T(8,128)S(1)}, s32[]{:S(2)}) async-start(f32[512,16,64]{0,2,1:T(8,128)} %copy-done.18), calls=%async_computation.16 | async-start | bytes 2097152 | tf_op jit(solution)/shard_map/slice | solution.py:260
  390.5 44.8 %slice-start.7 = ((f32[512,16,64]{0,2,1:T(8,128)}), f32[256,16,64]{0,2,1:T(8,128)S(1)}, s32[]{:S(2)}) async-start(f32[512,16,64]{0,2,1:T(8,128)} %copy-done.23), calls=%async_computation.19 | async-start | bytes 2097152 | tf_op jit(solution)/shard_map/slice | solution.py:261
  410.6 25.2 %slice-start.5 = ((f32[512,16,64]{0,2,1:T(8,128)}), f32[256,16,64]{0,2,1:T(8,128)S(1)}, s32[]{:S(2)}) async-start(f32[512,16,64]{0,2,1:T(8,128)} %copy-done.19), calls=%async_computation.17 | async-start | bytes 2097152 | tf_op jit(solution)/shard_map/slice | solution.py:260
  410.6 25.1 %slice-start.6 = ((f32[512,16,64]{0,2,1:T(8,128)}), f32[256,16,64]{0,2,1:T(8,128)S(1)}, s32[]{:S(2)}) async-start(f32[512,16,64]{0,2,1:T(8,128)} %copy-done.22), calls=%async_computation.18 | async-start | bytes 2097152 | tf_op jit(solution)/shard_map/slice | solution.py:261
  445.0 387.8 %reduce-scatter.11.cloned.1.call-start = ((), (), s32[]{:S(2)}) async-start(), calls=%async_computation.11 | async-start | bytes 17301504 | tf_op jit(solution)/shard_map/reduce_scatter | solution.py:290
  467.2 552.8 %reduce-scatter.9.cloned.1.call-start = ((), (), s32[]{:S(2)}) async-start(), calls=%async_computation.10 | async-start | bytes 17301504 | tf_op jit(solution)/shard_map/reduce_scatter | solution.py:288
  482.9 15.2 %slice-start.8 = ((s8[6291456]{0:T(1024)(128)(4,1)}), s8[4194304]{0:T(1024)(128)(4,1)S(1)}, s32[]{:S(2)}) async-start(s8[6291456]{0:T(1024)(128)(4,1)} %bitcast.275), calls=%async_computation.20 | async-start | bytes 8388608
  500.2 44.2 %copy-start.10 = (bf16[2,1,1,256,1024]{4,3,2,1,0:T(8,128)(2,1)S(1)}, bf16[2,1,1,256,1024]{4,3,2,1,0:T(8,128)(2,1)}, u32[]{:S(2)}) copy-start(bf16[2,1,1,256,1024]{4,3,2,1,0:T(8,128)(2,1)} %param.15) | copy-start | bytes 3145732
  500.2 44.2 %copy-start.70 = (f32[256]{0:T(256)S(1)}, f32[256]{0:T(256)}, u32[]{:S(2)}) copy-start(f32[256]{0:T(256)} %copy-done.69) | copy-start | bytes 3076
  500.2 44.2 %copy-start.72 = (f32[256]{0:T(256)S(1)}, f32[256]{0:T(256)}, u32[]{:S(2)}) copy-start(f32[256]{0:T(256)} %copy-done.71) | copy-start | bytes 3076
  (70 other events, 312.7 us)
Sparse Core Ops, SparseCore 0:
  10.9 72.3 all-gather.5
  86.1 55.0 all-gather.7
  144.1 80.4 all-gather.9
  227.3 76.1 all-gather.11
  351.1 140.2 reduce-scatter.6
  497.8 151.8 reduce-scatter.4
  652.7 180.0 reduce-scatter.10
  835.8 184.1 reduce-scatter.8
where the time goes:
time: 1040 us; the launch traced here: 1030 us
  waiting for transfers between devices  637 us (61%)
  matrix products  165 us (16%)
  blocking collectives  120 us (12%)
  other arithmetic  40.8 us (4%)
  local copies, waits for them, and re-layouts  37.4 us (4%)
  between operations  15.8 us (2%)
  starting transfers between devices  10.4 us (1%)
    reduce_scatter x1, waiting for transfers between devices, shards(): lax.psum_scatter(local_grads[6], ('pair', 'rows'), scatter_dimension=0, t...  187 us
    reduce_scatter x1, waiting for transfers between devices, shards(): lax.psum_scatter(local_grads[8], ('pair', 'rows'), scatter_dimension=0, t...  183 us
    reduce_scatter x1, waiting for transfers between devices, shards(): lax.psum_scatter(local_grads[2], ('pair', 'rows'), scatter_dimension=0, t...  101 us
    unnamed x2, blocking collectives  79.9 us
    ppermute x4, waiting for transfers between devices, passed_along(): return lax.ppermute(block, axis, route)  72.5 us
    all_gather x1, waiting for transfers between devices, fetch_forward(): lax.all_gather(params[8], ('pair', 'rows'), axis=0, tiled=True)  66.1 us
    dot_general x8, matrix products, transposed_times(): lax.dot_general(left, right, (((0,), (0,)), ((), ())), preferred_element_...  53.3 us
    all_gather x1, blocking collectives, fetch_forward(): lax.all_gather(params[7], ('pair', 'rows'), axis=0, tiled=True)  40.5 us
  transfers between devices with their start and end apart: 12, of which 9 were waited for; matrix products, arithmetic and copies ran while one was open for 19% of the time, Pallas kernels for 0%

commit v1 on v0

v1 whole, which is shorter than its diff:
```python
import functools

import jax
import jax.numpy as jnp
from jax import lax
from jax.experimental import pallas as pl
from jax.experimental.pallas import tpu as pltpu
from jax.sharding import PartitionSpec as P

D = 1024
HEADS = 16
HEAD = 64
FF = 4096
ROW = 256
MICRO = 2
BF = jnp.bfloat16
F32 = jnp.float32
NEG = -1e30


def position():
    row = lax.axis_index("rows")
    return lax.axis_index("pair"), row // 4, (row // 2) % 2, row % 2


def depth():
    return lax.axis_size("rows") // 4


def swap(block, way):
    if way == "y":
        return lax.ppermute(block, "pair", [(i, i ^ 1) for i in range(2)])
    count = lax.axis_size("rows")
    return lax.ppermute(block, "rows", [(i, i ^ way) for i in range(count)])


def after(block, *others):
    return lax.optimization_barrier((block, *others))[0]


def z_groups():
    count = lax.axis_size("rows")
    return [[z * 4 + low for z in range(count // 4)] for low in range(4)]


def gather_chips(block):
    count = depth()
    if count == 4:
        parts = [block[None]] + [swap(block[None], 4 * k) for k in range(1, 4)]
        first, second = jnp.concatenate(parts[:2], 0), jnp.concatenate(parts[2:], 0)
        done = parts[1:]
    else:
        column = lax.all_gather(block, "rows", axis_index_groups=z_groups())
        first, second = column[: count // 2], column[count // 2 :]
        done = [column]
    half = count // 2
    first_x, second_y = swap(first, 2), swap(second, "y")
    first_two = jnp.concatenate([first, first_x], 0)
    second_two = jnp.concatenate([second, second_y], 0)
    first_y, second_x = swap(first_two, "y"), swap(second_two, 2)
    ids = range(half)
    pieces = [
        (first_two, [(0, i, 0) for i in ids] + [(0, i, 1) for i in ids]),
        (first_y, [(1, i, 0) for i in ids] + [(1, i, 1) for i in ids]),
        (second_two, [(0, half + i, 0) for i in ids] + [(1, half + i, 0) for i in ids]),
        (second_x, [(0, half + i, 1) for i in ids] + [(1, half + i, 1) for i in ids]),
    ]
    return pieces, done


def chip_slot(rel, where, count):
    jy, jz, jx = rel
    y, z, x, _ = where
    z_at = (z ^ jz) if count == 4 else jz
    return ((y ^ jy) * count + z_at) * 2 + (x ^ jx)


def assemble(pieces, cores, cuts):
    count = depth()
    chips = 4 * count
    arrays = [p[0] for part in pieces for p in part]
    names = [(core, p[1]) for core, part in enumerate(pieces) for p in part]
    rows = arrays[0].shape[1]

    def kernel(*refs):
        ins = refs[: len(arrays)]
        outs, sems = refs[len(arrays) : -1], refs[-1]
        where = position()
        copies = []
        for ref, (core, rels) in zip(ins, names):
            for i, rel in enumerate(rels):
                slot = chip_slot(rel, where, count)
                at = (where[3] ^ core) if cores == 2 else 0
                for out, (start, width) in zip(outs, cuts):
                    copy = pltpu.make_async_copy(
                        ref.at[i, :, pl.ds(start, width)], out.at[slot, at], sems.at[len(copies)]
                    )
                    copy.start()
                    copies.append(copy)
        for copy in copies:
            copy.wait()

    return pl.pallas_call(
        kernel,
        out_shape=[
            jax.ShapeDtypeStruct((chips, cores, rows, width), arrays[0].dtype) for _, width in cuts
        ],
        in_specs=[pl.BlockSpec(memory_space=pl.ANY)] * len(arrays),
        out_specs=[pl.BlockSpec(memory_space=pltpu.VMEM)] * len(cuts),
        scratch_shapes=[pltpu.SemaphoreType.DMA((chips * cores * len(cuts),))],
        name="assemble",
    )(*arrays)


def layout():
    half = depth() // 2
    ids = range(half)
    return [
        [(1, i, jx) for jx in range(2) for i in ids],
        [(0, i, jx) for jx in range(2) for i in ids],
        [(jy, half + i, 1) for jy in range(2) for i in ids],
        [(jy, half + i, 0) for jy in range(2) for i in ids],
    ]


def disassemble(blocks):
    count = depth()
    shape = blocks.shape[1:]
    names = layout()

    def kernel(ref, *rest):
        outs, sems = rest[:4], rest[4]
        where = position()
        copies = []
        for out, rels in zip(outs, names):
            for i, rel in enumerate(rels):
                copy = pltpu.make_async_copy(
                    ref.at[chip_slot(rel, where, count)], out.at[i], sems.at[len(copies)]
                )
                copy.start()
                copies.append(copy)
        for copy in copies:
            copy.wait()

    return pl.pallas_call(
        kernel,
        out_shape=[jax.ShapeDtypeStruct((count, *shape), blocks.dtype)] * 4,
        in_specs=[pl.BlockSpec(memory_space=pltpu.VMEM)],
        out_specs=[pl.BlockSpec(memory_space=pl.ANY)] * 4,
        scratch_shapes=[pltpu.SemaphoreType.DMA((4 * count,))],
        name="disassemble",
    )(blocks)


def core_send(grads):
    chips, _, rows, _ = grads[0].shape
    widths = [g.shape[3] for g in grads]

    def kernel(*refs):
        ins, out, sems = refs[: len(grads)], refs[len(grads)], refs[-1]
        other = 1 - position()[3]
        copies, start = [], 0
        for n, (ref, width) in enumerate(zip(ins, widths)):
            copy = pltpu.make_async_copy(
                ref.at[:, other], out.at[:, :, pl.ds(start, width)], sems.at[n]
            )
            copy.start()
            copies.append(copy)
            start += width
        for copy in copies:
            copy.wait()

    return pl.pallas_call(
        kernel,
        out_shape=jax.ShapeDtypeStruct((chips, rows, sum(widths)), grads[0].dtype),
        in_specs=[pl.BlockSpec(memory_space=pltpu.VMEM)] * len(grads),
        out_specs=pl.BlockSpec(memory_space=pl.ANY),
        scratch_shapes=[pltpu.SemaphoreType.DMA((len(grads),))],
        name="core_send",
    )(*grads)


def core_sum(grads, arrived):
    count = depth()
    chips, _, rows, _ = grads[0].shape
    widths = [g.shape[3] for g in grads]
    names = layout()

    def kernel(*refs):
        ins, arr, outs = refs[: len(grads)], refs[len(grads)], refs[len(grads) + 1 :]
        where = position()
        for out, rels in zip(outs, names):
            for i, rel in enumerate(rels):
                slot = chip_slot(rel, where, count)
                start = 0
                for ref, width in zip(ins, widths):
                    own = ref[slot, where[3]].astype(F32)
                    other = arr[slot, :, start : start + width].astype(F32)
                    out[i, :, start : start + width] = (own + other).astype(BF)
                    start += width

    return pl.pallas_call(
        kernel,
        out_shape=[jax.ShapeDtypeStruct((count, rows, sum(widths)), grads[0].dtype)] * 4,
        in_specs=[pl.BlockSpec(memory_space=pltpu.VMEM)] * (len(grads) + 1),
        out_specs=[pl.BlockSpec(memory_space=pltpu.VMEM)] * 4,
        name="core_sum",
    )(*grads, arrived)


def plus(left, right):
    return (left.astype(F32) + right.astype(F32)).astype(left.dtype)


def scatter_chips(parts):
    count = depth()
    half = count // 2
    first_send, first_keep, second_send, second_keep = parts
    first_in, second_in = swap(first_send, "y"), swap(second_send, 2)
    first_out = plus(first_keep[half:], first_in[half:])
    first_own = plus(first_keep[:half], first_in[:half])
    second_out = plus(second_keep[half:], second_in[half:])
    second_own = plus(second_keep[:half], second_in[:half])
    first_in, second_in = swap(first_out, 2), swap(second_out, "y")
    if count == 4:
        total = first_own[0].astype(F32) + first_in[0].astype(F32)
        one = plus(first_own[1], first_in[1])
        two = plus(second_own, second_in)
        total = total + swap(one, 4).astype(F32)
        total = total + swap(two[0], 8).astype(F32)
        return total + swap(two[1], 12).astype(F32)
    column = jnp.concatenate([plus(first_own, first_in), plus(second_own, second_in)], 0)
    return lax.psum_scatter(
        column.astype(F32), "rows", scatter_dimension=0, axis_index_groups=z_groups()
    )


def ordered(flag, own, other, axis):
    return jnp.where(
        flag == 0,
        jnp.concatenate([own, other], axis),
        jnp.concatenate([other, own], axis),
    )


def ends(lengths_ref, count):
    out, total = [], 0
    for s in range(count):
        total = total + lengths_ref[s]
        out.append(total)
    return out


def frames(index, phone, prompt, target, segs):
    pre_end = ends_of([phone[s] + prompt[s] for s in range(segs)])
    tgt_end = ends_of([target[s] for s in range(segs)])
    is_target = index >= ROW
    local = jnp.where(is_target, index - ROW, index)
    seg = jnp.zeros_like(index)
    for s in range(segs):
        edge = jnp.where(is_target, tgt_end[s], pre_end[s])
        seg = seg + jnp.where(local >= edge, 1, 0)
    start = jnp.zeros_like(index)
    phones = jnp.zeros_like(index)
    prompts = jnp.zeros_like(index)
    for s in range(segs):
        pick = seg == s
        pre_start = pre_end[s] - phone[s] - prompt[s]
        tgt_start = tgt_end[s] - target[s]
        start = jnp.where(pick, jnp.where(is_target, tgt_start, pre_start), start)
        phones = jnp.where(pick, phone[s], phones)
        prompts = jnp.where(pick, prompt[s], prompts)
    off = local - start
    is_phone = jnp.where(is_target, 0, jnp.where(off < phones, 1, 0))
    pos = jnp.where(is_target, prompts + off, off - phones)
    return seg, is_phone, pos


def ends_of(lengths):
    out, total = [], 0
    for length in lengths:
        total = total + length
        out.append(total)
    return out


def bias_of(query, key):
    q_seg, q_phone, q_pos = query
    k_seg, k_phone, k_pos = key
    audio = (k_phone == 1) | (k_pos <= q_pos)
    good = (q_seg == k_seg) & (((q_phone == 1) & (k_phone == 1)) | ((q_phone == 0) & audio))
    return jnp.where(good, 0.0, NEG)


def bdot(left, right, dims):
    return lax.dot_general(left, right, (dims, ((), ())), preferred_element_type=F32)


NT = ((1,), (1,))
NN = ((1,), (0,))
TN = ((0,), (0,))


def attention_forward(qkv, phone, prompt, target):
    segs = phone.shape[0]

    def kernel(phone_ref, prompt_ref, target_ref, q_ref, k_ref, v_ref, out_ref, bias_ref):
        @pl.when(pl.program_id(0) == 0)
        def _():
            ph = [phone_ref[s] for s in range(segs)]
            pr = [prompt_ref[s] for s in range(segs)]
            tg = [target_ref[s] for s in range(segs)]
            rows = lax.broadcasted_iota(jnp.int32, (2 * ROW, 1), 0)
            cols = lax.broadcasted_iota(jnp.int32, (1, 2 * ROW), 1)
            bias_ref[...] = bias_of(
                frames(rows, ph, pr, tg, segs), frames(cols, ph, pr, tg, segs)
            )

        lane = lax.broadcasted_iota(jnp.int32, (1, 2 * HEAD), 1)
        for rows, keys in ((0, ROW), (ROW, 2 * ROW)):
            outs = []
            for j in range(2):
                sel = (lane // HEAD) == j
                q = jnp.where(sel, q_ref[rows : rows + ROW, :], jnp.zeros((), BF))
                s = bdot(q, k_ref[:keys, :], NT) * HEAD**-0.5
                s = s + bias_ref[rows : rows + ROW, :keys]
                e = jnp.exp(s - jnp.max(s, 1, keepdims=True))
                p = (e * (1.0 / jnp.sum(e, 1, keepdims=True))).astype(BF)
                outs.append(bdot(p, v_ref[:keys, :], NN))
            out_ref[rows : rows + ROW, :] = jnp.where(lane < HEAD, outs[0], outs[1]).astype(BF)

    pairs = HEADS // 2
    smem = pl.BlockSpec(memory_space=pltpu.SMEM)
    return pl.pallas_call(
        kernel,
        grid=(pairs,),
        out_shape=jax.ShapeDtypeStruct((2 * ROW, D), BF),
        in_specs=[
            smem,
            smem,
            smem,
            pl.BlockSpec((2 * ROW, 2 * HEAD), lambda h: (0, h)),
            pl.BlockSpec((2 * ROW, 2 * HEAD), lambda h: (0, h + pairs)),
            pl.BlockSpec((2 * ROW, 2 * HEAD), lambda h: (0, h + 2 * pairs)),
        ],
        out_specs=pl.BlockSpec((2 * ROW, 2 * HEAD), lambda h: (0, h)),
        scratch_shapes=[pltpu.VMEM((2 * ROW, 2 * ROW), F32)],
        cost_estimate=pl.CostEstimate(
            flops=HEADS * 4 * 196608 * HEAD, bytes_accessed=4 << 20, transcendentals=3 << 20
        ),
        name="attention_forward",
    )(phone, prompt, target, qkv, qkv, qkv)


def attention_backward(qkv, grad_mixed, phone, prompt, target):
    segs = phone.shape[0]

    def kernel(
        phone_ref, prompt_ref, target_ref, q_ref, k_ref, v_ref, g_ref, dq_ref, dk_ref, dv_ref, bias_ref
    ):
        @pl.when(pl.program_id(0) == 0)
        def _():
            ph = [phone_ref[s] for s in range(segs)]
            pr = [prompt_ref[s] for s in range(segs)]
            tg = [target_ref[s] for s in range(segs)]
            rows = lax.broadcasted_iota(jnp.int32, (2 * ROW, 1), 0)
            cols = lax.broadcasted_iota(jnp.int32, (1, 2 * ROW), 1)
            bias_ref[...] = bias_of(
                frames(cols, ph, pr, tg, segs), frames(rows, ph, pr, tg, segs)
            )

        lane = lax.broadcasted_iota(jnp.int32, (1, 2 * HEAD), 1)
        zero = jnp.zeros((), BF)
        dqs = {}
        dks = {}
        dvs = {}
        for rows, keys in ((0, ROW), (ROW, 2 * ROW)):
            for j in range(2):
                sel = (lane // HEAD) == j
                q_all = q_ref[rows : rows + ROW, :]
                g_all = g_ref[rows : rows + ROW, :]
                q = jnp.where(sel, q_all, zero)
                g = jnp.where(sel, g_all, zero)
                k = k_ref[:keys, :]
                v = v_ref[:keys, :]
                s = bdot(k, q, NT) * HEAD**-0.5 + bias_ref[:keys, rows : rows + ROW]
                e = jnp.exp(s - jnp.max(s, 0, keepdims=True))
                p = e * (1.0 / jnp.sum(e, 0, keepdims=True))
                dp = bdot(v, g, NT)
                inner = jnp.sum(dp * p, 0, keepdims=True)
                ds = (p * (dp - inner)).astype(BF)
                dvs[rows, j] = bdot(p.astype(BF), g_all, NN)
                dks[rows, j] = bdot(ds, q_all, NN)
                dqs[rows, j] = bdot(ds, k, TN)
        low = lane < HEAD
        scale = HEAD**-0.5
        for rows in (0, ROW):
            dq_ref[rows : rows + ROW, :] = (
                jnp.where(low, dqs[rows, 0], dqs[rows, 1]) * scale
            ).astype(BF)
        for out, part, factor in ((dk_ref, dks, scale), (dv_ref, dvs, 1.0)):
            early = jnp.where(low, part[0, 0], part[0, 1])
            late = jnp.where(low, part[ROW, 0], part[ROW, 1])
            out[:ROW, :] = ((early + late[:ROW]) * factor).astype(BF)
            out[ROW:, :] = (late[ROW:] * factor).astype(BF)

    pairs = HEADS // 2
    smem = pl.BlockSpec(memory_space=pltpu.SMEM)
    block = (2 * ROW, 2 * HEAD)
    return pl.pallas_call(
        kernel,
        grid=(pairs,),
        out_shape=[jax.ShapeDtypeStruct((2 * ROW, D), BF)] * 3,
        in_specs=[
            smem,
            smem,
            smem,
            pl.BlockSpec(block, lambda h: (0, h)),
            pl.BlockSpec(block, lambda h: (0, h + pairs)),
            pl.BlockSpec(block, lambda h: (0, h + 2 * pairs)),
            pl.BlockSpec(block, lambda h: (0, h)),
        ],
        out_specs=[pl.BlockSpec(block, lambda h: (0, h))] * 3,
        scratch_shapes=[pltpu.VMEM((2 * ROW, 2 * ROW), F32)],
        cost_estimate=pl.CostEstimate(
            flops=HEADS * 10 * 196608 * HEAD, bytes_accessed=7 << 20, transcendentals=3 << 20
        ),
        name="attention_backward",
    )(phone, prompt, target, qkv, qkv, qkv, grad_mixed)


def norm_parts(values):
    center = values - jnp.mean(values, -1, keepdims=True)
    spread = jnp.mean(center * center, -1, keepdims=True)
    inv = lax.rsqrt(spread + 1e-05)
    return center * inv, inv


def norm_back(grad, normal, inv, gain):
    e = grad * gain
    return inv * (
        e - jnp.mean(e, -1, keepdims=True) - normal * jnp.mean(e * normal, -1, keepdims=True)
    )


def gelu_grad(v):
    c = (2.0 / jnp.pi) ** 0.5
    t = jnp.tanh(c * (v + 0.044715 * v * v * v))
    return 0.5 * (1.0 + t) + 0.5 * v * (1.0 - t * t) * c * (1.0 + 3 * 0.044715 * v * v)


def shards(
    inputs,
    cotangent,
    phone_len,
    prompt_len,
    target_len,
    ln1_gain,
    ln1_bias,
    w_qkv,
    w_out,
    ln2_gain,
    ln2_bias,
    w_up,
    up_bias,
    w_down,
):
    y, z, x, c = position()
    count = depth()
    chips = 4 * count
    row_w = w_qkv.shape[0]
    row_f = w_down.shape[0]

    def mine(stack):
        return lax.dynamic_index_in_dim(stack, y, 0, keepdims=False)

    def others(stack):
        return lax.dynamic_index_in_dim(stack, 1 - y, 0, keepdims=False)

    in_blocks = inputs[:, 0, 0]
    ct_blocks = cotangent[:, 0, 0]
    resident = ordered(y, mine(in_blocks), swap(others(in_blocks), "y"), 0)
    grad_result = ordered(y, mine(ct_blocks), swap(others(ct_blocks), "y"), 0)
    lengths = (mine(phone_len)[0], mine(prompt_len)[0], mine(target_len)[0])

    small = jnp.concatenate([ln1_gain, ln1_bias, ln2_gain, ln2_bias, up_bias])
    small = jnp.pad(small.reshape(row_w, -1), ((0, 0), (0, 128 - small.shape[0] // row_w)))
    attn_shard = jnp.concatenate([w_qkv, w_out, small], 1)
    up_split = w_up.reshape(row_w, chips, 2, FF // chips // 2)
    up_own = lax.dynamic_index_in_dim(up_split, c, 2, keepdims=False).reshape(row_w, FF // 2)
    up_other = lax.dynamic_index_in_dim(up_split, 1 - c, 2, keepdims=False).reshape(row_w, FF // 2)
    up_shard = ordered(c, up_own, swap(up_other, 1), 0)

    attn_pieces, attn_done = gather_chips(attn_shard)
    up_pieces, up_done = gather_chips(after(up_shard, *attn_done))
    down_pieces, _ = gather_chips(after(w_down, *up_done))

    attn_core = [(swap(array, 1), rels) for array, rels in attn_pieces]
    qkv_weight, out_weight, smalls = assemble(
        [attn_pieces, attn_core], 2, [(0, 3 * D), (3 * D, D), (4 * D, 128)]
    )
    qkv_weight = qkv_weight.reshape(D, 3 * D)
    out_weight = out_weight.reshape(D, D)
    width = (4 * row_w + row_f) // row_w
    smalls = smalls[..., :width].reshape(2 * chips, row_w * width)
    gain_one, bias_one, gain_two, bias_two = (
        smalls[:, i * row_w : (i + 1) * row_w].reshape(D).astype(F32) for i in range(4)
    )
    shift = smalls[:, 4 * row_w :].reshape(chips, 2, row_f).astype(F32)
    shift = lax.dynamic_index_in_dim(shift, c, 1, keepdims=False).reshape(FF // 2)
    [up_weight] = assemble([up_pieces], 1, [(0, FF // 2)])
    up_weight = up_weight.reshape(D, FF // 2)
    [down_weight] = assemble([down_pieces], 1, [(0, D)])
    down_weight = down_weight.reshape(FF // 2, D)

    resident_f = resident.astype(F32)
    normal_one, inv_one = norm_parts(resident_f)
    normed = (normal_one * gain_one + bias_one).astype(BF)
    qkv = jnp.dot(normed, qkv_weight, preferred_element_type=F32).astype(BF)
    mixed = attention_forward(qkv, *lengths)
    hidden = resident_f + jnp.dot(mixed, out_weight, preferred_element_type=F32)
    normal_two, inv_two = norm_parts(hidden)
    normed_two = (normal_two * gain_two + bias_two).astype(BF)
    normed_both = jnp.concatenate([normed_two, swap(normed_two, 1)], 0)
    pre_act = jnp.dot(normed_both, up_weight, preferred_element_type=F32) + shift
    activ = jax.nn.gelu(pre_act, approximate=True).astype(BF)
    ct_both = jnp.concatenate([grad_result, swap(grad_result, 1)], 0)
    grad_down = bdot(activ, ct_both, TN).astype(BF)
    sum_down = scatter_chips(disassemble(grad_down.reshape(chips, row_f, D)))
    down_out = jnp.dot(activ, down_weight, preferred_element_type=F32)
    result = hidden + down_out[: 2 * ROW] + swap(down_out[2 * ROW :], 1)
    result = result.astype(BF).reshape(2, ROW, D)

    grad_activ = bdot(ct_both, down_weight, NT)
    grad_pre_f = grad_activ * gelu_grad(pre_act)
    grad_pre = grad_pre_f.astype(BF)
    grad_up = bdot(normed_both, grad_pre, TN).astype(BF)
    sum_up = scatter_chips(disassemble(grad_up.reshape(chips, 2 * row_w, FF // 2)))
    grad_shift = jnp.sum(grad_pre.astype(F32), 0)
    grad_two_part = bdot(grad_pre, up_weight, NT)
    grad_two = grad_two_part[: 2 * ROW] + swap(grad_two_part[2 * ROW :], 1)
    grad_gain_two = jnp.sum(grad_two * normal_two, 0)
    grad_bias_two = jnp.sum(grad_two, 0)
    grad_hidden = grad_result.astype(F32) + norm_back(grad_two, normal_two, inv_two, gain_two)
    grad_low = grad_hidden.astype(BF)
    grad_out = bdot(mixed, grad_low, TN).astype(BF)
    grad_mixed = bdot(grad_low, out_weight, NT).astype(BF)
    dq, dk, dv = attention_backward(qkv, grad_mixed, *lengths)
    grad_qkv_rows = jnp.concatenate([dq, dk, dv], 1)
    grad_qkv = bdot(normed, grad_qkv_rows, TN).astype(BF)
    attn_grads = [grad_qkv.reshape(chips, 2, row_w, 3 * D), grad_out.reshape(chips, 2, row_w, D)]
    sum_attn = scatter_chips(core_sum(attn_grads, swap(core_send(attn_grads), 1)))
    grad_one = bdot(grad_qkv_rows, qkv_weight, NT)
    grad_gain_one = jnp.sum(grad_one * normal_one, 0)
    grad_bias_one = jnp.sum(grad_one, 0)
    input_grad = grad_hidden + norm_back(grad_one, normal_one, inv_one, gain_one)

    shift_two = grad_shift.reshape(chips, 1, row_f)
    shift_none = jnp.zeros_like(shift_two)
    shift_two = ordered(c, shift_two, shift_none, 1)
    parts = [
        v.reshape(chips, 2, row_w)
        for v in (grad_gain_one, grad_bias_one, grad_gain_two, grad_bias_two)
    ]
    small_grads = jnp.concatenate([*parts, shift_two], 2)
    small_send = lax.dynamic_index_in_dim(small_grads, 1 - c, 1, keepdims=False)
    small_keep = lax.dynamic_index_in_dim(small_grads, c, 1, keepdims=False)
    small_sum = small_keep + swap(small_send, 1)
    length = small_sum.shape[1]
    lines = -(-length // 1024) * 8
    small_sum = jnp.pad(small_sum, ((0, 0), (0, lines * 128 - length))).reshape(chips, lines, 128)
    small_sum = scatter_chips(disassemble(small_sum)).reshape(-1)

    def home(pair):
        own = lax.dynamic_index_in_dim(pair, y, 0, keepdims=False)
        away = swap(lax.dynamic_index_in_dim(pair, 1 - y, 0, keepdims=False), "y")
        return ordered(y, own[None], away[None], 0).reshape(MICRO, 1, 1, ROW, D)

    out_stack = home(result)
    grad_stack = home(input_grad.reshape(2, ROW, D))

    up_rows = sum_up.reshape(2, row_w, FF // 2)
    up_mine = lax.dynamic_index_in_dim(up_rows, c, 0, keepdims=False)
    up_theirs = swap(lax.dynamic_index_in_dim(up_rows, 1 - c, 0, keepdims=False), 1)
    lines_up = (row_w, chips, 1, FF // chips // 2)
    up_final = ordered(c, up_mine.reshape(lines_up), up_theirs.reshape(lines_up), 2)
    edges = [i * row_w for i in range(5)]
    small_out = [small_sum[a:b] for a, b in zip(edges[:4], edges[1:])]
    return (
        out_stack,
        grad_stack,
        small_out[0],
        small_out[1],
        sum_attn[:, : 3 * D],
        sum_attn[:, 3 * D :],
        small_out[2],
        small_out[3],
        up_final.reshape(row_w, FF),
        small_sum[4 * row_w : 4 * row_w + row_f],
        sum_down,
    )


def solution(mesh):
    rows = P(None, "rows", "pair", None, None)
    line = P(("pair", "rows"))
    flat = P(("pair", "rows"), None)
    lens = P(None, "rows", None)
    return jax.shard_map(
        shards,
        mesh=mesh,
        in_specs=(rows, rows, lens, lens, lens, line, line, flat, flat, line, line, flat, line, flat),
        out_specs=(rows, rows, line, line, flat, flat, line, line, flat, line, flat),
        check_vma=False,
    )
```

time: 1040 us -> 468 us (0.45)
  the two profiles are of different devices: /device:TPU:0 before, /device:TPU:9 now
where the time goes in v1:
time: 468 us; the launch traced here: 462 us
  waiting for transfers between devices  135 us (29%)
  starting transfers between devices  89.7 us (19%)
  matrix products  86.1 us (18%)
  Pallas kernels  77 us (16%)
  local copies, waits for them, and re-layouts  37.8 us (8%)
  other arithmetic  34.7 us (7%)
    ppermute x47, waiting for transfers between devices, swap(): return lax.ppermute(block, 'rows', [(i, i ^ way) for i in range(count)])  77.1 us
    ppermute x47, starting transfers between devices, swap(): return lax.ppermute(block, 'rows', [(i, i ^ way) for i in range(count)])  72.3 us
    dot_general x8, matrix products, bdot(): lax.dot_general(left, right, (dims, ((), ())), preferred_element_type=F32)  59.6 us
    ppermute x18, waiting for transfers between devices, swap(): return lax.ppermute(block, 'pair', [(i, i ^ 1) for i in range(2)])  57.5 us
    pallas_call x1, Pallas kernels, attention_backward(): pl.pallas_call(kernel, grid=(pairs,), out_shape=[jax.ShapeDtypeStruct((2...  20.6 us
    ppermute x18, starting transfers between devices, swap(): return lax.ppermute(block, 'pair', [(i, i ^ 1) for i in range(2)])  17.4 us
    pallas_call x1, Pallas kernels, attention_forward(): pl.pallas_call(kernel, grid=(pairs,), out_shape=jax.ShapeDtypeStruct((2 *...  16.6 us
    pallas_call x3, Pallas kernels, assemble(): pl.pallas_call(kernel, out_shape=[jax.ShapeDtypeStruct((chips, cores, row...  16.5 us
  transfers between devices with their start and end apart: 65, of which 18 were waited for; matrix products, arithmetic and copies ran while one was open for 28% of the time, Pallas kernels for 16%

profile of v1, /device:TPU:9, one launch (start us, length us, event | category | flops | bytes accessed | tf_op | source)
XLA Modules:
  0.0 461.6 jit_solution(15619998620657985769)
XLA Ops:
  18.7 5.6 %collective-permute-done.5 = bf16[1,32,4224]{2,1,0:T(8,128)(2,1)S(1)} collective-permute-done((bf16[1,32,4224]{2,1,0:T(8,128)(2,1)S(1)}, bf16[1,32,4224]{2,1,0:T(8,128)(2,1)S(1)}, u32[]{:S(2)}, u32[]{:S(2)}) %collective-permute-start.5) | collective-permute-done | bytes 270368 | tf_op jit(solution)/shard_map/ppermute | solution.py:34
  24.4 4.7 %collective-permute-done.4 = bf16[1,32,4224]{2,1,0:T(8,128)(2,1)S(1)} collective-permute-done((bf16[1,32,4224]{2,1,0:T(8,128)(2,1)S(1)}, bf16[1,32,4224]{2,1,0:T(8,128)(2,1)S(1)}, u32[]{:S(2)}, u32[]{:S(2)}) %collective-permute-start.4) | collective-permute-done | bytes 270368 | tf_op jit(solution)/shard_map/ppermute | solution.py:34
  37.1 8.0 %collective-permute-done.6 = bf16[2,32,4224]{2,1,0:T(8,128)(2,1)S(1)} collective-permute-done((bf16[2,32,4224]{2,1,0:T(8,128)(2,1)S(1)}, bf16[2,32,4224]{2,1,0:T(8,128)(2,1)S(1)}, u32[]{:S(2)}, u32[]{:S(2)}) %collective-permute-start.6) | collective-permute-done | bytes 540704 | tf_op jit(solution)/shard_map/ppermute | solution.py:32
  55.5 10.6 %collective-permute-done.25 = bf16[1,128,1024]{2,1,0:T(8,128)(2,1)S(1)} collective-permute-done((bf16[1,128,1024]{2,1,0:T(8,128)(2,1)S(1)}, bf16[1,128,1024]{2,1,0:T(8,128)(2,1)S(1)}, u32[]{:S(2)}, u32[]{:S(2)}) %collective-permute-start.25) | collective-permute-done | bytes 262176 | tf_op jit(solution)/shard_map/ppermute | solution.py:34
  67.4 5.2 %collective-permute-done.24 = bf16[1,128,1024]{2,1,0:T(8,128)(2,1)S(1)} collective-permute-done((bf16[1,128,1024]{2,1,0:T(8,128)(2,1)S(1)}, bf16[1,128,1024]{2,1,0:T(8,128)(2,1)S(1)}, u32[]{:S(2)}, u32[]{:S(2)}) %collective-permute-start.24) | collective-permute-done | bytes 262176 | tf_op jit(solution)/shard_map/ppermute | solution.py:34
  79.2 9.6 %collective-permute-start.10 = (bf16[4,32,4224]{2,1,0:T(8,128)(2,1)S(1)}, bf16[4,32,4224]{2,1,0:T(8,128)(2,1)S(1)}, u32[]{:S(2)}, u32[]{:S(2)}) collective-permute-start(bf16[4,32,4224]{2,1,0:T(8,128)(2,1)S(1)} %constant_dynamic-update-slice_fusion.refs_2_), channel_id=1, source_target_pairs={{0,1},{1,0},{2,3},{3,2},{4,5},{5,4},{6,7},{7,6},{8,9},{9,8},{10,11... | collective-permute-start | bytes 3244040 | tf_op jit(solution)/shard_map/ppermute | solution.py:34
  95.0 5.1 %collective-permute-done.22 = bf16[2,128,1024]{2,1,0:T(8,128)(2,1)S(1)} collective-permute-done((bf16[2,128,1024]{2,1,0:T(8,128)(2,1)S(1)}, bf16[2,128,1024]{2,1,0:T(8,128)(2,1)S(1)}, u32[]{:S(2)}, u32[]{:S(2)}) %collective-permute-start.22) | collective-permute-done | bytes 524320 | tf_op jit(solution)/shard_map/ppermute | solution.py:34
  108.3 7.9 %assemble.3 = (bf16[16,2,32,3072]{3,2,1,0:T(8,128)(2,1)}, bf16[16,2,32,1024]{3,2,1,0:T(8,128)(2,1)}, bf16[16,2,32,128]{3,2,1,0:T(8,128)(2,1)}) custom-call(bf16[4,32,4224]{2,1,0:T(8,128)(2,1)} %copy-done.4, bf16[4,32,4224]{2,1,0:T(8,128)(2,1)} %copy-done.15, bf16[4,32,4224]{2,1,0:T(8,128)(2,1)} %copy-done.13, bf16[4,32,4224]{2,1,0:T(8,128)(2,1)} %copy-done.14, ...), custom_call_target="tpu_custom_call" | custom-call | tf_op jit(solution)/shard_map/assemble/pallas_call | solution.py:103
  117.9 9.2 %convolution_convert_fusion.1.q_ref.k_ref.v_ref = bf16[512,3072]{1,0:T(8,128)(2,1)} fusion(bf16[1024,3072]{1,0:T(8,128)(2,1)} %bitcast.166, f32[1024]{0:T(1024)S(1)} %reshape.359, f32[1024]{0:T(1024)S(1)} %reshape.358, f32[512]{0:T(512)S(1)} %add_rsqrt_fusion.1, f32[512]{0:T(512)S(1)} %broadcast_multiply_fusion.5, ...), kind=kOutput, calls=%fused_computation.20 | convolution fusion | flops 3230662656 | bytes 10498049 | tf_op jit(solution)/shard_map/dot_general | solution.py:519
  127.1 16.6 %attention_forward.1 = bf16[512,1024]{1,0:T(8,128)(2,1)} custom-call(s32[2]{0:T(128)} %get-tuple-element.111.phone_ref, s32[2]{0:T(128)} %get-tuple-element.112.prompt_ref, s32[2]{0:T(128)} %fusion.54.target_ref, bf16[512,3072]{1,0:T(8,128)(2,1)} %convolution_convert_fusion.1.q_ref.k_ref.v_ref, ...), custom_call_target="tpu_custom_call" | custom-call | flops 805306368 | bytes 4194304 | tf_op jit(solution)/shard_map/attention_forward/pallas_call | solution.py:334
  148.9 5.4 %collective-permute-start.12 = (bf16[512,1024]{1,0:T(8,128)(2,1)}, bf16[512,1024]{1,0:T(8,128)(2,1)}, u32[]{:S(2)}, u32[]{:S(2)}) collective-permute-start(bf16[512,1024]{1,0:T(8,128)(2,1)} %add_convert_fusion), channel_id=1, source_target_pairs={{0,1},{1,0},{2,3},{3,2},{4,5},{5,4},{6,7},{7,6},{8,9},{9,8},{10,11... | collective-permute-start | bytes 3145736 | tf_op jit(solution)/shard_map/ppermute | solution.py:34
  165.6 7.0 %fusion.31 = f32[1024,2048]{1,0:T(8,128)S(1)} fusion(bf16[1024,2048]{1,0:T(8,128)(2,1)} %bitcast.136, bf16[512,1024]{1,0:T(8,128)(2,1)} %collective-permute-done.12, bf16[512,1024]{1,0:T(8,128)(2,1)} %add_convert_fusion), kind=kOutput, calls=%fused_computation.57 | convolution fusion | flops 4299161600 | bytes 14680064 | tf_op jit(solution)/shard_map/dot_general | solution.py:525
  172.6 7.0 %fusion.62 = f32[1024,1024]{1,0:T(8,128)} fusion(bf16[2048,1024]{1,0:T(8,128)(2,1)S(1)} %bitcast.138, f32[1024,2048]{1,0:T(8,128)S(1)} %fusion.31, f32[2048]{0:T(1024)S(1)} %bitcast.163), kind=kOutput, calls=%fused_computation.182 | convolution fusion | flops 4315938816 | bytes 16785408 | tf_op jit(solution)/shard_map/dot_general | solution.py:530
  179.6 10.9 %convert_reduce_fusion = (f32[2048]{0:T(1024)S(1)}, bf16[1024,2048]{1,0:T(8,128)(2,1)S(1)}) fusion(f32[1024,2048]{1,0:T(8,128)S(1)} %fusion.31, f32[2048]{0:T(1024)S(1)} %bitcast.164, bf16[2048,1024]{1,0:T(8,128)(2,1)S(1)} %bitcast.139, bf16[512,1024]{1,0:T(8,128)(2,1)} %collective-permute-done.31, bf16[512,1024]{1,0:T(8,128)(2,1)} %maximum_select_fusion.3), kind=kOutput, calls=%fused_computation.18 | convolution fusion | flops 4345296896 | bytes 18890752 | tf_op jit(solution)/shard_map/dot_general | solution.py:296
  190.6 9.5 %convolution_convert_fusion.3 = bf16[1024,2048]{1,0:T(8,128)(2,1)} fusion(bf16[1024,2048]{1,0:T(8,128)(2,1)S(1)} %get-tuple-element.110, bf16[512,1024]{1,0:T(8,128)(2,1)} %collective-permute-done.12, bf16[512,1024]{1,0:T(8,128)(2,1)} %add_convert_fusion), kind=kOutput, calls=%fused_computation.22 | convolution fusion | flops 4301258752 | bytes 10485760 | tf_op jit(solution)/shard_map/dot_general | solution.py:296
  205.4 12.6 %convolution_convert_fusion.2 = bf16[2048,1024]{1,0:T(8,128)(2,1)} fusion(bf16[512,1024]{1,0:T(8,128)(2,1)} %collective-permute-done.31, bf16[512,1024]{1,0:T(8,128)(2,1)} %maximum_select_fusion.3, f32[1024,2048]{1,0:T(8,128)} %copy-done.41, f32[2048]{0:T(1024)S(1)} %bitcast.165), kind=kOutput, calls=%fused_computation.21 | convolution fusion | flops 4322230272 | bytes 14688256 | tf_op jit(solution)/shard_map/dot_general | solution.py:296
  217.9 6.3 %fusion.66 = f32[1024,1024]{1,0:T(8,128)} fusion(bf16[1024,2048]{1,0:T(8,128)(2,1)S(1)} %copy-done.43, bf16[1024,2048]{1,0:T(8,128)(2,1)S(1)} %bitcast.137), kind=kOutput, calls=%fused_computation.185 | convolution fusion | flops 4294967296 | bytes 12582912 | tf_op jit(solution)/shard_map/dot_general | solution.py:296
  224.2 4.4 disassemble.5
  238.9 12.8 %collective-permute-done.58 = bf16[4,128,1024]{2,1,0:T(8,128)(2,1)S(1)} collective-permute-done((bf16[4,128,1024]{2,1,0:T(8,128)(2,1)}, bf16[4,128,1024]{2,1,0:T(8,128)(2,1)S(1)}, u32[]{:S(2)}, u32[]{:S(2)}) %collective-permute-start.58) | collective-permute-done | bytes 1048608 | tf_op jit(solution)/shard_map/ppermute | solution.py:32
  255.3 9.2 %collective-permute-done.51 = bf16[2,64,2048]{2,1,0:T(8,128)(2,1)S(1)} collective-permute-done((bf16[2,64,2048]{2,1,0:T(8,128)(2,1)S(1)}, bf16[2,64,2048]{2,1,0:T(8,128)(2,1)S(1)}, u32[]{:S(2)}, u32[]{:S(2)}) %collective-permute-start.51) | collective-permute-done | bytes 524320 | tf_op jit(solution)/shard_map/ppermute | solution.py:34
  287.8 20.6 %attention_backward.1 = (bf16[512,1024]{1,0:T(8,128)(2,1)}, bf16[512,1024]{1,0:T(8,128)(2,1)}, bf16[512,1024]{1,0:T(8,128)(2,1)}) custom-call(s32[2]{0:T(128)} %get-tuple-element.111.phone_ref, s32[2]{0:T(128)} %get-tuple-element.112.prompt_ref, s32[2]{0:T(128)} %fusion.54.target_ref, bf16[512,3072]{1,0:T(8,128)(2,1)} %convolution_convert_fusion.1.q_ref.k_ref.v_ref, ...), custom_call_target="tpu_custom_call" | custom-call | flops 2013265920 | bytes 7340032 | tf_op jit(solution)/shard_map/attention_backward/pallas_call | solution.py:410
  310.4 6.3 %convolution_convert_fusion = bf16[1024,3072]{1,0:T(8,128)(2,1)} fusion(bf16[512,3072]{1,0:T(8,128)(2,1)S(1)} %constant_dynamic-update-slice_fusion.9, f32[1024]{0:T(1024)S(1)} %reshape.359, f32[1024]{0:T(1024)S(1)} %reshape.358, f32[512]{0:T(512)S(1)} %add_rsqrt_fusion.1, f32[512]{0:T(512)S(1)} %broadcast_multiply_fusion.5, ...), kind=kOutput, calls=%fused_computation.19 | convolution fusion | flops 3232235520 | bytes 10498049 | tf_op jit(solution)/shard_map/dot_general | solution.py:296
  319.5 5.4 %core_send.1 = bf16[16,32,4096]{2,1,0:T(8,128)(2,1)} custom-call(bf16[16,2,32,3072]{3,2,1,0:T(8,128)(2,1)} %bitcast.130, bf16[16,2,32,1024]{3,2,1,0:T(8,128)(2,1)} %bitcast.133), custom_call_target="tpu_custom_call" | custom-call | tf_op jit(solution)/shard_map/core_send/pallas_call | solution.py:173
  325.5 6.8 %collective-permute-start.42 = (bf16[16,32,4096]{2,1,0:T(8,128)(2,1)}, bf16[16,32,4096]{2,1,0:T(8,128)(2,1)}, u32[]{:S(2)}, u32[]{:S(2)}) collective-permute-start(bf16[16,32,4096]{2,1,0:T(8,128)(2,1)} %core_send.1), channel_id=1, source_target_pairs={{0,1},{1,0},{2,3},{3,2},{4,5},{5,4},{6,7},{7,6},{8,9},{9,8},{10,11... | collective-permute-start | bytes 12582920 | tf_op jit(solution)/shard_map/ppermute | solution.py:34
  341.4 9.0 %fusion.27 = (f32[1024]{0:T(1024)S(1)}, f32[512]{0:T(512)S(1)}, f32[512]{0:T(512)S(1)}, f32[1024]{0:T(1024)S(1)}, f32[512,1024]{1,0:T(8,128)}) fusion(f32[512]{0:T(512)S(1)} %add_rsqrt_fusion.1, f32[512]{0:T(512)S(1)} %broadcast_multiply_fusion.5, bf16[256,1024]{1,0:T(8,128)(2,1)S(1)} %get-tuple-element.85, bf16[256,1024]{1,0:T(8,128)(2,1)S(1)} %collective-permute-done, ...), kind=kOutput, calls=%fused_computation.38 | convolution fusion | flops 3231183872 | bytes 12603393 | tf_op jit(solution)/shard_map/dot_general | solution.py:296
  350.7 5.8 %collective-permute-start.34 = (f32[16,256]{1,0:T(8,128)S(1)}, f32[16,256]{1,0:T(8,128)S(1)}, u32[]{:S(2)}, u32[]{:S(2)}) collective-permute-start(f32[16,256]{1,0:T(8,128)S(1)} %dynamic-slice_bitcast_fusion.9), channel_id=1, source_target_pairs={{0,1},{1,0},{2,3},{3,2},{4,5},{5,4},{6,7},{7,6},{8,9},{9,8},{10,11... | collective-permute-start | bytes 49160 | tf_op jit(solution)/shard_map/ppermute | solution.py:34
  369.5 7.5 %core_sum.1 = (bf16[4,32,4096]{2,1,0:T(8,128)(2,1)}, bf16[4,32,4096]{2,1,0:T(8,128)(2,1)}, bf16[4,32,4096]{2,1,0:T(8,128)(2,1)}, bf16[4,32,4096]{2,1,0:T(8,128)(2,1)}) custom-call(bf16[16,2,32,3072]{3,2,1,0:T(8,128)(2,1)} %bitcast.131, bf16[16,2,32,1024]{3,2,1,0:T(8,128)(2,1)} %bitcast.134, bf16[16,32,4096]{2,1,0:T(8,128)(2,1)} %collective-permute-done.42.refs_2_), custom_call_target="tpu_custom_call" | custom-call | tf_op jit(solution)/shard_map/core_sum/pallas_call | solution.py:202
  385.1 14.8 %collective-permute-done.43 = bf16[4,32,4096]{2,1,0:T(8,128)(2,1)} collective-permute-done((bf16[4,32,4096]{2,1,0:T(8,128)(2,1)}, bf16[4,32,4096]{2,1,0:T(8,128)(2,1)}, u32[]{:S(2)}, u32[]{:S(2)}) %collective-permute-start.43) | collective-permute-done | bytes 1048608 | tf_op jit(solution)/shard_map/ppermute | solution.py:32
  406.4 10.0 %collective-permute-done.44 = bf16[2,32,4096]{2,1,0:T(8,128)(2,1)S(1)} collective-permute-done((bf16[2,32,4096]{2,1,0:T(8,128)(2,1)S(1)}, bf16[2,32,4096]{2,1,0:T(8,128)(2,1)S(1)}, u32[]{:S(2)}, u32[]{:S(2)}) %collective-permute-start.44) | collective-permute-done | bytes 524320 | tf_op jit(solution)/shard_map/ppermute | solution.py:34
  417.7 15.8 %collective-permute-done.47 = bf16[2,32,4096]{2,1,0:T(8,128)(2,1)S(1)} collective-permute-done((bf16[2,32,4096]{2,1,0:T(8,128)(2,1)S(1)}, bf16[2,32,4096]{2,1,0:T(8,128)(2,1)S(1)}, u32[]{:S(2)}, u32[]{:S(2)}) %collective-permute-start.47) | collective-permute-done | bytes 524320 | tf_op jit(solution)/shard_map/ppermute | solution.py:32
  440.1 12.3 %collective-permute-done.48 = bf16[32,4096]{1,0:T(8,128)(2,1)S(1)} collective-permute-done((bf16[32,4096]{1,0:T(8,128)(2,1)S(1)}, bf16[32,4096]{1,0:T(8,128)(2,1)S(1)}, u32[]{:S(2)}, u32[]{:S(2)}) %collective-permute-start.48) | collective-permute-done | bytes 262176 | tf_op jit(solution)/shard_map/ppermute | solution.py:34
  452.3 7.4 %collective-permute-done.49 = bf16[32,4096]{1,0:T(8,128)(2,1)S(1)} collective-permute-done((bf16[32,4096]{1,0:T(8,128)(2,1)S(1)}, bf16[32,4096]{1,0:T(8,128)(2,1)S(1)}, u32[]{:S(2)}, u32[]{:S(2)}) %collective-permute-start.49) | collective-permute-done | bytes 262176 | tf_op jit(solution)/shard_map/ppermute | solution.py:34
  (318 shorter events, 170.2 us)
Async XLA Ops:
  6.5 22.5 %collective-permute-start.4 = (bf16[1,32,4224]{2,1,0:T(8,128)(2,1)S(1)}, bf16[1,32,4224]{2,1,0:T(8,128)(2,1)S(1)}, u32[]{:S(2)}, u32[]{:S(2)}) collective-permute-start(bf16[1,32,4224]{2,1,0:T(8,128)(2,1)S(1)} %fusion.42), channel_id=1, source_target_pairs={{0,8},{1,9},{2,10},{3,11},{4,12},{5,13},{6,14},{7,15},{8,0},{9,1},... | collective-permute-start | bytes 811016 | tf_op jit(solution)/shard_map/ppermute | solution.py:34
  45.1 43.7 %collective-permute-start.7 = (bf16[4,32,4224]{2,1,0:T(8,128)(2,1)S(1)}, bf16[4,32,4224]{2,1,0:T(8,128)(2,1)S(1)}, u32[]{:S(2)}, u32[]{:S(2)}) collective-permute-start(bf16[4,32,4224]{2,1,0:T(8,128)(2,1)S(1)} %constant_dynamic-update-slice_fusion.refs_2_), channel_id=1, source_target_pairs={{0,2},{1,3},{2,0},{3,1},{4,6},{5,7},{6,4},{7,5},{8,10},{9,11},{10,... | collective-permute-start | bytes 3244040 | tf_op jit(solution)/shard_map/ppermute | solution.py:34
  46.6 42.7 %collective-permute-start.3 = (bf16[4,32,4224]{2,1,0:T(8,128)(2,1)S(1)}, bf16[4,32,4224]{2,1,0:T(8,128)(2,1)S(1)}, u32[]{:S(2)}, u32[]{:S(2)}) collective-permute-start(bf16[4,32,4224]{2,1,0:T(8,128)(2,1)S(1)} %pad_maximum_fusion.6.refs_0_), channel_id=1, source_target_pairs={{0,16},{16,0},{1,17},{17,1},{2,18},{18,2},{3,19},{19,3},{4,20},{20... | collective-permute-start | bytes 3244040 | tf_op jit(solution)/shard_map/ppermute | solution.py:32
  79.2 23.4 %collective-permute-start.10 = (bf16[4,32,4224]{2,1,0:T(8,128)(2,1)S(1)}, bf16[4,32,4224]{2,1,0:T(8,128)(2,1)S(1)}, u32[]{:S(2)}, u32[]{:S(2)}) collective-permute-start(bf16[4,32,4224]{2,1,0:T(8,128)(2,1)S(1)} %constant_dynamic-update-slice_fusion.refs_2_), channel_id=1, source_target_pairs={{0,1},{1,0},{2,3},{3,2},{4,5},{5,4},{6,7},{7,6},{8,9},{9,8},{10,11... | collective-permute-start | bytes 3244040 | tf_op jit(solution)/shard_map/ppermute | solution.py:34
  100.1 48.7 %collective-permute-start.30 = (bf16[256,1024]{1,0:T(8,128)(2,1)}, bf16[256,1024]{1,0:T(8,128)(2,1)}, u32[]{:S(2)}, u32[]{:S(2)}) collective-permute-start(bf16[256,1024]{1,0:T(8,128)(2,1)} %get-tuple-element.81), channel_id=1, source_target_pairs={{0,16},{16,0},{1,17},{17,1},{2,18},{18,2},{3,19},{19,3},{4,20},{20... | collective-permute-start | bytes 1572872 | tf_op jit(solution)/shard_map/ppermute | solution.py:32
  102.6 54.4 %collective-permute-start.20 = (bf16[4,64,2048]{2,1,0:T(8,128)(2,1)}, bf16[4,64,2048]{2,1,0:T(8,128)(2,1)}, u32[]{:S(2)}, u32[]{:S(2)}) collective-permute-start(bf16[4,64,2048]{2,1,0:T(8,128)(2,1)} %constant_dynamic-update-slice_fusion.3.refs_2_), channel_id=1, source_target_pairs={{0,2},{1,3},{2,0},{3,1},{4,6},{5,7},{6,4},{7,5},{8,10},{9,11},{10,... | collective-permute-start | bytes 3145736 | tf_op jit(solution)/shard_map/ppermute | solution.py:34
  104.7 52.2 %collective-permute-start.16 = (bf16[4,64,2048]{2,1,0:T(8,128)(2,1)}, bf16[4,64,2048]{2,1,0:T(8,128)(2,1)}, u32[]{:S(2)}, u32[]{:S(2)}) collective-permute-start(bf16[4,64,2048]{2,1,0:T(8,128)(2,1)} %pad_maximum_fusion.7.refs_0_), channel_id=1, source_target_pairs={{0,16},{16,0},{1,17},{17,1},{2,18},{18,2},{3,19},{19,3},{4,20},{20... | collective-permute-start | bytes 3145736 | tf_op jit(solution)/shard_map/ppermute | solution.py:32
  104.8 56.4 %collective-permute-start.27 = (bf16[4,128,1024]{2,1,0:T(8,128)(2,1)}, bf16[4,128,1024]{2,1,0:T(8,128)(2,1)}, u32[]{:S(2)}, u32[]{:S(2)}) collective-permute-start(bf16[4,128,1024]{2,1,0:T(8,128)(2,1)} %constant_dynamic-update-slice_fusion.6.refs_2_), channel_id=1, source_target_pairs={{0,2},{1,3},{2,0},{3,1},{4,6},{5,7},{6,4},{7,5},{8,10},{9,11},{10,... | collective-permute-start | bytes 3145736 | tf_op jit(solution)/shard_map/ppermute | solution.py:34
  107.2 54.0 %collective-permute-start.23 = (bf16[4,128,1024]{2,1,0:T(8,128)(2,1)}, bf16[4,128,1024]{2,1,0:T(8,128)(2,1)}, u32[]{:S(2)}, u32[]{:S(2)}) collective-permute-start(bf16[4,128,1024]{2,1,0:T(8,128)(2,1)} %pad_maximum_fusion.8.refs_0_), channel_id=1, source_target_pairs={{0,16},{16,0},{1,17},{17,1},{2,18},{18,2},{3,19},{19,3},{4,20},{20... | collective-permute-start | bytes 3145736 | tf_op jit(solution)/shard_map/ppermute | solution.py:32
  156.9 22.7 %collective-permute-start.31 = (bf16[512,1024]{1,0:T(8,128)(2,1)}, bf16[512,1024]{1,0:T(8,128)(2,1)}, u32[]{:S(2)}, u32[]{:S(2)}) collective-permute-start(bf16[512,1024]{1,0:T(8,128)(2,1)} %maximum_select_fusion.3), channel_id=1, source_target_pairs={{0,1},{1,0},{2,3},{3,2},{4,5},{5,4},{6,7},{7,6},{8,9},{9,8},{10,11... | collective-permute-start | bytes 3145736 | tf_op jit(solution)/shard_map/ppermute | solution.py:34
  204.4 30.6 %collective-permute-start.50 = (bf16[4,64,2048]{2,1,0:T(8,128)(2,1)}, bf16[4,64,2048]{2,1,0:T(8,128)(2,1)}, u32[]{:S(2)}, u32[]{:S(2)}) collective-permute-start(bf16[4,64,2048]{2,1,0:T(8,128)(2,1)} %get-tuple-element.52), channel_id=1, source_target_pairs={{0,16},{16,0},{1,17},{17,1},{2,18},{18,2},{3,19},{19,3},{4,20},{20... | collective-permute-start | bytes 3145736 | tf_op jit(solution)/shard_map/ppermute | solution.py:32
  204.7 32.1 %collective-permute-start.53 = (bf16[4,64,2048]{2,1,0:T(8,128)(2,1)}, bf16[4,64,2048]{2,1,0:T(8,128)(2,1)}, u32[]{:S(2)}, u32[]{:S(2)}) collective-permute-start(bf16[4,64,2048]{2,1,0:T(8,128)(2,1)} %get-tuple-element.54), channel_id=1, source_target_pairs={{0,2},{1,3},{2,0},{3,1},{4,6},{5,7},{6,4},{7,5},{8,10},{9,11},{10,... | collective-permute-start | bytes 3145736 | tf_op jit(solution)/shard_map/ppermute | solution.py:34
  228.7 23.0 %collective-permute-start.58 = (bf16[4,128,1024]{2,1,0:T(8,128)(2,1)}, bf16[4,128,1024]{2,1,0:T(8,128)(2,1)S(1)}, u32[]{:S(2)}, u32[]{:S(2)}) collective-permute-start(bf16[4,128,1024]{2,1,0:T(8,128)(2,1)} %get-tuple-element.56), channel_id=1, source_target_pairs={{0,16},{16,0},{1,17},{17,1},{2,18},{18,2},{3,19},{19,3},{4,20},{20... | collective-permute-start | bytes 3145736 | tf_op jit(solution)/shard_map/ppermute | solution.py:32
  230.0 24.0 %collective-permute-start.61 = (bf16[4,128,1024]{2,1,0:T(8,128)(2,1)}, bf16[4,128,1024]{2,1,0:T(8,128)(2,1)S(1)}, u32[]{:S(2)}, u32[]{:S(2)}) collective-permute-start(bf16[4,128,1024]{2,1,0:T(8,128)(2,1)} %get-tuple-element.58), channel_id=1, source_target_pairs={{0,2},{1,3},{2,0},{3,1},{4,6},{5,7},{6,4},{7,5},{8,10},{9,11},{10,... | collective-permute-start | bytes 3145736 | tf_op jit(solution)/shard_map/ppermute | solution.py:34
  233.3 46.8 %collective-permute-start.28 = (f32[512,1024]{1,0:T(8,128)S(1)}, f32[512,1024]{1,0:T(8,128)S(1)}, u32[]{:S(2)}, u32[]{:S(2)}) collective-permute-start(f32[512,1024]{1,0:T(8,128)S(1)} %slice.302), channel_id=1, source_target_pairs={{0,1},{1,0},{2,3},{3,2},{4,5},{5,4},{6,7},{7,6},{8,9},{9,8},{10,11... | collective-permute-start | bytes 6291464 | tf_op jit(solution)/shard_map/ppermute | solution.py:34
  235.0 42.7 %collective-permute-start.32 = (f32[512,1024]{1,0:T(8,128)S(1)}, f32[512,1024]{1,0:T(8,128)S(1)}, u32[]{:S(2)}, u32[]{:S(2)}) collective-permute-start(f32[512,1024]{1,0:T(8,128)S(1)} %slice.304), channel_id=1, source_target_pairs={{0,1},{1,0},{2,3},{3,2},{4,5},{5,4},{6,7},{7,6},{8,9},{9,8},{10,11... | collective-permute-start | bytes 6291464 | tf_op jit(solution)/shard_map/ppermute | solution.py:34
  236.7 27.8 %collective-permute-start.51 = (bf16[2,64,2048]{2,1,0:T(8,128)(2,1)S(1)}, bf16[2,64,2048]{2,1,0:T(8,128)(2,1)S(1)}, u32[]{:S(2)}, u32[]{:S(2)}) collective-permute-start(bf16[2,64,2048]{2,1,0:T(8,128)(2,1)S(1)} %get-tuple-element.73), channel_id=1, source_target_pairs={{0,2},{1,3},{2,0},{3,1},{4,6},{5,7},{6,4},{7,5},{8,10},{9,11},{10,... | collective-permute-start | bytes 1572872 | tf_op jit(solution)/shard_map/ppermute | solution.py:34
  254.0 21.8 %collective-permute-start.59 = (bf16[2,128,1024]{2,1,0:T(8,128)(2,1)S(1)}, bf16[2,128,1024]{2,1,0:T(8,128)(2,1)S(1)}, u32[]{:S(2)}, u32[]{:S(2)}) collective-permute-start(bf16[2,128,1024]{2,1,0:T(8,128)(2,1)S(1)} %get-tuple-element.71), channel_id=1, source_target_pairs={{0,2},{1,3},{2,0},{3,1},{4,6},{5,7},{6,4},{7,5},{8,10},{9,11},{10,... | collective-permute-start | bytes 1572872 | tf_op jit(solution)/shard_map/ppermute | solution.py:34
  265.4 59.4 %collective-permute-start.52 = (bf16[64,2048]{1,0:T(8,128)(2,1)}, bf16[64,2048]{1,0:T(8,128)(2,1)S(1)}, u32[]{:S(2)}, u32[]{:S(2)}) collective-permute-start(bf16[64,2048]{1,0:T(8,128)(2,1)} %fusion.44), channel_id=1, source_target_pairs={{0,4},{1,5},{2,6},{3,7},{4,0},{5,1},{6,2},{7,3},{8,12},{9,13},{10,... | collective-permute-start | bytes 786440 | tf_op jit(solution)/shard_map/ppermute | solution.py:34
  273.4 52.2 %collective-permute-start.55 = (bf16[64,2048]{1,0:T(8,128)(2,1)}, bf16[64,2048]{1,0:T(8,128)(2,1)}, u32[]{:S(2)}, u32[]{:S(2)}) collective-permute-start(bf16[64,2048]{1,0:T(8,128)(2,1)} %get-tuple-element.90), channel_id=1, source_target_pairs={{0,8},{1,9},{2,10},{3,11},{4,12},{5,13},{6,14},{7,15},{8,0},{9,1},... | collective-permute-start | bytes 786440 | tf_op jit(solution)/shard_map/ppermute | solution.py:34
  275.8 56.6 %collective-permute-start.56 = (bf16[64,2048]{1,0:T(8,128)(2,1)}, bf16[64,2048]{1,0:T(8,128)(2,1)}, u32[]{:S(2)}, u32[]{:S(2)}) collective-permute-start(bf16[64,2048]{1,0:T(8,128)(2,1)} %get-tuple-element.91), channel_id=1, source_target_pairs={{0,12},{1,13},{2,14},{3,15},{4,8},{5,9},{6,10},{7,11},{8,4},{9,5},... | collective-permute-start | bytes 786440 | tf_op jit(solution)/shard_map/ppermute | solution.py:34
  277.7 57.8 %collective-permute-start.60 = (bf16[128,1024]{1,0:T(8,128)(2,1)}, bf16[128,1024]{1,0:T(8,128)(2,1)}, u32[]{:S(2)}, u32[]{:S(2)}) collective-permute-start(bf16[128,1024]{1,0:T(8,128)(2,1)} %fusion.45), channel_id=1, source_target_pairs={{0,4},{1,5},{2,6},{3,7},{4,0},{5,1},{6,2},{7,3},{8,12},{9,13},{10,... | collective-permute-start | bytes 786440 | tf_op jit(solution)/shard_map/ppermute | solution.py:34
  280.2 55.4 %collective-permute-start.63 = (bf16[128,1024]{1,0:T(8,128)(2,1)}, bf16[128,1024]{1,0:T(8,128)(2,1)}, u32[]{:S(2)}, u32[]{:S(2)}) collective-permute-start(bf16[128,1024]{1,0:T(8,128)(2,1)} %get-tuple-element.86), channel_id=1, source_target_pairs={{0,8},{1,9},{2,10},{3,11},{4,12},{5,13},{6,14},{7,15},{8,0},{9,1},... | collective-permute-start | bytes 786440 | tf_op jit(solution)/shard_map/ppermute | solution.py:34
  325.5 43.9 %collective-permute-start.42 = (bf16[16,32,4096]{2,1,0:T(8,128)(2,1)}, bf16[16,32,4096]{2,1,0:T(8,128)(2,1)}, u32[]{:S(2)}, u32[]{:S(2)}) collective-permute-start(bf16[16,32,4096]{2,1,0:T(8,128)(2,1)} %core_send.1), channel_id=1, source_target_pairs={{0,1},{1,0},{2,3},{3,2},{4,5},{5,4},{6,7},{7,6},{8,9},{9,8},{10,11... | collective-permute-start | bytes 12582920 | tf_op jit(solution)/shard_map/ppermute | solution.py:34
  335.5 29.5 %collective-permute-start.57 = (f32[32,2048]{1,0:T(8,128)}, f32[32,2048]{1,0:T(8,128)S(1)}, u32[]{:S(2)}, u32[]{:S(2)}) collective-permute-start(f32[32,2048]{1,0:T(8,128)} %get-tuple-element.89), channel_id=1, source_target_pairs={{0,1},{1,0},{2,3},{3,2},{4,5},{5,4},{6,7},{7,6},{8,9},{9,8},{10,11... | collective-permute-start | bytes 786440 | tf_op jit(solution)/shard_map/ppermute | solution.py:34
  340.2 96.0 %collective-permute-start.29 = (bf16[256,1024]{1,0:T(8,128)(2,1)}, bf16[256,1024]{1,0:T(8,128)(2,1)}, u32[]{:S(2)}, u32[]{:S(2)}) collective-permute-start(bf16[256,1024]{1,0:T(8,128)(2,1)} %get-tuple-element.83), channel_id=1, source_target_pairs={{0,16},{16,0},{1,17},{17,1},{2,18},{18,2},{3,19},{19,3},{4,20},{20... | collective-permute-start | bytes 1572872 | tf_op jit(solution)/shard_map/ppermute | solution.py:32
  377.0 22.9 %collective-permute-start.43 = (bf16[4,32,4096]{2,1,0:T(8,128)(2,1)}, bf16[4,32,4096]{2,1,0:T(8,128)(2,1)}, u32[]{:S(2)}, u32[]{:S(2)}) collective-permute-start(bf16[4,32,4096]{2,1,0:T(8,128)(2,1)} %get-tuple-element.48), channel_id=1, source_target_pairs={{0,16},{16,0},{1,17},{17,1},{2,18},{18,2},{3,19},{19,3},{4,20},{20... | collective-permute-start | bytes 3145736 | tf_op jit(solution)/shard_map/ppermute | solution.py:32
  382.4 56.1 %collective-permute-start.33 = (f32[256,1024]{1,0:T(8,128)S(1)}, f32[256,1024]{1,0:T(8,128)S(1)}, u32[]{:S(2)}, u32[]{:S(2)}) collective-permute-start(f32[256,1024]{1,0:T(8,128)S(1)} %get-tuple-element.77), channel_id=1, source_target_pairs={{0,16},{16,0},{1,17},{17,1},{2,18},{18,2},{3,19},{19,3},{4,20},{20... | collective-permute-start | bytes 3145736 | tf_op jit(solution)/shard_map/ppermute | solution.py:32
  383.5 21.7 %collective-permute-start.46 = (bf16[4,32,4096]{2,1,0:T(8,128)(2,1)}, bf16[4,32,4096]{2,1,0:T(8,128)(2,1)S(1)}, u32[]{:S(2)}, u32[]{:S(2)}) collective-permute-start(bf16[4,32,4096]{2,1,0:T(8,128)(2,1)} %get-tuple-element.50), channel_id=1, source_target_pairs={{0,2},{1,3},{2,0},{3,1},{4,6},{5,7},{6,4},{7,5},{8,10},{9,11},{10,... | collective-permute-start | bytes 3145736 | tf_op jit(solution)/shard_map/ppermute | solution.py:34
  405.3 28.2 %collective-permute-start.47 = (bf16[2,32,4096]{2,1,0:T(8,128)(2,1)S(1)}, bf16[2,32,4096]{2,1,0:T(8,128)(2,1)S(1)}, u32[]{:S(2)}, u32[]{:S(2)}) collective-permute-start(bf16[2,32,4096]{2,1,0:T(8,128)(2,1)S(1)} %add_convert_fusion.12), channel_id=1, source_target_pairs={{0,16},{16,0},{1,17},{17,1},{2,18},{18,2},{3,19},{19,3},{4,20},{20... | collective-permute-start | bytes 1572872 | tf_op jit(solution)/shard_map/ppermute | solution.py:32
  416.5 23.6 %collective-permute-start.45 = (bf16[32,4096]{1,0:T(8,128)(2,1)S(1)}, bf16[32,4096]{1,0:T(8,128)(2,1)S(1)}, u32[]{:S(2)}, u32[]{:S(2)}) collective-permute-start(bf16[32,4096]{1,0:T(8,128)(2,1)S(1)} %fusion.43), channel_id=1, source_target_pairs={{0,4},{1,5},{2,6},{3,7},{4,0},{5,1},{6,2},{7,3},{8,12},{9,13},{10,... | collective-permute-start | bytes 786440 | tf_op jit(solution)/shard_map/ppermute | solution.py:34
  435.3 24.5 %collective-permute-start.49 = (bf16[32,4096]{1,0:T(8,128)(2,1)S(1)}, bf16[32,4096]{1,0:T(8,128)(2,1)S(1)}, u32[]{:S(2)}, u32[]{:S(2)}) collective-permute-start(bf16[32,4096]{1,0:T(8,128)(2,1)S(1)} %get-tuple-element.93), channel_id=1, source_target_pairs={{0,12},{1,13},{2,14},{3,15},{4,8},{5,9},{6,10},{7,11},{8,4},{9,5},... | collective-permute-start | bytes 786440 | tf_op jit(solution)/shard_map/ppermute | solution.py:34
  (77 other events, 886.6 us)

commit v2 on v0

v2 whole, which is shorter than its diff:
```python
import functools

import jax
import jax.numpy as jnp
from jax import lax
from jax.experimental import pallas as pl
from jax.experimental.pallas import tpu as pltpu
from jax.sharding import PartitionSpec as P

D = 1024
HEADS = 16
HEAD = 64
FF = 4096
ROW = 256
MICRO = 2
BF = jnp.bfloat16
F32 = jnp.float32
NEG = -1e30


def position():
    row = lax.axis_index("rows")
    return lax.axis_index("pair"), row // 4, (row // 2) % 2, row % 2


def depth():
    return lax.axis_size("rows") // 4


def swap(block, way):
    if way == "y":
        return lax.ppermute(block, "pair", [(i, i ^ 1) for i in range(2)])
    count = lax.axis_size("rows")
    return lax.ppermute(block, "rows", [(i, i ^ way) for i in range(count)])


def after(block, *others):
    return lax.optimization_barrier((block, *others))[0]


class Chain:
    def __init__(self):
        self.last = None

    def __call__(self, step, *args):
        if self.last is not None:
            args, _ = lax.optimization_barrier((args, self.last))
        out = step(*args)
        self.last = out
        return out


def z_groups():
    count = lax.axis_size("rows")
    return [[z * 4 + low for z in range(count // 4)] for low in range(4)]


def z_gather(block):
    return lax.all_gather(block, "rows", axis_index_groups=z_groups())


def z_scatter(column):
    return lax.psum_scatter(column, "rows", scatter_dimension=0, axis_index_groups=z_groups())


class Gather:
    def __init__(self, chain, by_permutes):
        self.chain = chain
        self.rel_z = by_permutes and depth() == 4

    def over_z(self, block, *first):
        block = after(block, *first)
        if self.rel_z:
            self.column = [block[None]] + [swap(block[None], 4 * k) for k in range(1, 4)]
            return self.column[1:]
        self.column = [z_gather(block)]
        return self.column

    def one(self, *first, extras=()):
        half = depth() // 2

        def halves(column, extras):
            if self.rel_z:
                left, right = jnp.concatenate(column[:2], 0), jnp.concatenate(column[2:], 0)
            else:
                left, right = column[0][:half], column[0][half:]
            return beside((left, right), extras)

        self.halves = self.chain(halves, self.column, extras)
        return self.send(*first)

    def one_halves(self):
        half = depth() // 2
        self.halves = self.chain(lambda v: (v[:half], v[half:]), self.column[0])

    def send(self, *first):
        left, right = lax.optimization_barrier((self.halves, first))[0]
        self.sides = swap(left, 2), swap(right, "y")
        return list(self.sides)

    def two(self, *first, extras=()):
        rows, cols = self.column[0].shape[-2:]
        block = (depth() // 2, rows, cols)

        def planes(halves, sides):
            left, right = halves
            left_x, right_y = sides
            if not extras:
                return jnp.concatenate([left, left_x], 0), jnp.concatenate([right, right_y], 0)
            main = [v[:, :cols].reshape(block) for v in (left, left_x, right, right_y)]
            more = [v[:, cols:].reshape(extras) for v in (left, left_x, right, right_y)]
            return (
                jnp.concatenate(main[:2], 0),
                jnp.concatenate(main[2:], 0),
                jnp.stack(more, 0),
            )

        sides = lax.optimization_barrier((self.sides, first))[0]
        self.planes = self.chain(planes, self.halves, sides)
        left, right = self.planes[:2]
        left_y, right_x = swap(left, "y"), swap(right, 2)
        half = depth() // 2
        low, high = range(half), range(half, 2 * half)
        self.pieces = [
            (left, [(0, i, 0) for i in low] + [(0, i, 1) for i in low]),
            (left_y, [(1, i, 0) for i in low] + [(1, i, 1) for i in low]),
            (right, [(0, i, 0) for i in high] + [(1, i, 0) for i in high]),
            (right_x, [(0, i, 1) for i in high] + [(1, i, 1) for i in high]),
        ]
        return [left_y, right_x]


def beside(blocks, extras):
    if not extras:
        return tuple(blocks)
    out = []
    for block, extra in zip(blocks, extras):
        rows = block.shape[0] * block.shape[1]
        out.append(
            jnp.concatenate([block.reshape(rows, -1), extra.reshape(rows, -1)], 1)
        )
    return tuple(out)


class GatherXZY:
    def __init__(self, chain):
        self.chain = chain

    def over_z(self, lines, *first):
        self.column = z_gather(after(lines, *first))
        return self.column

    def two(self, *first):
        def cut(column):
            shape = (2 * depth(), *column.shape[2:])
            return column[:, :2].reshape(shape), column[:, 2:].reshape(shape)

        upper, lower = self.chain(cut, after(self.column, *first))
        upper_y, lower_x = swap(upper, "y"), swap(lower, 2)
        ids = range(depth())
        self.pieces = [
            (upper, [(0, i, j) for i in ids for j in range(2)]),
            (upper_y, [(1, i, j) for i in ids for j in range(2)]),
            (lower, [(j, i, 0) for i in ids for j in range(2)]),
            (lower_x, [(j, i, 1) for i in ids for j in range(2)]),
        ]
        return [upper_y, lower_x]


def chip_slot(chip, where, rel_z):
    jy, jz, jx = chip
    y, z, x, _ = where
    z_at = (z ^ jz) if rel_z else jz
    return ((y ^ jy) * depth() + z_at) * 2 + (x ^ jx)


def layout_yzx():
    ids = range(depth())
    return [
        [(1, i, j) for i in ids for j in range(2)],
        [(0, i, j) for i in ids for j in range(2)],
        [(j, i, 1) for i in ids for j in range(2)],
        [(j, i, 0) for i in ids for j in range(2)],
    ]


def layout_yxz():
    half = depth() // 2
    low, high = range(half), range(half, 2 * half)
    return [
        [(1, i, j) for j in range(2) for i in low],
        [(0, i, j) for j in range(2) for i in low],
        [(j, i, 1) for j in range(2) for i in high],
        [(j, i, 0) for j in range(2) for i in high],
    ]


def plus(left, right):
    return (left.astype(F32) + right.astype(F32)).astype(left.dtype)


class Scatter:
    def __init__(self, chain, by_permutes):
        self.chain = chain
        self.rel_z = by_permutes and depth() == 4

    def one(self, parts, *first):
        self.parts = parts
        left, _, right, _ = parts
        self.sides = swap(after(left, *first), "y"), swap(after(right, *first), 2)
        return list(self.sides)

    def two(self, *first, extras=()):
        half = depth() // 2

        def add(left, left_in, right, right_in, extras):
            send = (plus(left[half:], left_in[half:]), plus(right[half:], right_in[half:]))
            return (
                *beside(send, extras),
                plus(left[:half], left_in[:half]),
                plus(right[:half], right_in[:half]),
            )

        _, left, _, right = self.parts
        left_in, right_in = lax.optimization_barrier((self.sides, first))[0]
        self.sums = self.chain(add, left, left_in, right, right_in, extras)
        self.ends = swap(self.sums[0], 2), swap(self.sums[1], "y")
        return list(self.ends)

    def over_z(self, *first):
        _, _, left, right = self.sums
        left_in, right_in = self.ends

        def add(left, left_in, right, right_in):
            left_in, right_in = (
                v if v.ndim == 3 else v[:, : left.shape[2]].reshape(left.shape)
                for v in (left_in, right_in)
            )
            if self.rel_z:
                return (
                    plus(left[1], left_in[1]),
                    *plus(right, right_in),
                    left[0].astype(F32) + left_in[0].astype(F32),
                )
            return jnp.concatenate([plus(left, left_in), plus(right, right_in)], 0)

        made = self.chain(add, left, left_in, right, right_in)
        if not self.rel_z:
            return z_scatter(after(made, *first))
        one, two, three, own = made
        return own, swap(one, 4), swap(two, 8), swap(three, 12)

    def total(self, parts):
        if not self.rel_z:
            return parts.astype(F32)
        own, *arrived = parts

        def add(own, *arrived):
            for part in arrived:
                own = own + part.astype(F32)
            return own

        return self.chain(add, own, *arrived)


class ScatterYZX:
    def __init__(self, chain):
        self.chain = chain

    def one(self, parts, *first):
        self.parts = parts
        left, _, right, _ = parts
        self.sides = swap(after(left, *first), "y"), swap(after(right, *first), 2)
        return list(self.sides)

    def over_z(self, *first):
        def add(left, left_in, right, right_in):
            shape = (depth(), 2, *left.shape[1:])
            upper, lower = plus(left, left_in).reshape(shape), plus(right, right_in).reshape(shape)
            return jnp.concatenate([upper, lower], 1)

        _, left, _, right = self.parts
        self.lines = z_scatter(self.chain(add, left, self.sides[0], right, self.sides[1]))
        return self.lines

    def last(self):
        def cut(lines):
            lines = lines.reshape(4, *lines.shape[-2:])
            return lines[1], lines[3], lines[0], lines[2]

        return self.chain(cut, self.lines)


def ordered(flag, own, other, axis):
    return jnp.where(
        flag == 0,
        jnp.concatenate([own, other], axis),
        jnp.concatenate([other, own], axis),
    )


def frames(index, phone, prompt, target, segs):
    pre_end = ends_of([phone[s] + prompt[s] for s in range(segs)])
    tgt_end = ends_of([target[s] for s in range(segs)])
    is_target = index >= ROW
    local = jnp.where(is_target, index - ROW, index)
    seg = jnp.zeros_like(index)
    for s in range(segs):
        edge = jnp.where(is_target, tgt_end[s], pre_end[s])
        seg = seg + jnp.where(local >= edge, 1, 0)
    start = jnp.zeros_like(index)
    phones = jnp.zeros_like(index)
    prompts = jnp.zeros_like(index)
    for s in range(segs):
        pick = seg == s
        pre_start = pre_end[s] - phone[s] - prompt[s]
        tgt_start = tgt_end[s] - target[s]
        start = jnp.where(pick, jnp.where(is_target, tgt_start, pre_start), start)
        phones = jnp.where(pick, phone[s], phones)
        prompts = jnp.where(pick, prompt[s], prompts)
    off = local - start
    is_phone = jnp.where(is_target, 0, jnp.where(off < phones, 1, 0))
    pos = jnp.where(is_target, prompts + off, off - phones)
    return seg, is_phone, pos


def ends_of(lengths):
    out, total = [], 0
    for length in lengths:
        total = total + length
        out.append(total)
    return out


def bias_of(query, key):
    q_seg, q_phone, q_pos = query
    k_seg, k_phone, k_pos = key
    audio = (k_phone == 1) | (k_pos <= q_pos)
    good = (q_seg == k_seg) & (((q_phone == 1) & (k_phone == 1)) | ((q_phone == 0) & audio))
    return jnp.where(good, 0.0, NEG)


def bdot(left, right, dims):
    return lax.dot_general(left, right, (dims, ((), ())), preferred_element_type=F32)


NT = ((1,), (1,))
NN = ((1,), (0,))
TN = ((0,), (0,))


def attention_forward(qkv, phone, prompt, target):
    segs = phone.shape[0]
    group = 2

    def kernel(phone_ref, prompt_ref, target_ref, q_ref, k_ref, v_ref, out_ref, bias_ref):
        @pl.when(pl.program_id(0) == 0)
        def _():
            ph = [phone_ref[s] for s in range(segs)]
            pr = [prompt_ref[s] for s in range(segs)]
            tg = [target_ref[s] for s in range(segs)]
            rows = lax.broadcasted_iota(jnp.int32, (2 * ROW, 1), 0)
            cols = lax.broadcasted_iota(jnp.int32, (1, 2 * ROW), 1)
            bias_ref[...] = bias_of(
                frames(cols, ph, pr, tg, segs), frames(rows, ph, pr, tg, segs)
            )

        lane = lax.broadcasted_iota(jnp.int32, (1, 2 * HEAD), 1)
        zero = jnp.zeros((), BF)
        scale = jnp.asarray(HEAD**-0.5, BF)
        for pair in range(group):
            cols = slice(pair * 2 * HEAD, (pair + 1) * 2 * HEAD)
            for rows, keys in ((0, ROW), (ROW, 2 * ROW)):
                at = slice(rows, rows + ROW)
                outs = []
                for j in range(2):
                    q = jnp.where((lane // HEAD) == j, q_ref[at, cols] * scale, zero)
                    s = bdot(k_ref[:keys, cols], q, NT) + bias_ref[:keys, at]
                    e = jnp.exp(s - jnp.max(s, 0, keepdims=True))
                    p = (e * (1.0 / jnp.sum(e, 0, keepdims=True))).astype(BF)
                    outs.append(bdot(v_ref[:keys, cols], p, TN)[j * HEAD : (j + 1) * HEAD])
                out_ref[at, cols] = jnp.transpose(jnp.concatenate(outs, 0)).astype(BF)

    steps = HEADS // 2 // group
    smem = pl.BlockSpec(memory_space=pltpu.SMEM)
    part = (2 * ROW, 2 * HEAD * group)
    return pl.pallas_call(
        kernel,
        grid=(steps,),
        out_shape=jax.ShapeDtypeStruct((2 * ROW, D), BF),
        in_specs=[
            smem,
            smem,
            smem,
            pl.BlockSpec(part, lambda h: (0, h)),
            pl.BlockSpec(part, lambda h: (0, h + steps)),
            pl.BlockSpec(part, lambda h: (0, h + 2 * steps)),
        ],
        out_specs=pl.BlockSpec(part, lambda h: (0, h)),
        scratch_shapes=[pltpu.VMEM((2 * ROW, 2 * ROW), F32)],
        compiler_params=pltpu.CompilerParams(vmem_limit_bytes=16 << 20),
        cost_estimate=pl.CostEstimate(flops=1 << 20, bytes_accessed=1 << 10, transcendentals=0),
        name="attention_forward",
    )(phone, prompt, target, qkv, qkv, qkv)


def attention_backward(qkv, grad_mixed, phone, prompt, target):
    segs = phone.shape[0]
    group = 2

    def kernel(
        phone_ref, prompt_ref, target_ref, q_ref, k_ref, v_ref, g_ref, out_ref, bias_ref
    ):
        @pl.when(pl.program_id(0) == 0)
        def _():
            ph = [phone_ref[s] for s in range(segs)]
            pr = [prompt_ref[s] for s in range(segs)]
            tg = [target_ref[s] for s in range(segs)]
            rows = lax.broadcasted_iota(jnp.int32, (2 * ROW, 1), 0)
            cols = lax.broadcasted_iota(jnp.int32, (1, 2 * ROW), 1)
            bias_ref[...] = bias_of(
                frames(cols, ph, pr, tg, segs), frames(rows, ph, pr, tg, segs)
            )

        lane = lax.broadcasted_iota(jnp.int32, (1, 2 * HEAD), 1)
        zero = jnp.zeros((), BF)
        scale = HEAD**-0.5
        for pair in range(group):
            cols = slice(pair * 2 * HEAD, (pair + 1) * 2 * HEAD)
            dks, dvs = {}, {}
            for rows, keys in ((0, ROW), (ROW, 2 * ROW)):
                at = slice(rows, rows + ROW)
                dqs = []
                for j in range(2):
                    sel = (lane // HEAD) == j
                    q_all, g_all = q_ref[at, cols], g_ref[at, cols]
                    q = jnp.where(sel, q_all * jnp.asarray(scale, BF), zero)
                    g = jnp.where(sel, g_all, zero)
                    k, v = k_ref[:keys, cols], v_ref[:keys, cols]
                    s = bdot(k, q, NT) + bias_ref[:keys, at]
                    dp = bdot(v, g, NT)
                    e = jnp.exp(s - jnp.max(s, 0, keepdims=True))
                    p = e * (1.0 / jnp.sum(e, 0, keepdims=True))
                    inner = jnp.sum(dp * p, 0, keepdims=True)
                    ds = (p * (dp - inner)).astype(BF)
                    dvs[rows, j] = bdot(p.astype(BF), g_all, NN)
                    dks[rows, j] = bdot(ds, q_all, NN)
                    dqs.append(bdot(k, ds, TN)[j * HEAD : (j + 1) * HEAD])
                dq = jnp.transpose(jnp.concatenate(dqs, 0)) * scale
                out_ref[0, at, cols] = dq.astype(BF)
            low = lane < HEAD
            for place, part, factor in ((1, dks, scale), (2, dvs, 1.0)):
                early = jnp.where(low, part[0, 0], part[0, 1])
                late = jnp.where(low, part[ROW, 0], part[ROW, 1])
                out_ref[place, :ROW, cols] = ((early + late[:ROW]) * factor).astype(BF)
                out_ref[place, ROW:, cols] = (late[ROW:] * factor).astype(BF)

    steps = HEADS // 2 // group
    smem = pl.BlockSpec(memory_space=pltpu.SMEM)
    block = (2 * ROW, 2 * HEAD * group)
    return pl.pallas_call(
        kernel,
        grid=(steps,),
        out_shape=jax.ShapeDtypeStruct((3, 2 * ROW, D), BF),
        in_specs=[
            smem,
            smem,
            smem,
            pl.BlockSpec(block, lambda h: (0, h)),
            pl.BlockSpec(block, lambda h: (0, h + steps)),
            pl.BlockSpec(block, lambda h: (0, h + 2 * steps)),
            pl.BlockSpec(block, lambda h: (0, h)),
        ],
        out_specs=pl.BlockSpec((3, *block), lambda h: (0, 0, h)),
        scratch_shapes=[pltpu.VMEM((2 * ROW, 2 * ROW), F32)],
        compiler_params=pltpu.CompilerParams(vmem_limit_bytes=16 << 20),
        cost_estimate=pl.CostEstimate(flops=1 << 20, bytes_accessed=1 << 10, transcendentals=0),
        name="attention_backward",
    )(phone, prompt, target, qkv, qkv, qkv, grad_mixed)


VMEM = pl.BlockSpec(memory_space=pltpu.VMEM)
SMEM = pl.BlockSpec(memory_space=pltpu.SMEM)
ANY = pl.BlockSpec(memory_space=pl.ANY)


def shape_of(shape, dtype=BF):
    return jax.ShapeDtypeStruct(shape, dtype)


def call(name, kernel, outs, args, specs=None, scratch=(), megabytes=12, long=False):
    return pl.pallas_call(
        kernel,
        out_shape=outs,
        in_specs=[VMEM] * len(args) if specs is None else specs,
        out_specs=[VMEM] * len(outs),
        scratch_shapes=list(scratch),
        compiler_params=pltpu.CompilerParams(vmem_limit_bytes=megabytes << 20),
        cost_estimate=pl.CostEstimate(
            flops=1 << (35 if long else 20), bytes_accessed=1 << 10, transcendentals=0
        ),
        name=name,
    )(*args)


def block(ref, slot, size):
    return ref[:, pl.ds(pl.multiple_of(slot * size, size), size)]


def pack(w_qkv, w_out, vectors):
    rows = w_qkv.shape[0]
    sizes = [v.shape[0] for v in vectors]
    wide = max(sizes)
    table = jnp.stack([jnp.pad(v, (0, wide - v.shape[0])) for v in vectors], 0)

    def kernel(table_ref, qkv_ref, out_ref, to, sems):
        copies = [
            pltpu.make_async_copy(qkv_ref, to.at[:, pl.ds(0, 3 * D)], sems.at[0]),
            pltpu.make_async_copy(out_ref, to.at[:, pl.ds(3 * D, D)], sems.at[1]),
        ]
        for copy in copies:
            copy.start()
        row = lax.broadcasted_iota(jnp.int32, (rows, wide), 0)
        column = lax.broadcasted_iota(jnp.int32, (rows, wide), 1)
        lane = lax.broadcasted_iota(jnp.int32, (rows, 128), 1)
        total, place = jnp.zeros((rows, 128), F32), 0
        for n, size in enumerate(sizes):
            value = table_ref[n : n + 1, :].astype(F32)
            for start in range(0, size, rows):
                picked = jnp.sum(jnp.where(column == row + start, value, 0.0), 1, keepdims=True)
                total = total + jnp.where(lane == place, picked, 0.0)
                place += 1
        to[:, 4 * D :] = total.astype(BF)
        for copy in copies:
            copy.wait()

    return call(
        "pack",
        kernel,
        [shape_of((rows, 4 * D + 128))],
        (table, w_qkv, w_out),
        [VMEM, ANY, ANY],
        [pltpu.SemaphoreType.DMA((2,))],
    )[0]


def unpack(own, other, rel_z, count):
    chips, rows = 4 * depth(), own[0][0].shape[1]
    flat = [(core, p) for core, part in enumerate((own, other)) for p in part]
    arrays = [p[0] for _, p in flat]
    cuts = [(0, 3 * D), (3 * D, D), (4 * D, 128)]

    def kernel(*refs):
        ins = refs[: len(arrays)]
        qkv_ref, out_ref, vec_ref, small_ref, sems = refs[len(arrays) :]
        where = position()
        copies = []
        for n in (2, 0, 1):
            to = (qkv_ref, out_ref, small_ref)[n]
            start, width = cuts[n]
            for ref, (core, (_, names)) in zip(ins, flat):
                at = where[3] ^ core
                for i, name in enumerate(names):
                    copy = pltpu.make_async_copy(
                        ref.at[i, :, pl.ds(start, width)],
                        to.at[chip_slot(name, where, rel_z), at],
                        sems.at[len(copies)],
                    )
                    copy.start()
                    copies.append(copy)
        for copy in copies[: len(copies) // 3]:
            copy.wait()
        small = small_ref[...].reshape(2 * chips * rows, 128).astype(F32)
        vec_ref[...] = jnp.transpose(small)[:count]
        for copy in copies[len(copies) // 3 :]:
            copy.wait()

    shapes = [(chips, 2, rows, w) for _, w in cuts]
    qkv, out, vec = call(
        "unpack",
        kernel,
        [shape_of(shapes[0]), shape_of(shapes[1]), shape_of((count, D), F32)],
        arrays,
        [ANY] * len(arrays),
        [pltpu.VMEM(shapes[2], BF), pltpu.SemaphoreType.DMA((6 * chips,))],
    )
    return qkv.reshape(D, 3 * D), out.reshape(D, D), vec


def normal_of(values):
    center = values - jnp.mean(values, -1, keepdims=True)
    inv = lax.rsqrt(jnp.mean(center * center, -1, keepdims=True) + 1e-05)
    return center * inv, inv


def norm_back(grad, normal, inv, gain):
    e = grad * gain
    return inv * (
        e - jnp.mean(e, -1, keepdims=True) - normal * jnp.mean(e * normal, -1, keepdims=True)
    )


def project(resident, vec, weight):
    def kernel(x_ref, vec_ref, w_ref, normed_ref, qkv_ref):
        for r in range(0, 2 * ROW, ROW):
            normal, _ = normal_of(x_ref[r : r + ROW, :].astype(F32))
            normed_ref[r : r + ROW, :] = (normal * vec_ref[0:1, :] + vec_ref[1:2, :]).astype(BF)
        for n in range(0, 3 * D, 512):
            qkv_ref[:, n : n + 512] = bdot(normed_ref[...], w_ref[:, n : n + 512], NN).astype(BF)

    outs = [shape_of((2 * ROW, D)), shape_of((2 * ROW, 3 * D))]
    return call("project", kernel, outs, (resident, vec, weight))


def attend(mixed, weight, resident, vec):
    def kernel(m_ref, w_ref, x_ref, vec_ref, normed_ref, hidden_ref):
        for r in range(0, 2 * ROW, ROW):
            rows = slice(r, r + ROW)
            hidden = x_ref[rows, :].astype(F32) + bdot(m_ref[rows, :], w_ref[...], NN)
            hidden_ref[rows, :] = hidden
            normal, _ = normal_of(hidden)
            normed_ref[rows, :] = (normal * vec_ref[2:3, :] + vec_ref[3:4, :]).astype(BF)

    outs = [shape_of((2 * ROW, D)), shape_of((2 * ROW, D), F32)]
    return call("attend", kernel, outs, (mixed, weight, resident, vec))


def gelu_both(v):
    c = (2.0 / jnp.pi) ** 0.5
    square = v * v
    t = jnp.tanh(v * (c + (c * 0.044715) * square))
    half = 0.5 + 0.5 * t
    return v * half, half + 0.5 * v * (1.0 - t * t) * (c + (3 * c * 0.044715) * square)


def feed_step(n_ref, w_ref, shift_ref, act_ref, slope_ref, start, size):
    cols = slice(start, start + size)
    pre = bdot(n_ref[...], w_ref[:, cols], NN) + shift_ref[:, cols]
    act, slope = gelu_both(pre)
    act_ref[:, cols] = act.astype(BF)
    slope_ref[:, cols] = slope.astype(BF)


def feed_first(normed, pieces, shift):
    chips, (rows, wide) = 4 * depth(), pieces[0][0].shape[1:]
    arrays = [p[0] for p in pieces]
    size = 512

    def kernel(n_ref, shift_ref, *refs):
        ins = refs[: len(arrays)]
        act_ref, slope_ref, w_ref, sems = refs[len(arrays) :]
        where = position()
        copies = []
        for start in range(0, wide, size):
            for ref, (_, names) in zip(ins, pieces):
                for i, name in enumerate(names):
                    to = pl.multiple_of(chip_slot(name, where, False) * rows, rows)
                    copy = pltpu.make_async_copy(
                        ref.at[i, :, pl.ds(start, size)],
                        w_ref.at[pl.ds(to, rows), pl.ds(start, size)],
                        sems.at[len(copies)],
                    )
                    copy.start()
                    copies.append(copy)
        for n, start in enumerate(range(0, wide, size)):
            for copy in copies[n * chips : (n + 1) * chips]:
                copy.wait()
            feed_step(n_ref, w_ref, shift_ref, act_ref, slope_ref, start, size)

    part = shape_of((2 * ROW, wide))
    return call(
        "feed_first",
        kernel,
        [part, part, shape_of((chips * rows, wide))],
        (normed, shift, *arrays),
        [VMEM, VMEM] + [ANY] * len(arrays),
        [pltpu.SemaphoreType.DMA((chips * (wide // size),))],
        long=True,
    )


def feed_second(normed, weight, shift):
    def kernel(n_ref, w_ref, shift_ref, act_ref, slope_ref):
        for start in range(0, weight.shape[1], 512):
            feed_step(n_ref, w_ref, shift_ref, act_ref, slope_ref, start, 512)

    part = shape_of((2 * ROW, weight.shape[1]))
    return call("feed_second", kernel, [part, part], (normed, weight, shift))


def down_grad(acts, cts):
    lists = layout_yzx()
    chips = 4 * depth()
    size = acts[0].shape[1] // chips
    half = size // 2
    group = 4

    def kernel(a0, a1, c0, c1, *outs):
        where = position()
        for jy in range(2):
            for jx in range(2):
                for z in range(0, depth(), group):
                    names = [(jy, z + i, jx) for i in range(group)]
                    slots = [chip_slot(name, where, False) for name in names]
                    total = 0.0
                    for a, ct in ((a0, c0), (a1, c1)):
                        left = jnp.concatenate([block(a, slot, size) for slot in slots], 1)
                        total = total + bdot(left, ct[...], TN)
                    total = total.astype(BF).reshape(group, size, D)
                    for i, name in enumerate(names):
                        upper, lower = outs[1 - jy], outs[3 - jx]
                        upper[lists[1 - jy].index(name)] = total[i, :half]
                        lower[lists[3 - jx].index(name)] = total[i, half:]

    outs = [shape_of((len(v), half, D)) for v in lists]
    return call("down_grad", kernel, outs, (*acts, *cts))


def back_act(cts, pieces, slopes):
    wide = slopes[0].shape[1]
    chips = 4 * depth()
    size = wide // chips
    arrays = [p[0] for p in pieces]
    half = size // 2
    wave = chips // 2

    def kernel(c0, c1, s0, s1, *refs):
        ins, (g0, g1, sum_ref, w_ref, sems) = refs[: len(arrays)], refs[len(arrays) :]
        where = position()

        def copy_of(n, i):
            name = pieces[n][1][i]
            row = pl.multiple_of(chip_slot(name, where, False) * size + (n // 2) * half, half)
            return pltpu.make_async_copy(
                ins[n].at[i], w_ref.at[pl.ds(row, half), :], sems.at[n * wave + i]
            )

        waves = [[], []]
        for n in range(4):
            for i, (jy, _, _) in enumerate(pieces[n][1]):
                copy = copy_of(n, i)
                copy.start()
                waves[jy].append(copy)
        for jy in range(2):
            for copy in waves[jy]:
                copy.wait()
            for j in range(0, wave * size, 256):
                start = pl.multiple_of((where[0] ^ jy) * (wave * size) + j, 256)
                at = pl.ds(start, 256)
                sums = 0.0
                for ct, slope, out in ((c0, s0, g0), (c1, s1, g1)):
                    grad = bdot(ct[...], w_ref[at, :], NT) * slope[:, at].astype(F32)
                    grad = grad.astype(BF)
                    sums = sums + jnp.sum(grad.astype(F32), 0, keepdims=True)
                    out[:, at] = grad
                sum_ref[:, at] = sums

    part = shape_of((2 * ROW, wide))
    return call(
        "back_act",
        kernel,
        [part, part, shape_of((1, wide), F32), shape_of((wide, D))],
        (*cts, *slopes, *arrays),
        [VMEM] * 4 + [ANY] * 4,
        [pltpu.SemaphoreType.DMA((4 * wave,))],
    )


def back_up(grad, weight, dtype):
    def kernel(g_ref, w_ref, out_ref):
        for n in range(0, D, 256):
            out_ref[:, n : n + 256] = bdot(g_ref[...], w_ref[n : n + 256, :], NT).astype(dtype)

    outs = [shape_of((2 * ROW, D), dtype)]
    return call("back_up", kernel, outs, (grad, weight), long=dtype == F32)[0]


def up_grad(normeds, grads, out_own, out_in):
    lists = layout_yxz()
    half, wide = depth() // 2, grads[0].shape[1]
    rows = D // (4 * depth())
    extra = rows // 4

    def kernel(n0, n1, g0, g1, a_ref, b_ref, *outs_and_scratch):
        outs, part_ref = outs_and_scratch[:4], outs_and_scratch[4]
        where = position()
        for out, names in zip(outs, lists):
            for i, name in enumerate(names):
                slot = chip_slot(name, where, False)
                total = (a_ref[slot].astype(F32) + b_ref[slot].astype(F32)).astype(BF)
                out[i, rows:, :D] = total[:extra]
                out[i, rows:, D:] = total[extra:]
        for side in range(2):
            for jy in range(2):
                base = (where[0] ^ jy) * depth() + side * half
                for n in range(0, wide, 512):
                    total = 0.0
                    for normed, grad in ((n0, g0), (n1, g1)):
                        left = jnp.concatenate(
                            [block(normed, base + i, 2 * rows) for i in range(half)], 1
                        )
                        total = total + bdot(left, grad[:, n : n + 512], TN)
                    part_ref[:, :, :, n : n + 512] = total.astype(BF).reshape(half, 2, rows, 512)
                for jx in range(2):
                    for i in range(half):
                        if side == 0:
                            out, at = outs[1 - jy], jx * half + i
                        else:
                            out, at = outs[3 - jx], jy * half + i
                        out[at, :rows] = part_ref[i, where[2] ^ jx]

    outs = [shape_of((len(v), rows + extra, wide)) for v in lists]
    scratch = [pltpu.VMEM((half, 2, rows, wide), BF)]
    return call("up_grad", kernel, outs, (*normeds, *grads, out_own, out_in), None, scratch)


def out_grad(mixed, low):
    chips = 4 * depth()
    rows = D // (2 * chips)
    group = 256 // (2 * rows)

    def kernel(m_ref, l_ref, send_ref, keep_ref):
        core = position()[3]
        for g in range(D // 256):
            at, cols = slice(g * group, (g + 1) * group), slice(g * 256, (g + 1) * 256)
            total = bdot(m_ref[:, cols], l_ref[...], TN).astype(BF).reshape(group, 2, rows, D)
            first, second = total[:, 0], total[:, 1]
            send_ref[at] = jnp.where(core == 0, second, first)
            keep_ref[at] = jnp.where(core == 0, first, second)

    outs = [shape_of((chips, rows, D))] * 2
    return call("out_grad", kernel, outs, (mixed, low))


def back_norm(own, other, hidden, vec, ct, weight):
    def kernel(a_ref, b_ref, h_ref, vec_ref, ct_ref, w_ref, mixed_ref, low_ref, grad_ref, sum_ref):
        first, second = 0.0, 0.0
        for r in range(0, 2 * ROW, ROW):
            rows = slice(r, r + ROW)
            normal, inv = normal_of(h_ref[rows, :])
            grad = a_ref[rows, :] + b_ref[rows, :].astype(F32)
            first = first + jnp.sum(grad * normal, 0, keepdims=True)
            second = second + jnp.sum(grad, 0, keepdims=True)
            total = ct_ref[rows, :].astype(F32) + norm_back(grad, normal, inv, vec_ref[2:3, :])
            grad_ref[rows, :] = total
            low_ref[rows, :] = total.astype(BF)
            mixed_ref[rows, :] = bdot(low_ref[rows, :], w_ref[...], NT).astype(BF)
        sum_ref[0:1, :] = first
        sum_ref[1:2, :] = second

    part = shape_of((2 * ROW, D))
    outs = [part, part, shape_of((2 * ROW, D), F32), shape_of((2, D), F32)]
    return call("back_norm", kernel, outs, (own, other, hidden, vec, ct, weight))


def attn_grad(normed, grads):
    chips = 4 * depth()
    rows = D // (2 * chips)
    group = 256 // (2 * rows)

    def kernel(n_ref, g_ref, send_ref, keep_ref):
        core = position()[3]
        for g in range(D // 256):
            at, cols = slice(g * group, (g + 1) * group), slice(g * 256, (g + 1) * 256)
            for part in range(3):
                total = bdot(n_ref[:, cols], g_ref[part], TN).astype(BF)
                total = total.reshape(group, 2, rows, D)
                first, second = total[:, 0], total[:, 1]
                to = slice(part * D, (part + 1) * D)
                send_ref[at, :, to] = jnp.where(core == 0, second, first)
                keep_ref[at, :, to] = jnp.where(core == 0, first, second)

    outs = [shape_of((chips, rows, 3 * D))] * 2
    return call("attn_grad", kernel, outs, (normed, grads))


def core_sum(own, arrived, sums, sums_in, rel_z):
    lists = layout_yxz()
    chips, rows, wide = own.shape
    lines = sums.shape[0]

    def kernel(a_ref, b_ref, s_ref, t_ref, *rest):
        outs, pad_ref, small_ref = rest[:4], rest[4], rest[5]
        where = position()
        pad_ref[...] = jnp.zeros_like(pad_ref)
        pad_ref[:lines, :] = s_ref[...] + t_ref[...]
        small_ref[...] = jnp.transpose(pad_ref[...]).astype(BF).reshape(chips, 2, rows, 128)
        for out, names in zip(outs, lists):
            for i, name in enumerate(names):
                slot = chip_slot(name, where, rel_z)
                total = a_ref[slot].astype(F32) + b_ref[slot].astype(F32)
                out[i, :, :wide] = total.astype(BF)
                out[i, :, wide:] = small_ref[slot, where[3]]

    outs = [shape_of((len(v), rows, wide + 128)) for v in lists]
    scratch = [pltpu.VMEM((128, D), F32), pltpu.VMEM((chips, 2, rows, 128), BF)]
    return call("core_sum", kernel, outs, (own, arrived, sums, sums_in), None, scratch)


def back_first(grads, weight, resident, vec, hidden_grad):
    def kernel(g_ref, w_ref, x_ref, vec_ref, h_ref, out_ref, sum_ref):
        first, second = 0.0, 0.0
        for half in range(2):
            rows = slice(half * ROW, (half + 1) * ROW)
            normal, inv = normal_of(x_ref[rows, :].astype(F32))
            grad = 0.0
            for part in range(3):
                grad = grad + bdot(g_ref[part, rows, :], w_ref[:, part * D : (part + 1) * D], NT)
            first = first + jnp.sum(grad * normal, 0, keepdims=True)
            second = second + jnp.sum(grad, 0, keepdims=True)
            total = h_ref[rows, :] + norm_back(grad, normal, inv, vec_ref[0:1, :])
            out_ref[half] = total.astype(BF)
        sum_ref[0:1, :] = first
        sum_ref[1:2, :] = second

    outs = [shape_of((2, ROW, D)), shape_of((2, D), F32)]
    args = (grads, weight, resident, vec, hidden_grad)
    return call("back_first", kernel, outs, args, long=True)


def down_back(act, weight, dtype, hidden=None, late=None):
    extra = tuple(v for v in (hidden, late) if v is not None)

    def kernel(a_ref, w_ref, *refs):
        out_ref = refs[-1]
        for n in range(0, D, 256):
            total = bdot(a_ref[...], w_ref[:, n : n + 256], NN)
            if hidden is not None:
                total = total + refs[0][:, n : n + 256]
            out_ref[:, n : n + 256] = total.astype(dtype)

    return call("down_back", kernel, [shape_of((2 * ROW, D), dtype)], (act, weight, *extra))[0]


def interleave(own, other):
    rows, wide = own.shape
    size = wide // (4 * depth())

    def kernel(a_ref, b_ref, out_ref):
        core = position()[3]
        for n in range(wide // size):
            cols = slice(n * size, (n + 1) * size)
            for ref, at in ((a_ref, core), (b_ref, 1 - core)):
                to = pl.multiple_of((2 * n + at) * size, size)
                out_ref[:, pl.ds(to, size)] = ref[:, cols]

    return call("interleave", kernel, [shape_of((rows, 2 * wide), F32)], (own, other))[0]


def shards(
    inputs,
    cotangent,
    phone_len,
    prompt_len,
    target_len,
    ln1_gain,
    ln1_bias,
    w_qkv,
    w_out,
    ln2_gain,
    ln2_bias,
    w_up,
    up_bias,
    w_down,
):
    y, z, x, c = position()
    count = depth()
    chips = 4 * count
    row_w = w_qkv.shape[0]
    row_f = w_down.shape[0]

    chain = Chain()

    def split_halves(blocks):
        return (
            lax.dynamic_index_in_dim(blocks, 1 - y, 0, keepdims=False),
            lax.dynamic_index_in_dim(blocks, y, 0, keepdims=False),
        )

    attn_g, up_g, down_g = Gather(chain, True), Gather(chain, False), GatherXZY(chain)
    down_s, up_s, attn_s = ScatterYZX(chain), Scatter(chain, False), Scatter(chain, True)

    vectors = (ln1_gain, ln1_bias, ln2_gain, ln2_bias, up_bias)
    attn_z = attn_g.over_z(chain(pack, w_qkv, w_out, vectors))
    def split_both(inputs, cotangent):
        x_send, x_own = split_halves(inputs)
        ct_send, ct_own = split_halves(cotangent)
        return jnp.stack([x_send, ct_send], 0), x_own, ct_own

    both_send, x_own, ct_own = chain(split_both, inputs[:, 0, 0], cotangent[:, 0, 0])
    both_other = swap(both_send, "y")
    lengths = tuple(
        lax.dynamic_index_in_dim(v, y, 0, keepdims=False)[0]
        for v in (phone_len, prompt_len, target_len)
    )

    def split_up(w_up):
        split = w_up.reshape(row_w, chips, 2, FF // chips // 2)
        return tuple(
            lax.dynamic_index_in_dim(split, i, 2, keepdims=False).reshape(row_w, FF // 2)
            for i in (1 - c, c)
        )

    up_send, up_own = chain(split_up, w_up)
    up_other = swap(up_send, 1)
    up_shard = chain(lambda own, other: ordered(c, own, other, 0), up_own, up_other)
    half_f = row_f // 2

    def join_both(x_own, ct_own, other):
        return ordered(y, x_own, other[0], 0), ordered(y, ct_own, other[1], 0)

    resident, grad_result = chain(join_both, x_own, ct_own, both_other)
    attn_one = attn_g.one(extras=(w_down[:half_f], w_down[half_f:]))
    up_z = up_g.over_z(up_shard, *attn_z)


    attn_two = attn_g.two(extras=(half_f, D))
    early = [(swap(array, 1), rels) for array, rels in attn_g.pieces[::2]]
    down_z = down_g.over_z(attn_g.planes[2], *up_z)
    up_g.one_halves()
    late = [(swap(after(array, *up_g.halves), 1), rels) for array, rels in attn_g.pieces[1::2]]
    up_one = up_g.send(*[v[0] for v in early + late])
    lines = 4 + row_f // row_w
    attn_core = early + late
    many = len(attn_core)

    def unpack_pieces(*arrays):
        own = [(a, p[1]) for a, p in zip(arrays[:many], attn_g.pieces)]
        other = [(a, p[1]) for a, p in zip(arrays[many:], attn_core)]
        return unpack(own, other, attn_g.rel_z, lines)

    qkv_weight, out_weight, vec = chain(
        unpack_pieces, *[p[0] for p in attn_g.pieces + attn_core]
    )
    shift = vec[4:].reshape(row_f // row_w, chips, 2, row_w)
    shift = lax.dynamic_index_in_dim(shift, c, 2, keepdims=False)
    shift = shift.transpose(1, 0, 2).reshape(1, FF // 2)

    normed, qkv = chain(project, resident, vec, qkv_weight)
    up_two = up_g.two()
    mixed = chain(lambda v: attention_forward(v, *lengths), qkv)
    normed_two, hidden = chain(attend, mixed, out_weight, resident, vec)
    ct_sent = swap(grad_result, 1)
    normed_sent = swap(normed_two, 1)

    def with_pieces(step, pieces):
        def run(*args):
            arrays, rest = args[: len(pieces)], args[len(pieces) :]
            return step([(a, p[1]) for a, p in zip(arrays, pieces)], *rest)

        return run

    up_arrays = [p[0] for p in up_g.pieces]
    down_two = down_g.two(*up_two)
    act_own, slope_own, up_weight = chain(
        with_pieces(lambda p, n, s: feed_first(n, p, s), up_g.pieces), *up_arrays, normed_two, shift
    )
    act_other, slope_other = chain(feed_second, normed_sent, up_weight, shift)
    down_sone = down_s.one(
        chain(
            lambda a, b, p, q: down_grad((a, b), (p, q)), act_own, act_other, grad_result, ct_sent
        ),
    )

    pre_own, pre_other, grad_shift, down_weight = chain(
        with_pieces(lambda p, a, b, s, t: back_act((a, b), p, (s, t)), down_g.pieces),
        *[p[0] for p in down_g.pieces],
        grad_result,
        ct_sent,
        slope_own,
        slope_other,
    )
    two_other = swap(chain(lambda g, w: back_up(g, w, BF), pre_other, up_weight), 1)
    two_own = chain(lambda g, w: back_up(g, w, F32), pre_own, up_weight)
    grad_mixed, grad_low, grad_hidden, sums_two = chain(
        back_norm, two_own, two_other, hidden, vec, grad_result, out_weight
    )
    out_send, out_keep = chain(out_grad, mixed, grad_low)
    out_in = swap(out_send, 1)
    down_sz = down_s.over_z()
    up_sone = up_s.one(
        chain(
            lambda a, b, p, q, o, i: up_grad((a, b), (p, q), o, i),
            normed_two,
            normed_sent,
            pre_own,
            pre_other,
            out_keep,
            out_in,
        )
    )
    grads = chain(lambda a, b: attention_backward(a, b, *lengths), qkv, grad_mixed)
    up_stwo = up_s.two()
    attn_send, attn_keep = chain(attn_grad, normed, grads)
    attn_in = swap(attn_send, 1)
    grad_rows, sums_one = chain(back_first, grads, qkv_weight, resident, vec, grad_hidden)

    def small_lines(one, two, shift):
        last = shift.reshape(chips, row_f // row_w, row_w).transpose(1, 0, 2)[:, :, None]
        last = ordered(c, last, jnp.zeros_like(last), 2).reshape(-1, D)
        return jnp.concatenate([one, two, last], 0)

    sums = chain(small_lines, sums_one, sums_two, grad_shift)
    sums_in = swap(sums, 1)
    down_x, down_y, down_one_own, down_two_own = down_s.last()
    attn_parts = chain(
        lambda a, b, p, q: core_sum(a, b, p, q, attn_s.rel_z), attn_keep, attn_in, sums, sums_in
    )
    attn_sone = attn_s.one(attn_parts)
    later = swap(attn_parts[0][0, :16, :128], 1)
    down_sent = swap(
        chain(lambda a, w, v: down_back(a, w, BF, None, v), act_other, down_weight, later), 1
    )
    down_own = chain(lambda a, w, h: down_back(a, w, F32, h), act_own, down_weight, hidden)

    up_sz = up_s.over_z()

    def result_of(own, other):
        total = (own + other.astype(F32)).astype(BF).reshape(2, ROW, D)
        return split_halves(total)

    res_send, res_own = chain(result_of, down_own, down_sent)
    gx_send, gx_own = chain(split_halves, grad_rows)
    attn_stwo = attn_s.two(extras=(down_x, down_y))
    sum_up = chain(up_s.total, up_sz)
    sum_up = sum_up.reshape(-1, FF // 2)
    out_rows = sum_up[2 * row_w :]
    sum_out = jnp.concatenate([out_rows[:, :D], out_rows[:, D:]], 0)
    up_rows = sum_up[: 2 * row_w].reshape(2, row_w, FF // 2)
    up_mine = lax.dynamic_index_in_dim(up_rows, c, 0, keepdims=False)
    up_theirs = swap(lax.dynamic_index_in_dim(up_rows, 1 - c, 0, keepdims=False), 1)
    gx_other = swap(after(gx_send, *attn_stwo), "y")
    out_other = swap(after(res_send, *attn_stwo), "y")
    attn_sz = attn_s.over_z()

    def sum_of_down(upper, from_x, lower, from_y):
        from_x, from_y = (v[:, 3 * D + 128 :].reshape(half_f, D) for v in (from_x, from_y))
        return jnp.concatenate([plus(upper.astype(F32), from_x), plus(lower.astype(F32), from_y)], 0)

    sum_down = chain(sum_of_down, down_one_own, attn_stwo[0], down_two_own, attn_stwo[1])

    def home(own, other):
        return ordered(y, own[None], other[None], 0).reshape(MICRO, 1, 1, ROW, D)

    up_final = chain(interleave, up_mine, up_theirs)
    out_stack = chain(home, res_own, out_other)
    grad_stack = chain(lambda own, other: home(own, other).astype(F32), gx_own, gx_other)
    sum_attn = attn_s.total(attn_sz)
    small_sum = sum_attn[:, 3 * D : 3 * D + lines].T.reshape(-1)
    edges = [i * row_w for i in range(5)]
    small_out = [small_sum[a:b] for a, b in zip(edges[:4], edges[1:])]
    return (
        out_stack,
        grad_stack,
        small_out[0],
        small_out[1],
        sum_attn[:, : 3 * D],
        sum_out,
        small_out[2],
        small_out[3],
        up_final.reshape(row_w, FF),
        small_sum[4 * row_w : 4 * row_w + row_f],
        sum_down,
    )


def plain_passed_along(block, axis, distance):
    devices = range(lax.axis_size(axis))
    route = [(i - distance, i) for i in devices if i - distance in devices]
    return lax.ppermute(block, axis, route)


def plain_times_transposed(left, right):
    return lax.dot_general(
        left, right, (((1,), (1,)), ((), ())), preferred_element_type=jnp.float32
    )


def plain_transposed_times(left, right):
    return lax.dot_general(
        left, right, (((0,), (0,)), ((), ())), preferred_element_type=jnp.float32
    )


def plain_layer_norm(values, gain, bias):
    center = values - jnp.mean(values, -1, keepdims=True)
    spread = jnp.mean(center * center, -1, keepdims=True)
    return center * lax.rsqrt(spread + 1e-05) * gain + bias


def plain_locate(lengths, slot_ids):
    count = jnp.arange(lengths.shape[0])
    seg_ends = jnp.sum(jnp.where(count[None, :] <= count[:, None], lengths[None, :], 0), 1, dtype=jnp.int32)
    seg_ids = jnp.sum(
        (slot_ids[:, None] >= seg_ends[None, :]).astype(jnp.int32), 1, dtype=jnp.int32
    )
    one_hot = (seg_ids[:, None] == jnp.arange(lengths.shape[0], dtype=jnp.int32)[None, :]).astype(
        jnp.int32
    )
    seg_start = jnp.sum(one_hot * (seg_ends - lengths)[None, :], 1, dtype=jnp.int32)
    return (seg_ids, one_hot, slot_ids - seg_start)


def plain_frame_meta(phone_lens, prompt_lens, target_lens, slot_count):
    slot_ids = jnp.arange(slot_count, dtype=jnp.int32)
    pre_seg, pre_hot, pre_off = plain_locate(phone_lens + prompt_lens, slot_ids)
    pre_phone = jnp.sum(pre_hot * phone_lens[None, :], 1, dtype=jnp.int32)
    prefix = (pre_seg, pre_off < pre_phone, pre_off - pre_phone)
    tgt_seg, tgt_hot, tgt_off = plain_locate(target_lens, slot_ids)
    tgt_pos = jnp.sum(tgt_hot * prompt_lens[None, :], 1, dtype=jnp.int32) + tgt_off
    targets = (tgt_seg, tgt_off < 0, tgt_pos)
    return (prefix, targets)


def plain_allowed(query_meta, key_meta):
    same_seg = query_meta[0][:, None] == key_meta[0][None, :]
    audio_ok = key_meta[1][None, :] | (key_meta[2][None, :] <= query_meta[2][:, None])
    return same_seg & jnp.where(query_meta[1][:, None], key_meta[1][None, :], audio_ok)


def plain_masked_scores(queries, key_rows, allowed_mask, score_scale):
    scores = (
        jnp.einsum("qhd,khd->hqk", queries, key_rows, preferred_element_type=jnp.float32)
        * score_scale
    )
    return jnp.where(allowed_mask[None], scores, -1e30)


def plain_attention_forward(queries, key_rows, value_rows, allowed_mask, score_scale):
    scores = plain_masked_scores(queries, key_rows, allowed_mask, score_scale)
    peak = jnp.max(scores, -1, keepdims=True)
    exp_scores = jnp.exp(scores - peak)
    row_total = jnp.sum(exp_scores, -1, keepdims=True)
    probs = (exp_scores / row_total).astype(jnp.bfloat16)
    mixed = jnp.einsum("hqk,khd->qhd", probs, value_rows, preferred_element_type=jnp.float32)
    return (mixed.astype(jnp.bfloat16), peak + jnp.log(row_total))


def plain_attention_backward(
    queries, key_rows, value_rows, allowed_mask, log_total, grad_mixed, score_scale
):
    scores = plain_masked_scores(queries, key_rows, allowed_mask, score_scale)
    probs = jnp.where(allowed_mask[None], jnp.exp(scores - log_total), 0.0)
    grad_probs = jnp.einsum(
        "qhd,khd->hqk", grad_mixed, value_rows, preferred_element_type=jnp.float32
    )
    grad_values = jnp.einsum(
        "hqk,qhd->khd", probs.astype(jnp.bfloat16), grad_mixed, preferred_element_type=jnp.float32
    )
    inner = jnp.sum(grad_probs * probs, -1, keepdims=True)
    grad_scores = (probs * (grad_probs - inner)).astype(jnp.bfloat16)
    grad_queries = (
        jnp.einsum("hqk,khd->qhd", grad_scores, key_rows, preferred_element_type=jnp.float32)
        * score_scale
    )
    grad_keys = (
        jnp.einsum("hqk,qhd->khd", grad_scores, queries, preferred_element_type=jnp.float32)
        * score_scale
    )
    return (grad_queries, grad_keys, grad_values)


def plain_add_up(summed, fresh):
    if summed is None:
        return fresh
    return jax.tree.map(lambda summed_part, fresh_part: summed_part + fresh_part, summed, fresh)


def plain_fetch_forward(params):
    return (
        lax.all_gather(params[0], ("pair", "rows"), axis=0, tiled=True),
        lax.all_gather(params[1], ("pair", "rows"), axis=0, tiled=True),
        lax.all_gather(params[2], ("pair", "rows"), axis=0, tiled=True),
        lax.all_gather(params[3], ("pair", "rows"), axis=0, tiled=True),
        lax.all_gather(params[4], ("pair", "rows"), axis=0, tiled=True),
        lax.all_gather(params[5], ("pair", "rows"), axis=0, tiled=True),
        lax.all_gather(params[6], ("pair", "rows"), axis=0, tiled=True),
        lax.all_gather(params[7], ("pair", "rows"), axis=0, tiled=True),
        lax.all_gather(params[8], ("pair", "rows"), axis=0, tiled=True),
    )


def plain_shards(
    inputs,
    cotangent,
    phone_len,
    prompt_len,
    target_len,
    ln1_gain,
    ln1_bias,
    w_qkv,
    w_out,
    ln2_gain,
    ln2_bias,
    w_up,
    up_bias,
    w_down,
):
    half_index = lax.axis_index("pair")
    score_scale = HEAD ** (-0.5)
    params = (ln1_gain, ln1_bias, w_qkv, w_out, ln2_gain, ln2_bias, w_up, up_bias, w_down)
    out_blocks = []
    grad_blocks = []
    summed = None
    for batch_index in range(MICRO):
        gathered = plain_fetch_forward(params)
        (
            gain_one,
            bias_one,
            qkv_weight,
            out_weight,
            gain_two,
            bias_two,
            up_weight,
            up_shift,
            down_weight,
        ) = gathered
        gain_one_f = gain_one.astype(jnp.float32)
        bias_one_f = bias_one.astype(jnp.float32)
        gain_two_f = gain_two.astype(jnp.float32)
        bias_two_f = bias_two.astype(jnp.float32)
        prefix, targets = plain_frame_meta(
            phone_len[batch_index, 0], prompt_len[batch_index, 0], target_len[batch_index, 0], ROW
        )
        query_meta = tuple(
            (
                jnp.where(half_index == 0, pre_field, tgt_field)
                for pre_field, tgt_field in zip(prefix, targets)
            )
        )
        remote_mask = plain_allowed(query_meta, prefix) & (half_index == 1)
        allowed_mask = jnp.concatenate([remote_mask, plain_allowed(query_meta, query_meta)], 1)
        resident = inputs[batch_index, 0, 0].astype(jnp.float32)
        normed = plain_layer_norm(resident, gain_one_f, bias_one_f).astype(jnp.bfloat16)
        qkv_rows = jnp.dot(normed, qkv_weight, preferred_element_type=jnp.float32).astype(
            jnp.bfloat16
        )
        own_kv = qkv_rows[:, D:]
        remote_kv = plain_passed_along(own_kv, "pair", 1)
        queries = qkv_rows[:, :D].reshape(ROW, HEADS, HEAD)
        key_rows = jnp.concatenate([remote_kv[:, :D], own_kv[:, :D]], 0).reshape(
            2 * ROW, HEADS, HEAD
        )
        value_rows = jnp.concatenate([remote_kv[:, D:], own_kv[:, D:]], 0).reshape(
            2 * ROW, HEADS, HEAD
        )
        mixed, log_total = plain_attention_forward(
            queries, key_rows, value_rows, allowed_mask, score_scale
        )
        mixed_flat = mixed.reshape(ROW, D)
        hidden_res = resident + jnp.dot(mixed_flat, out_weight, preferred_element_type=jnp.float32)
        normed_two = plain_layer_norm(hidden_res, gain_two_f, bias_two_f).astype(jnp.bfloat16)
        pre_act = jnp.dot(
            normed_two, up_weight, preferred_element_type=jnp.float32
        ) + up_shift.astype(jnp.float32)
        activ = jax.nn.gelu(pre_act, approximate=True).astype(jnp.bfloat16)
        result = hidden_res + jnp.dot(activ, down_weight, preferred_element_type=jnp.float32)
        out_blocks.append(result.astype(jnp.bfloat16))
        gathered = (
            lax.all_gather(params[0], ("pair", "rows"), axis=0, tiled=True),
            lax.all_gather(params[1], ("pair", "rows"), axis=0, tiled=True),
            lax.all_gather(params[2], ("pair", "rows"), axis=0, tiled=True),
            lax.all_gather(params[3], ("pair", "rows"), axis=0, tiled=True),
            lax.all_gather(params[4], ("pair", "rows"), axis=0, tiled=True),
            lax.all_gather(params[5], ("pair", "rows"), axis=0, tiled=True),
            lax.all_gather(params[6], ("pair", "rows"), axis=0, tiled=True),
            lax.all_gather(params[7], ("pair", "rows"), axis=0, tiled=True),
            lax.all_gather(params[8], ("pair", "rows"), axis=0, tiled=True),
        )
        (
            gain_one,
            bias_one,
            qkv_weight,
            out_weight,
            gain_two,
            bias_two,
            up_weight,
            up_shift,
            down_weight,
        ) = gathered
        gain_one_f = gain_one.astype(jnp.float32)
        bias_one_f = bias_one.astype(jnp.float32)
        gain_two_f = gain_two.astype(jnp.float32)
        bias_two_f = bias_two.astype(jnp.float32)
        grad_result = cotangent[batch_index, 0, 0]
        grad_down = plain_transposed_times(activ, grad_result)
        grad_activ = plain_times_transposed(grad_result, down_weight)
        _, gelu_back = jax.vjp(lambda pre_value: jax.nn.gelu(pre_value, approximate=True), pre_act)
        grad_pre = gelu_back(grad_activ)[0].astype(jnp.bfloat16)
        grad_up = plain_transposed_times(normed_two, grad_pre)
        grad_up_bias = jnp.sum(grad_pre.astype(jnp.float32), 0)
        grad_normed_two = plain_times_transposed(grad_pre, up_weight)
        _, norm_back_two = jax.vjp(plain_layer_norm, hidden_res, gain_two_f, bias_two_f)
        grad_hidden_ln, grad_gain_two, grad_bias_two = norm_back_two(grad_normed_two)
        grad_hidden = grad_result.astype(jnp.float32) + grad_hidden_ln
        grad_hidden_low = grad_hidden.astype(jnp.bfloat16)
        grad_out_w = plain_transposed_times(mixed_flat, grad_hidden_low)
        grad_mixed = (
            plain_times_transposed(grad_hidden_low, out_weight)
            .astype(jnp.bfloat16)
            .reshape(ROW, HEADS, HEAD)
        )
        grad_queries, grad_keys, grad_values = plain_attention_backward(
            queries, key_rows, value_rows, allowed_mask, log_total, grad_mixed, score_scale
        )
        remote_grads = jnp.concatenate(
            [grad_keys[:ROW].reshape(ROW, D), grad_values[:ROW].reshape(ROW, D)], 1
        )
        returned = plain_passed_along(remote_grads.astype(jnp.bfloat16), "pair", -1).astype(
            remote_grads.dtype
        )
        grad_qkv_rows = jnp.concatenate(
            [
                grad_queries.reshape(ROW, D),
                grad_keys[ROW:].reshape(ROW, D) + returned[:, :D],
                grad_values[ROW:].reshape(ROW, D) + returned[:, D:],
            ],
            1,
        ).astype(jnp.bfloat16)
        grad_qkv_w = plain_transposed_times(normed, grad_qkv_rows)
        grad_normed = plain_times_transposed(grad_qkv_rows, qkv_weight)
        _, norm_back_one = jax.vjp(plain_layer_norm, resident, gain_one_f, bias_one_f)
        grad_resident_ln, grad_gain_one, grad_bias_one = norm_back_one(grad_normed)
        grad_blocks.append(grad_hidden + grad_resident_ln)
        local_grads = (
            grad_gain_one,
            grad_bias_one,
            grad_qkv_w,
            grad_out_w,
            grad_gain_two,
            grad_bias_two,
            grad_up,
            grad_up_bias,
            grad_down,
        )
        shard_part = (
            lax.psum_scatter(local_grads[0], ("pair", "rows"), scatter_dimension=0, tiled=True),
            lax.psum_scatter(local_grads[1], ("pair", "rows"), scatter_dimension=0, tiled=True),
            lax.psum_scatter(local_grads[2], ("pair", "rows"), scatter_dimension=0, tiled=True),
            lax.psum_scatter(local_grads[3], ("pair", "rows"), scatter_dimension=0, tiled=True),
            lax.psum_scatter(local_grads[4], ("pair", "rows"), scatter_dimension=0, tiled=True),
            lax.psum_scatter(local_grads[5], ("pair", "rows"), scatter_dimension=0, tiled=True),
            lax.psum_scatter(local_grads[6], ("pair", "rows"), scatter_dimension=0, tiled=True),
            lax.psum_scatter(local_grads[7], ("pair", "rows"), scatter_dimension=0, tiled=True),
            lax.psum_scatter(local_grads[8], ("pair", "rows"), scatter_dimension=0, tiled=True),
        )
        summed = plain_add_up(summed, shard_part)
    block_shape = (MICRO, 1, 1, ROW, D)
    out_stack = jnp.stack(out_blocks, 0).reshape(block_shape)
    grad_stack = jnp.stack(grad_blocks, 0).reshape(block_shape)
    return (
        out_stack,
        grad_stack,
        summed[0],
        summed[1],
        summed[2],
        summed[3],
        summed[4],
        summed[5],
        summed[6],
        summed[7],
        summed[8],
    )


def solution(mesh):
    rows = P(None, "rows", "pair", None, None)
    line = P(("pair", "rows"))
    flat = P(("pair", "rows"), None)
    lens = P(None, "rows", None)
    return jax.shard_map(
        shards if mesh.shape["rows"] == 16 else plain_shards,
        mesh=mesh,
        in_specs=(rows, rows, lens, lens, lens, line, line, flat, flat, line, line, flat, line, flat),
        out_specs=(rows, rows, line, line, flat, flat, line, line, flat, line, flat),
        check_vma=False,
    )
```

time: 1040 us -> 356 us (0.34)
  waiting for transfers between devices: 637 us -> 97.5 us
  matrix products: 165 us -> 0 us
  blocking collectives: 120 us -> 0 us
  Pallas kernels: 0 us -> 119 us
  starting transfers between devices: 10.4 us -> 38.8 us
  local copies, waits for them, and re-layouts: 37.4 us -> 49.3 us
  other arithmetic: 40.8 us -> 30 us
    reduce_scatter x4 -> x2, waiting for transfers between devices: 471 us -> 0.01 us  [z_scatter(): lax.psum_scatter(column, 'rows', scatter_dimension=0, axis_index_groups=z...]
    dot_general x36 -> x0, matrix products: 165 us -> none  [the longest x8 53.3 us: transposed_times(): lax.dot_general(left, right, (((0,), (0,)), ((), ())), preferred_element_...]
    pallas_call x0 -> x21, Pallas kernels: none -> 119 us  [the longest x19 83.9 us: call(): pl.pallas_call(kernel, out_shape=outs, in_specs=[VMEM] * len(args) if spe...]
    all_gather x4 -> x2, waiting for transfers between devices: 90.1 us -> 7.25 us  [z_gather(): return lax.all_gather(block, 'rows', axis_index_groups=z_groups())]
    unnamed x2 -> x0, blocking collectives: 79.9 us -> none
    all_gather x1 -> x0, blocking collectives: 40.5 us -> none  [fetch_forward(): lax.all_gather(params[7], ('pair', 'rows'), axis=0, tiled=True)]
    ppermute x4 -> x43, starting transfers between devices: 9.72 us -> 38.4 us  [the longest x30 21 us: swap(): return lax.ppermute(block, 'rows', [(i, i ^ way) for i in range(count)])]
    ppermute x4 -> x43, waiting for transfers between devices: 72.5 us -> 90.2 us  [the longest x13 59.5 us: swap(): return lax.ppermute(block, 'pair', [(i, i ^ 1) for i in range(2)])]
  transfers between devices with their start and end apart: 12 -> 47, of which waited for: 9 -> 21; matrix products, arithmetic and copies ran while one was open for 19% -> 14% of each run, Pallas kernels for 0% -> 32%
where the time goes in v2:
time: 356 us; the launch traced here: 350 us
  Pallas kernels  119 us (33%)
  waiting for transfers between devices  97.5 us (27%)
  local copies, waits for them, and re-layouts  49.3 us (14%)
  starting transfers between devices  38.8 us (11%)
  other arithmetic  30 us (8%)
  between operations  15 us (4%)
    pallas_call x19, Pallas kernels, call(): pl.pallas_call(kernel, out_shape=outs, in_specs=[VMEM] * len(args) if spe...  83.9 us
    ppermute x13, waiting for transfers between devices, swap(): return lax.ppermute(block, 'pair', [(i, i ^ 1) for i in range(2)])  59.5 us
    ppermute x30, waiting for transfers between devices, swap(): return lax.ppermute(block, 'rows', [(i, i ^ way) for i in range(count)])  30.7 us
    unnamed x124, local copies, waits for them, and re-layouts  24.9 us
    ppermute x30, starting transfers between devices, swap(): return lax.ppermute(block, 'rows', [(i, i ^ way) for i in range(count)])  21 us
    pallas_call x1, Pallas kernels, attention_backward(): pl.pallas_call(kernel, grid=(steps,), out_shape=jax.ShapeDtypeStruct((3,...  19.5 us
    ppermute x13, starting transfers between devices, swap(): return lax.ppermute(block, 'pair', [(i, i ^ 1) for i in range(2)])  17.4 us
    pallas_call x1, Pallas kernels, attention_forward(): pl.pallas_call(kernel, grid=(steps,), out_shape=jax.ShapeDtypeStruct((2 *...  15.9 us
  transfers between devices with their start and end apart: 47, of which 21 were waited for; matrix products, arithmetic and copies ran while one was open for 14% of the time, Pallas kernels for 32%

profile of v2, /device:TPU:0, one launch (start us, length us, event | category | flops | bytes accessed | tf_op | source)
XLA Modules:
  0.0 350.0 jit_solution(1742118661926948177)
XLA Ops:
  13.8 3.0 collective-permute-start.4
  18.4 2.6 collective-permute-start.2
  25.9 14.3 %collective-permute-done.4 = bf16[2,256,1024]{2,1,0:T(8,128)(2,1)S(1)} collective-permute-done((bf16[2,256,1024]{2,1,0:T(8,128)(2,1)}, bf16[2,256,1024]{2,1,0:T(8,128)(2,1)S(1)}, u32[]{:S(2)}, u32[]{:S(2)}) %collective-permute-start.4) | collective-permute-done | bytes 1048608 | tf_op jit(solution)/shard_map/ppermute | solution.py:32
  47.8 13.0 %collective-permute-done.5 = bf16[64,5248]{1,0:T(8,128)(2,1)S(1)} collective-permute-done((bf16[64,5248]{1,0:T(8,128)(2,1)S(1)}, bf16[64,5248]{1,0:T(8,128)(2,1)S(1)}, u32[]{:S(2)}, u32[]{:S(2)}) %collective-permute-start.5) | collective-permute-done | bytes 671776 | tf_op jit(solution)/shard_map/ppermute | solution.py:34
  69.7 5.5 %all-gather.5.cloned.1.call-done = bf16[256,2048]{1,0:T(8,128)(2,1)} async-done(((bf16[64,2048]{1,0:T(8,128)(2,1)}), bf16[256,2048]{1,0:T(8,128)(2,1)}) %all-gather.5.cloned.1.call-update) | async-done | bytes 1048592 | tf_op jit(solution)/shard_map/all_gather | solution.py:59
  77.5 9.1 %collective-permute-done.11.refs_3_ = bf16[4,32,4224]{2,1,0:T(8,128)(2,1)S(1)} collective-permute-done((bf16[4,32,4224]{2,1,0:T(8,128)(2,1)S(1)}, bf16[4,32,4224]{2,1,0:T(8,128)(2,1)S(1)}, u32[]{:S(2)}, u32[]{:S(2)}) %collective-permute-start.11) | collective-permute-done | bytes 1081376 | tf_op jit(solution)/shard_map/ppermute | solution.py:34
  93.4 4.5 %unpack.1 = (bf16[16,2,32,3072]{3,2,1,0:T(8,128)(2,1)S(1)}, bf16[16,2,32,1024]{3,2,1,0:T(8,128)(2,1)S(1)}, f32[8,1024]{1,0:T(8,128)S(1)}) custom-call(bf16[4,32,4224]{2,1,0:T(8,128)(2,1)S(1)} %pad_maximum_fusion.2.refs_0_, bf16[4,32,4224]{2,1,0:T(8,128)(2,1)} %collective-permute-done.9.refs_1_, bf16[4,32,4224]{2,1,0:T(8,128)(2,1)S(1)} %pad_maximum_fusion.3.refs_2_, ...), custom_call_target="tpu_custom_call" | custom-call | flops 1048576 | bytes 1024 | tf_op jit(solution)/shard_map/unpack/pallas_call | solution.py:492
  97.9 3.9 %project.1 = (bf16[512,1024]{1,0:T(8,128)(2,1)S(1)}, bf16[512,3072]{1,0:T(8,128)(2,1)S(1)}) custom-call(bf16[512,1024]{1,0:T(8,128)(2,1)S(1)} %copy-done.4, f32[8,1024]{1,0:T(8,128)S(1)} %get-tuple-element.351.vec_ref, bf16[1024,3072]{1,0:T(8,128)(2,1)S(1)} %bitcast.112), custom_call_target="tpu_custom_call" | custom-call | flops 1048576 | bytes 1024 | tf_op jit(solution)/shard_map/project/pallas_call | solution.py:492
  101.8 2.6 copy-done.21
  112.4 15.9 %attention_forward.1.m_ref = bf16[512,1024]{1,0:T(8,128)(2,1)S(1)} custom-call(s32[2]{0:T(128)S(1)} %get-tuple-element.455.phone_ref, s32[2]{0:T(128)S(1)} %get-tuple-element.456.prompt_ref, s32[2]{0:T(128)S(1)} %fusion.5.target_ref, bf16[512,3072]{1,0:T(8,128)(2,1)S(1)} %get-tuple-element.336.q_ref.k_ref.v_ref, ...), custom_call_target="tpu_custom_call" | custom-call | flops 1048576 | bytes 1024 | tf_op jit(solution)/shard_map/attention_forward/pallas_call | solution.py:387
  128.4 2.7 attend.1
  139.3 7.9 %feed_first.1 = (bf16[512,2048]{1,0:T(8,128)(2,1)S(1)}, bf16[512,2048]{1,0:T(8,128)(2,1)S(1)}, bf16[1024,2048]{1,0:T(8,128)(2,1)S(1)}) custom-call(bf16[512,1024]{1,0:T(8,128)(2,1)} %get-tuple-element.326.n_ref.n0, f32[1,2048]{1,0:T(1,128)S(1)} %reshape.250.shift_ref, bf16[4,64,2048]{2,1,0:T(8,128)(2,1)} %constant_dynamic-update-slice_fusion.refs_0_, ...), custom_call_target="tpu_custom_call" | custom-call | flops 34359738368 | bytes 1024 | tf_op jit(solution)/shard_map/feed_first/pallas_call | solution.py:492
  147.2 6.3 %feed_second.1 = (bf16[512,2048]{1,0:T(8,128)(2,1)S(1)}, bf16[512,2048]{1,0:T(8,128)(2,1)S(1)}) custom-call(bf16[512,1024]{1,0:T(8,128)(2,1)} %collective-permute-done.20.n_ref.n1, bf16[1024,2048]{1,0:T(8,128)(2,1)S(1)} %get-tuple-element.307.w_ref, f32[1,2048]{1,0:T(1,128)S(1)} %reshape.250.shift_ref), custom_call_target="tpu_custom_call" | custom-call | flops 1048576 | bytes 1024 | tf_op jit(solution)/shard_map/feed_second/pallas_call | solution.py:492
  153.6 7.1 %down_grad.1 = (bf16[8,64,1024]{2,1,0:T(8,128)(2,1)S(1)}, bf16[8,64,1024]{2,1,0:T(8,128)(2,1)S(1)}, bf16[8,64,1024]{2,1,0:T(8,128)(2,1)S(1)}, bf16[8,64,1024]{2,1,0:T(8,128)(2,1)S(1)}) custom-call(bf16[512,2048]{1,0:T(8,128)(2,1)S(1)} %get-tuple-element.370.a0.a_ref, bf16[512,2048]{1,0:T(8,128)(2,1)S(1)} %get-tuple-element.367.a1.a_ref, ...), custom_call_target="tpu_custom_call" | custom-call | flops 1048576 | bytes 1024 | tf_op jit(solution)/shard_map/down_grad/pallas_call | solution.py:492
  162.4 12.5 %back_act.1 = (bf16[512,2048]{1,0:T(8,128)(2,1)S(1)}, bf16[512,2048]{1,0:T(8,128)(2,1)S(1)}, f32[1,2048]{1,0:T(1,128)S(1)}, bf16[2048,1024]{1,0:T(8,128)(2,1)S(1)}) custom-call(bf16[512,1024]{1,0:T(8,128)(2,1)} %maximum_select_fusion.1.c0.ct_ref, bf16[512,1024]{1,0:T(8,128)(2,1)} %collective-permute-done.19.c1, bf16[512,2048]{1,0:T(8,128)(2,1)S(1)} %get-tuple-element.294.s0, ...), custom_call_target="tpu_custom_call" | custom-call | flops 1048576 | bytes 1024 | tf_op jit(solution)/shard_map/back_act/pallas_call | solution.py:492
  177.6 2.4 back_up.3.a_ref
  181.3 4.1 %back_norm.1 = (bf16[512,1024]{1,0:T(8,128)(2,1)S(1)}, bf16[512,1024]{1,0:T(8,128)(2,1)S(1)}, f32[512,1024]{1,0:T(8,128)S(1)}, f32[2,1024]{1,0:T(2,128)S(1)}) custom-call(f32[512,1024]{1,0:T(8,128)S(1)} %back_up.3.a_ref, bf16[512,1024]{1,0:T(8,128)(2,1)S(1)} %collective-permute-done.21.b_ref, f32[512,1024]{1,0:T(8,128)S(1)} %copy-done.14, ...), custom_call_target="tpu_custom_call" | custom-call | flops 1048576 | bytes 1024 | tf_op jit(solution)/shard_map/back_norm/pallas_call | solution.py:492
  197.7 8.2 %up_grad.1 = (bf16[4,80,2048]{2,1,0:T(8,128)(2,1)}, bf16[4,80,2048]{2,1,0:T(8,128)(2,1)S(1)}, bf16[4,80,2048]{2,1,0:T(8,128)(2,1)}, bf16[4,80,2048]{2,1,0:T(8,128)(2,1)S(1)}) custom-call(bf16[512,1024]{1,0:T(8,128)(2,1)} %get-tuple-element.326.n_ref.n0, bf16[512,1024]{1,0:T(8,128)(2,1)} %collective-permute-done.20.n_ref.n1, ...), custom_call_target="tpu_custom_call" | custom-call | flops 1048576 | bytes 1024 | tf_op jit(solution)/shard_map/up_grad/pallas_call | solution.py:492
  211.8 19.5 %attention_backward.1.g_ref = bf16[3,512,1024]{2,1,0:T(8,128)(2,1)S(1)} custom-call(s32[2]{0:T(128)S(1)} %get-tuple-element.455.phone_ref, s32[2]{0:T(128)S(1)} %get-tuple-element.456.prompt_ref, s32[2]{0:T(128)S(1)} %fusion.5.target_ref, bf16[512,3072]{1,0:T(8,128)(2,1)S(1)} %get-tuple-element.336.q_ref.k_ref.v_ref, ...), custom_call_target="tpu_custom_call" | custom-call | flops 1048576 | bytes 1024 | tf_op jit(solution)/shard_map/attention_backward/pallas_call | solution.py:461
  231.3 8.2 %collective-permute-done.25 = bf16[4,80,2048]{2,1,0:T(8,128)(2,1)} collective-permute-done((bf16[4,80,2048]{2,1,0:T(8,128)(2,1)}, bf16[4,80,2048]{2,1,0:T(8,128)(2,1)}, u32[]{:S(2)}, u32[]{:S(2)}) %collective-permute-start.25) | collective-permute-done | bytes 1310752 | tf_op jit(solution)/shard_map/ppermute | solution.py:32
  240.2 2.9 add_convert_fusion.5
  244.1 2.9 add_convert_fusion.6
  248.7 5.2 %attn_grad.1 = (bf16[16,32,3072]{2,1,0:T(8,128)(2,1)}, bf16[16,32,3072]{2,1,0:T(8,128)(2,1)S(1)}) custom-call(bf16[512,1024]{1,0:T(8,128)(2,1)S(1)} %copy-done.32, bf16[3,512,1024]{2,1,0:T(8,128)(2,1)S(1)} %attention_backward.1.g_ref), custom_call_target="tpu_custom_call" | custom-call | flops 1048576 | bytes 1024 | tf_op jit(solution)/shard_map/attn_grad/pallas_call | solution.py:492
  253.9 2.8 copy-done.22
  256.7 4.4 %back_first.1 = (bf16[2,256,1024]{2,1,0:T(8,128)(2,1)S(1)}, f32[2,1024]{1,0:T(2,128)S(1)}) custom-call(bf16[3,512,1024]{2,1,0:T(8,128)(2,1)S(1)} %attention_backward.1.g_ref, bf16[1024,3072]{1,0:T(8,128)(2,1)S(1)} %bitcast.113, bf16[512,1024]{1,0:T(8,128)(2,1)S(1)} %copy-done.6, f32[8,1024]{1,0:T(8,128)S(1)} %get-tuple-element.351.vec_ref, ...), custom_call_target="tpu_custom_call" | custom-call | flops 34359738368 | bytes 1024 | tf_op jit(solution)/shard_map/back_first/pallas_call | solution.py:492
  266.0 4.1 %core_sum.1 = (bf16[4,32,3200]{2,1,0:T(8,128)(2,1)}, bf16[4,32,3200]{2,1,0:T(8,128)(2,1)S(1)}, bf16[4,32,3200]{2,1,0:T(8,128)(2,1)}, bf16[4,32,3200]{2,1,0:T(8,128)(2,1)S(1)}) custom-call(bf16[16,32,3072]{2,1,0:T(8,128)(2,1)S(1)} %get-tuple-element.359.a_ref, bf16[16,32,3072]{2,1,0:T(8,128)(2,1)} %collective-permute-done.27.b_ref, ...), custom_call_target="tpu_custom_call" | custom-call | flops 1048576 | bytes 1024 | tf_op jit(solution)/shard_map/core_sum/pallas_call | solution.py:492
  274.7 2.5 down_back.3
  281.1 10.6 %collective-permute-done.33 = bf16[4,32,3200]{2,1,0:T(8,128)(2,1)} collective-permute-done((bf16[4,32,3200]{2,1,0:T(8,128)(2,1)}, bf16[4,32,3200]{2,1,0:T(8,128)(2,1)}, u32[]{:S(2)}, u32[]{:S(2)}) %collective-permute-start.33) | collective-permute-done | bytes 819232 | tf_op jit(solution)/shard_map/ppermute | solution.py:32
  300.7 10.4 %collective-permute-done.36 = bf16[64,4224]{1,0:T(8,128)(2,1)S(1)} collective-permute-done((bf16[64,4224]{1,0:T(8,128)(2,1)S(1)}, bf16[64,4224]{1,0:T(8,128)(2,1)S(1)}, u32[]{:S(2)}, u32[]{:S(2)}) %collective-permute-start.36) | collective-permute-done | bytes 540704 | tf_op jit(solution)/shard_map/ppermute | solution.py:32
  311.0 2.5 collective-permute-done.35
  323.9 13.1 %collective-permute-done.37 = bf16[256,1024]{1,0:T(8,128)(2,1)S(1)} collective-permute-done((bf16[256,1024]{1,0:T(8,128)(2,1)}, bf16[256,1024]{1,0:T(8,128)(2,1)S(1)}, u32[]{:S(2)}, u32[]{:S(2)}) %collective-permute-start.37) | collective-permute-done | bytes 524320 | tf_op jit(solution)/shard_map/ppermute | solution.py:32
  338.2 2.7 fusion
  (295 shorter events, 117.7 us)
Async XLA Ops:
  7.2 68.0 %all-gather.5.cloned.1.call-start = ((), (), s32[]{:S(2)}) async-start(), calls=%async_computation.4 | async-start | bytes 1310720 | tf_op jit(solution)/shard_map/all_gather | solution.py:59
  13.8 26.3 %collective-permute-start.4 = (bf16[2,256,1024]{2,1,0:T(8,128)(2,1)}, bf16[2,256,1024]{2,1,0:T(8,128)(2,1)S(1)}, u32[]{:S(2)}, u32[]{:S(2)}) collective-permute-start(bf16[2,256,1024]{2,1,0:T(8,128)(2,1)} %pad_maximum_fusion.4), channel_id=1, source_target_pairs={{0,16},{16,0},{1,17},{17,1},{2,18},{18,2},{3,19},{19,3},{4,20},{20... | collective-permute-start | bytes 3145736 | tf_op jit(solution)/shard_map/ppermute | solution.py:32
  16.8 26.4 %collective-permute-start.1 = (bf16[1,32,4224]{2,1,0:T(8,128)(2,1)S(1)}, bf16[1,32,4224]{2,1,0:T(8,128)(2,1)S(1)}, u32[]{:S(2)}, u32[]{:S(2)}) collective-permute-start(bf16[1,32,4224]{2,1,0:T(8,128)(2,1)S(1)} %bitcast.118), channel_id=1, source_target_pairs={{0,4},{1,5},{2,6},{3,7},{4,0},{5,1},{6,2},{7,3},{8,12},{9,13},{10,... | collective-permute-start | bytes 811016 | tf_op jit(solution)/shard_map/ppermute | solution.py:34
  18.4 24.8 %collective-permute-start.2 = (bf16[1,32,4224]{2,1,0:T(8,128)(2,1)S(1)}, bf16[1,32,4224]{2,1,0:T(8,128)(2,1)S(1)}, u32[]{:S(2)}, u32[]{:S(2)}) collective-permute-start(bf16[1,32,4224]{2,1,0:T(8,128)(2,1)S(1)} %bitcast.119), channel_id=1, source_target_pairs={{0,8},{1,9},{2,10},{3,11},{4,12},{5,13},{6,14},{7,15},{8,0},{9,1},... | collective-permute-start | bytes 811016 | tf_op jit(solution)/shard_map/ppermute | solution.py:34
  20.9 22.2 %collective-permute-start.3 = (bf16[1,32,4224]{2,1,0:T(8,128)(2,1)S(1)}, bf16[1,32,4224]{2,1,0:T(8,128)(2,1)}, u32[]{:S(2)}, u32[]{:S(2)}) collective-permute-start(bf16[1,32,4224]{2,1,0:T(8,128)(2,1)S(1)} %bitcast.120), channel_id=1, source_target_pairs={{0,12},{1,13},{2,14},{3,15},{4,8},{5,9},{6,10},{7,11},{8,4},{9,5},... | collective-permute-start | bytes 811016 | tf_op jit(solution)/shard_map/ppermute | solution.py:34
  44.4 16.3 %collective-permute-start.5 = (bf16[64,5248]{1,0:T(8,128)(2,1)S(1)}, bf16[64,5248]{1,0:T(8,128)(2,1)S(1)}, u32[]{:S(2)}, u32[]{:S(2)}) collective-permute-start(bf16[64,5248]{1,0:T(8,128)(2,1)S(1)} %pad_maximum_fusion.5), channel_id=1, source_target_pairs={{0,2},{1,3},{2,0},{3,1},{4,6},{5,7},{6,4},{7,5},{8,10},{9,11},{10,... | collective-permute-start | bytes 2015240 | tf_op jit(solution)/shard_map/ppermute | solution.py:34
  47.7 86.9 %all-gather.7.cloned.1.call-start = ((), (), s32[]{:S(2)}) async-start(), calls=%async_computation.5 | async-start | bytes 2621440 | tf_op jit(solution)/shard_map/all_gather | solution.py:59
  62.8 23.7 %collective-permute-start.11 = (bf16[4,32,4224]{2,1,0:T(8,128)(2,1)S(1)}, bf16[4,32,4224]{2,1,0:T(8,128)(2,1)S(1)}, u32[]{:S(2)}, u32[]{:S(2)}) collective-permute-start(bf16[4,32,4224]{2,1,0:T(8,128)(2,1)S(1)} %pad_maximum_fusion.3.refs_2_), channel_id=1, source_target_pairs={{0,2},{1,3},{2,0},{3,1},{4,6},{5,7},{6,4},{7,5},{8,10},{9,11},{10,... | collective-permute-start | bytes 3244040 | tf_op jit(solution)/shard_map/ppermute | solution.py:34
  63.9 23.8 %collective-permute-start.9 = (bf16[4,32,4224]{2,1,0:T(8,128)(2,1)S(1)}, bf16[4,32,4224]{2,1,0:T(8,128)(2,1)}, u32[]{:S(2)}, u32[]{:S(2)}) collective-permute-start(bf16[4,32,4224]{2,1,0:T(8,128)(2,1)S(1)} %pad_maximum_fusion.2.refs_0_), channel_id=1, source_target_pairs={{0,16},{16,0},{1,17},{17,1},{2,18},{18,2},{3,19},{19,3},{4,20},{20... | collective-permute-start | bytes 3244040 | tf_op jit(solution)/shard_map/ppermute | solution.py:32
  66.4 21.7 %collective-permute-start.8 = (bf16[4,32,4224]{2,1,0:T(8,128)(2,1)S(1)}, bf16[4,32,4224]{2,1,0:T(8,128)(2,1)}, u32[]{:S(2)}, u32[]{:S(2)}) collective-permute-start(bf16[4,32,4224]{2,1,0:T(8,128)(2,1)S(1)} %pad_maximum_fusion.3.refs_2_), channel_id=1, source_target_pairs={{0,1},{1,0},{2,3},{3,2},{4,5},{5,4},{6,7},{7,6},{8,9},{9,8},{10,11... | collective-permute-start | bytes 3244040 | tf_op jit(solution)/shard_map/ppermute | solution.py:34
  66.5 21.6 %collective-permute-start.7 = (bf16[4,32,4224]{2,1,0:T(8,128)(2,1)S(1)}, bf16[4,32,4224]{2,1,0:T(8,128)(2,1)}, u32[]{:S(2)}, u32[]{:S(2)}) collective-permute-start(bf16[4,32,4224]{2,1,0:T(8,128)(2,1)S(1)} %pad_maximum_fusion.2.refs_0_), channel_id=1, source_target_pairs={{0,1},{1,0},{2,3},{3,2},{4,5},{5,4},{6,7},{7,6},{8,9},{9,8},{10,11... | collective-permute-start | bytes 3244040 | tf_op jit(solution)/shard_map/ppermute | solution.py:34
  87.7 176.5 %reduce-scatter.3.cloned.1.call-start = ((), (), s32[]{:S(2)}) async-start(), calls=%async_computation.2 | async-start | bytes 2621440 | tf_op jit(solution)/shard_map/reduce_scatter | solution.py:63
  107.7 26.9 %collective-permute-start.16 = (bf16[4,64,2048]{2,1,0:T(8,128)(2,1)}, bf16[4,64,2048]{2,1,0:T(8,128)(2,1)}, u32[]{:S(2)}, u32[]{:S(2)}) collective-permute-start(bf16[4,64,2048]{2,1,0:T(8,128)(2,1)} %constant_dynamic-update-slice_fusion.2.refs_2_), channel_id=1, source_target_pairs={{0,2},{1,3},{2,0},{3,1},{4,6},{5,7},{6,4},{7,5},{8,10},{9,11},{10,... | collective-permute-start | bytes 3145736 | tf_op jit(solution)/shard_map/ppermute | solution.py:34
  110.5 24.2 %collective-permute-start.15 = (bf16[4,64,2048]{2,1,0:T(8,128)(2,1)}, bf16[4,64,2048]{2,1,0:T(8,128)(2,1)}, u32[]{:S(2)}, u32[]{:S(2)}) collective-permute-start(bf16[4,64,2048]{2,1,0:T(8,128)(2,1)} %constant_dynamic-update-slice_fusion.refs_0_), channel_id=1, source_target_pairs={{0,16},{16,0},{1,17},{17,1},{2,18},{18,2},{3,19},{19,3},{4,20},{20... | collective-permute-start | bytes 3145736 | tf_op jit(solution)/shard_map/ppermute | solution.py:32
  112.0 41.5 %collective-permute-start.19 = (bf16[512,1024]{1,0:T(8,128)(2,1)}, bf16[512,1024]{1,0:T(8,128)(2,1)}, u32[]{:S(2)}, u32[]{:S(2)}) collective-permute-start(bf16[512,1024]{1,0:T(8,128)(2,1)} %maximum_select_fusion.1.c0.ct_ref), channel_id=1, source_target_pairs={{0,1},{1,0},{2,3},{3,2},{4,5},{5,4},{6,7},{7,6},{8,9},{9,8},{10,11... | collective-permute-start | bytes 3145736 | tf_op jit(solution)/shard_map/ppermute | solution.py:34
  136.4 25.6 %collective-permute-start.17 = (bf16[8,64,1024]{2,1,0:T(8,128)(2,1)S(1)}, bf16[8,64,1024]{2,1,0:T(8,128)(2,1)S(1)}, u32[]{:S(2)}, u32[]{:S(2)}) collective-permute-start(bf16[8,64,1024]{2,1,0:T(8,128)(2,1)S(1)} %bitcast.116), channel_id=1, source_target_pairs={{0,16},{16,0},{1,17},{17,1},{2,18},{18,2},{3,19},{19,3},{4,20},{20... | collective-permute-start | bytes 3145736 | tf_op jit(solution)/shard_map/ppermute | solution.py:32
  138.0 24.4 %collective-permute-start.18 = (bf16[8,64,1024]{2,1,0:T(8,128)(2,1)S(1)}, bf16[8,64,1024]{2,1,0:T(8,128)(2,1)S(1)}, u32[]{:S(2)}, u32[]{:S(2)}) collective-permute-start(bf16[8,64,1024]{2,1,0:T(8,128)(2,1)S(1)} %bitcast.114), channel_id=1, source_target_pairs={{0,2},{1,3},{2,0},{3,1},{4,6},{5,7},{6,4},{7,5},{8,10},{9,11},{10,... | collective-permute-start | bytes 3145736 | tf_op jit(solution)/shard_map/ppermute | solution.py:34
  160.7 29.9 %collective-permute-start.23 = (bf16[8,64,1024]{2,1,0:T(8,128)(2,1)S(1)}, bf16[8,64,1024]{2,1,0:T(8,128)(2,1)S(1)}, u32[]{:S(2)}, u32[]{:S(2)}) collective-permute-start(bf16[8,64,1024]{2,1,0:T(8,128)(2,1)S(1)} %get-tuple-element.288), channel_id=1, source_target_pairs={{0,16},{16,0},{1,17},{17,1},{2,18},{18,2},{3,19},{19,3},{4,20},{20... | collective-permute-start | bytes 3145736 | tf_op jit(solution)/shard_map/ppermute | solution.py:32
  161.4 29.2 %collective-permute-start.24 = (bf16[8,64,1024]{2,1,0:T(8,128)(2,1)S(1)}, bf16[8,64,1024]{2,1,0:T(8,128)(2,1)S(1)}, u32[]{:S(2)}, u32[]{:S(2)}) collective-permute-start(bf16[8,64,1024]{2,1,0:T(8,128)(2,1)S(1)} %get-tuple-element.290), channel_id=1, source_target_pairs={{0,2},{1,3},{2,0},{3,1},{4,6},{5,7},{6,4},{7,5},{8,10},{9,11},{10,... | collective-permute-start | bytes 3145736 | tf_op jit(solution)/shard_map/ppermute | solution.py:34
  208.1 31.3 %collective-permute-start.25 = (bf16[4,80,2048]{2,1,0:T(8,128)(2,1)}, bf16[4,80,2048]{2,1,0:T(8,128)(2,1)}, u32[]{:S(2)}, u32[]{:S(2)}) collective-permute-start(bf16[4,80,2048]{2,1,0:T(8,128)(2,1)} %get-tuple-element.332), channel_id=1, source_target_pairs={{0,16},{16,0},{1,17},{17,1},{2,18},{18,2},{3,19},{19,3},{4,20},{20... | collective-permute-start | bytes 3932168 | tf_op jit(solution)/shard_map/ppermute | solution.py:32
  209.2 31.1 %collective-permute-start.26 = (bf16[4,80,2048]{2,1,0:T(8,128)(2,1)}, bf16[4,80,2048]{2,1,0:T(8,128)(2,1)}, u32[]{:S(2)}, u32[]{:S(2)}) collective-permute-start(bf16[4,80,2048]{2,1,0:T(8,128)(2,1)} %get-tuple-element.334), channel_id=1, source_target_pairs={{0,2},{1,3},{2,0},{3,1},{4,6},{5,7},{6,4},{7,5},{8,10},{9,11},{10,... | collective-permute-start | bytes 3932168 | tf_op jit(solution)/shard_map/ppermute | solution.py:34
  210.5 105.1 %reduce-scatter.5.cloned.1.call-start = ((), (), s32[]{:S(2)}) async-start(), calls=%async_computation.3 | async-start | bytes 1638400 | tf_op jit(solution)/shard_map/reduce_scatter | solution.py:63
  243.1 34.2 %collective-permute-start.32 = (bf16[2,80,2048]{2,1,0:T(8,128)(2,1)}, bf16[2,80,2048]{2,1,0:T(8,128)(2,1)}, u32[]{:S(2)}, u32[]{:S(2)}) collective-permute-start(bf16[2,80,2048]{2,1,0:T(8,128)(2,1)} %get-tuple-element.416), channel_id=1, source_target_pairs={{0,16},{16,0},{1,17},{17,1},{2,18},{18,2},{3,19},{19,3},{4,20},{20... | collective-permute-start | bytes 1966088 | tf_op jit(solution)/shard_map/ppermute | solution.py:32
  246.9 30.4 %collective-permute-start.31 = (bf16[2,80,2048]{2,1,0:T(8,128)(2,1)}, bf16[2,80,2048]{2,1,0:T(8,128)(2,1)}, u32[]{:S(2)}, u32[]{:S(2)}) collective-permute-start(bf16[2,80,2048]{2,1,0:T(8,128)(2,1)} %get-tuple-element.418), channel_id=1, source_target_pairs={{0,2},{1,3},{2,0},{3,1},{4,6},{5,7},{6,4},{7,5},{8,10},{9,11},{10,... | collective-permute-start | bytes 1966088 | tf_op jit(solution)/shard_map/ppermute | solution.py:34
  270.8 20.9 %collective-permute-start.33 = (bf16[4,32,3200]{2,1,0:T(8,128)(2,1)}, bf16[4,32,3200]{2,1,0:T(8,128)(2,1)}, u32[]{:S(2)}, u32[]{:S(2)}) collective-permute-start(bf16[4,32,3200]{2,1,0:T(8,128)(2,1)} %get-tuple-element.363), channel_id=1, source_target_pairs={{0,16},{16,0},{1,17},{17,1},{2,18},{18,2},{3,19},{19,3},{4,20},{20... | collective-permute-start | bytes 2457608 | tf_op jit(solution)/shard_map/ppermute | solution.py:32
  271.5 20.6 %collective-permute-start.34 = (bf16[4,32,3200]{2,1,0:T(8,128)(2,1)}, bf16[4,32,3200]{2,1,0:T(8,128)(2,1)}, u32[]{:S(2)}, u32[]{:S(2)}) collective-permute-start(bf16[4,32,3200]{2,1,0:T(8,128)(2,1)} %get-tuple-element.365), channel_id=1, source_target_pairs={{0,2},{1,3},{2,0},{3,1},{4,6},{5,7},{6,4},{7,5},{8,10},{9,11},{10,... | collective-permute-start | bytes 2457608 | tf_op jit(solution)/shard_map/ppermute | solution.py:34
  274.6 17.5 %collective-permute-start.30 = (bf16[512,1024]{1,0:T(8,128)(2,1)S(1)}, bf16[512,1024]{1,0:T(8,128)(2,1)}, u32[]{:S(2)}, u32[]{:S(2)}) collective-permute-start(bf16[512,1024]{1,0:T(8,128)(2,1)S(1)} %down_back.2), channel_id=1, source_target_pairs={{0,1},{1,0},{2,3},{3,2},{4,5},{5,4},{6,7},{7,6},{8,9},{9,8},{10,11... | collective-permute-start | bytes 3145736 | tf_op jit(solution)/shard_map/ppermute | solution.py:34
  313.6 24.6 %collective-permute-start.39 = (bf16[256,1024]{1,0:T(8,128)(2,1)}, bf16[256,1024]{1,0:T(8,128)(2,1)}, u32[]{:S(2)}, u32[]{:S(2)}) collective-permute-start(bf16[256,1024]{1,0:T(8,128)(2,1)} %get-tuple-element.402), channel_id=1, source_target_pairs={{0,16},{16,0},{1,17},{17,1},{2,18},{18,2},{3,19},{19,3},{4,20},{20... | collective-permute-start | bytes 1572872 | tf_op jit(solution)/shard_map/ppermute | solution.py:32
  314.2 22.8 %collective-permute-start.37 = (bf16[256,1024]{1,0:T(8,128)(2,1)}, bf16[256,1024]{1,0:T(8,128)(2,1)S(1)}, u32[]{:S(2)}, u32[]{:S(2)}) collective-permute-start(bf16[256,1024]{1,0:T(8,128)(2,1)} %get-tuple-element.388), channel_id=1, source_target_pairs={{0,16},{16,0},{1,17},{17,1},{2,18},{18,2},{3,19},{19,3},{4,20},{20... | collective-permute-start | bytes 1572872 | tf_op jit(solution)/shard_map/ppermute | solution.py:32
  316.8 24.1 %collective-permute-start.41 = (bf16[32,3200]{1,0:T(8,128)(2,1)S(1)}, bf16[32,3200]{1,0:T(8,128)(2,1)S(1)}, u32[]{:S(2)}, u32[]{:S(2)}) collective-permute-start(bf16[32,3200]{1,0:T(8,128)(2,1)S(1)} %get-tuple-element.446), channel_id=1, source_target_pairs={{0,8},{1,9},{2,10},{3,11},{4,12},{5,13},{6,14},{7,15},{8,0},{9,1},... | collective-permute-start | bytes 614408 | tf_op jit(solution)/shard_map/ppermute | solution.py:34
  318.4 22.5 %collective-permute-start.42 = (bf16[32,3200]{1,0:T(8,128)(2,1)S(1)}, bf16[32,3200]{1,0:T(8,128)(2,1)S(1)}, u32[]{:S(2)}, u32[]{:S(2)}) collective-permute-start(bf16[32,3200]{1,0:T(8,128)(2,1)S(1)} %get-tuple-element.445), channel_id=1, source_target_pairs={{0,12},{1,13},{2,14},{3,15},{4,8},{5,9},{6,10},{7,11},{8,4},{9,5},... | collective-permute-start | bytes 614408 | tf_op jit(solution)/shard_map/ppermute | solution.py:34
  322.3 18.6 %collective-permute-start.40 = (bf16[32,3200]{1,0:T(8,128)(2,1)S(1)}, bf16[32,3200]{1,0:T(8,128)(2,1)S(1)}, u32[]{:S(2)}, u32[]{:S(2)}) collective-permute-start(bf16[32,3200]{1,0:T(8,128)(2,1)S(1)} %get-tuple-element.438), channel_id=1, source_target_pairs={{0,4},{1,5},{2,6},{3,7},{4,0},{5,1},{6,2},{7,3},{8,12},{9,13},{10,... | collective-permute-start | bytes 614408 | tf_op jit(solution)/shard_map/ppermute | solution.py:34
  (76 other events, 511.0 us)
Sparse Core Ops, SparseCore 0:
  47.9 27.2 all-gather.4
  87.8 46.7 all-gather.6
  210.6 43.3 reduce-scatter.2
  281.3 30.9 reduce-scatter.4

commit v3 on v2

--- a/solution.py
+++ b/solution.py
@@ -199,6 +199,63 @@
     return (left.astype(F32) + right.astype(F32)).astype(left.dtype)
 
 
+def add_halves(left, left_in, right, right_in, extras):
+    count, rows, cols = left.shape
+    half = count // 2
+    more = extras[0].shape[2] if extras else 0
+    extras = list(extras) * 2
+
+    def kernel(*refs):
+        ins, outs = refs[: 8 + len(extras)], refs[8 + len(extras) :]
+        for side in range(2):
+            a, b, c, d = ins[4 * side : 4 * side + 4]
+            own, send = outs[2 + side], outs[side]
+            own[...] = (a[...].astype(F32) + b[...].astype(F32)).astype(BF)
+            total = (c[0].astype(F32) + d[0].astype(F32)).astype(BF)
+            if extras:
+                send[:, :cols] = total
+                send[:, cols:] = ins[8 + side][0]
+            else:
+                send[0] = total
+
+    low = pl.BlockSpec((1, rows, cols), lambda i: (i, 0, 0))
+    high = pl.BlockSpec((1, rows, cols), lambda i: (i + half, 0, 0))
+    wide = pl.BlockSpec((rows, cols + more), lambda i: (i, 0))
+    send = jax.ShapeDtypeStruct((half * rows, cols + more) if extras else (half, rows, cols), BF)
+    own = jax.ShapeDtypeStruct((half, rows, cols), BF)
+    return pl.pallas_call(
+        kernel,
+        grid=(half,),
+        out_shape=[send, send, own, own],
+        in_specs=[low, low, high, high] * 2
+        + [pl.BlockSpec((1, rows, more), lambda i, n=n: (n, i, 0)) for n in (1, 3)[: len(extras)]],
+        out_specs=[wide if extras else low] * 2 + [low] * 2,
+        compiler_params=pltpu.CompilerParams(vmem_limit_bytes=16 << 20),
+        cost_estimate=pl.CostEstimate(flops=1 << 35, bytes_accessed=1 << 10, transcendentals=0),
+        name="add_halves",
+    )(left, left_in, left, left_in, right, right_in, right, right_in, *extras)
+
+
+def add_column(left, left_in, right, right_in):
+    half, rows, cols = left.shape
+
+    def kernel(a_ref, b_ref, c_ref, d_ref, out_ref):
+        out_ref[0] = (a_ref[0].astype(F32) + b_ref[0].astype(F32)).astype(BF)
+        out_ref[1] = (c_ref[0].astype(F32) + d_ref[0].astype(F32)).astype(BF)
+
+    part = pl.BlockSpec((1, rows, cols), lambda i: (i, 0, 0))
+    return pl.pallas_call(
+        kernel,
+        grid=(half,),
+        out_shape=jax.ShapeDtypeStruct((2, half, rows, cols), BF),
+        in_specs=[part] * 4,
+        out_specs=pl.BlockSpec((2, None, rows, cols), lambda i: (0, i, 0, 0)),
+        compiler_params=pltpu.CompilerParams(vmem_limit_bytes=16 << 20),
+        cost_estimate=pl.CostEstimate(flops=1 << 20, bytes_accessed=1 << 10, transcendentals=0),
+        name="add_column",
+    )(left, left_in, right, right_in).reshape(2 * half, rows, cols)
+
+
 class Scatter:
     def __init__(self, chain, by_permutes):
         self.chain = chain
@@ -211,19 +268,9 @@
         return list(self.sides)
 
     def two(self, *first, extras=()):
-        half = depth() // 2
-
-        def add(left, left_in, right, right_in, extras):
-            send = (plus(left[half:], left_in[half:]), plus(right[half:], right_in[half:]))
-            return (
-                *beside(send, extras),
-                plus(left[:half], left_in[:half]),
-                plus(right[:half], right_in[:half]),
-            )
-
         _, left, _, right = self.parts
         left_in, right_in = lax.optimization_barrier((self.sides, first))[0]
-        self.sums = self.chain(add, left, left_in, right, right_in, extras)
+        self.sums = self.chain(add_halves, left, left_in, right, right_in, extras)
         self.ends = swap(self.sums[0], 2), swap(self.sums[1], "y")
         return list(self.ends)
 
@@ -242,7 +289,7 @@
                     *plus(right, right_in),
                     left[0].astype(F32) + left_in[0].astype(F32),
                 )
-            return jnp.concatenate([plus(left, left_in), plus(right, right_in)], 0)
+            return add_column(left, left_in, right, right_in)
 
         made = self.chain(add, left, left_in, right, right_in)
         if not self.rel_z:
@@ -282,13 +329,6 @@
         _, left, _, right = self.parts
         self.lines = z_scatter(self.chain(add, left, self.sides[0], right, self.sides[1]))
         return self.lines
-
-    def last(self):
-        def cut(lines):
-            lines = lines.reshape(4, *lines.shape[-2:])
-            return lines[1], lines[3], lines[0], lines[2]
-
-        return self.chain(cut, self.lines)
 
 
 def ordered(flag, own, other, axis):
@@ -353,7 +393,9 @@
     segs = phone.shape[0]
     group = 2
 
-    def kernel(phone_ref, prompt_ref, target_ref, q_ref, k_ref, v_ref, out_ref, bias_ref):
+    def kernel(
+        phone_ref, prompt_ref, target_ref, q_ref, k_ref, v_ref, out_ref, log_ref, bias_ref
+    ):
         @pl.when(pl.program_id(0) == 0)
         def _():
             ph = [phone_ref[s] for s in range(segs)]
@@ -376,8 +418,11 @@
                 for j in range(2):
                     q = jnp.where((lane // HEAD) == j, q_ref[at, cols] * scale, zero)
                     s = bdot(k_ref[:keys, cols], q, NT) + bias_ref[:keys, at]
-                    e = jnp.exp(s - jnp.max(s, 0, keepdims=True))
-                    p = (e * (1.0 / jnp.sum(e, 0, keepdims=True))).astype(BF)
+                    peak = jnp.max(s, 0, keepdims=True)
+                    e = jnp.exp(s - peak)
+                    total = jnp.sum(e, 0, keepdims=True)
+                    log_ref[0, 2 * pair + j : 2 * pair + j + 1, at] = peak + jnp.log(total)
+                    p = (e * (1.0 / total)).astype(BF)
                     outs.append(bdot(v_ref[:keys, cols], p, TN)[j * HEAD : (j + 1) * HEAD])
                 out_ref[at, cols] = jnp.transpose(jnp.concatenate(outs, 0)).astype(BF)
 
@@ -387,7 +432,10 @@
     return pl.pallas_call(
         kernel,
         grid=(steps,),
-        out_shape=jax.ShapeDtypeStruct((2 * ROW, D), BF),
+        out_shape=[
+            jax.ShapeDtypeStruct((2 * ROW, D), BF),
+            jax.ShapeDtypeStruct((steps, 2 * group, 2 * ROW), F32),
+        ],
         in_specs=[
             smem,
             smem,
@@ -396,7 +444,10 @@
             pl.BlockSpec(part, lambda h: (0, h + steps)),
             pl.BlockSpec(part, lambda h: (0, h + 2 * steps)),
         ],
-        out_specs=pl.BlockSpec(part, lambda h: (0, h)),
+        out_specs=[
+            pl.BlockSpec(part, lambda h: (0, h)),
+            pl.BlockSpec((1, 2 * group, 2 * ROW), lambda h: (h, 0, 0)),
+        ],
         scratch_shapes=[pltpu.VMEM((2 * ROW, 2 * ROW), F32)],
         compiler_params=pltpu.CompilerParams(vmem_limit_bytes=16 << 20),
         cost_estimate=pl.CostEstimate(flops=1 << 20, bytes_accessed=1 << 10, transcendentals=0),
@@ -404,12 +455,12 @@
     )(phone, prompt, target, qkv, qkv, qkv)
 
 
-def attention_backward(qkv, grad_mixed, phone, prompt, target):
+def attention_backward(qkv, grad_mixed, logs, phone, prompt, target):
     segs = phone.shape[0]
     group = 2
 
     def kernel(
-        phone_ref, prompt_ref, target_ref, q_ref, k_ref, v_ref, g_ref, out_ref, bias_ref
+        phone_ref, prompt_ref, target_ref, q_ref, k_ref, v_ref, g_ref, log_ref, out_ref, bias_ref
     ):
         @pl.when(pl.program_id(0) == 0)
         def _():
@@ -439,8 +490,7 @@
                     k, v = k_ref[:keys, cols], v_ref[:keys, cols]
                     s = bdot(k, q, NT) + bias_ref[:keys, at]
                     dp = bdot(v, g, NT)
-                    e = jnp.exp(s - jnp.max(s, 0, keepdims=True))
-                    p = e * (1.0 / jnp.sum(e, 0, keepdims=True))
+                    p = jnp.exp(s - log_ref[0, 2 * pair + j : 2 * pair + j + 1, at])
                     inner = jnp.sum(dp * p, 0, keepdims=True)
                     ds = (p * (dp - inner)).astype(BF)
                     dvs[rows, j] = bdot(p.astype(BF), g_all, NN)
@@ -470,13 +520,14 @@
             pl.BlockSpec(block, lambda h: (0, h + steps)),
             pl.BlockSpec(block, lambda h: (0, h + 2 * steps)),
             pl.BlockSpec(block, lambda h: (0, h)),
+            pl.BlockSpec((1, 2 * group, 2 * ROW), lambda h: (h, 0, 0)),
         ],
         out_specs=pl.BlockSpec((3, *block), lambda h: (0, 0, h)),
         scratch_shapes=[pltpu.VMEM((2 * ROW, 2 * ROW), F32)],
         compiler_params=pltpu.CompilerParams(vmem_limit_bytes=16 << 20),
         cost_estimate=pl.CostEstimate(flops=1 << 20, bytes_accessed=1 << 10, transcendentals=0),
         name="attention_backward",
-    )(phone, prompt, target, qkv, qkv, qkv, grad_mixed)
+    )(phone, prompt, target, qkv, qkv, qkv, grad_mixed, logs)
 
 
 VMEM = pl.BlockSpec(memory_space=pltpu.VMEM)
@@ -738,9 +789,9 @@
         waves = [[], []]
         for n in range(4):
             for i, (jy, _, _) in enumerate(pieces[n][1]):
-                copy = copy_of(n, i)
-                copy.start()
-                waves[jy].append(copy)
+                waves[jy].append(copy_of(n, i))
+        for copy in waves[0] + waves[1]:
+            copy.start()
         for jy in range(2):
             for copy in waves[jy]:
                 copy.wait()
@@ -898,10 +949,11 @@
 
 
 def back_first(grads, weight, resident, vec, hidden_grad):
-    def kernel(g_ref, w_ref, x_ref, vec_ref, h_ref, out_ref, sum_ref):
+    def kernel(g_ref, w_ref, x_ref, vec_ref, h_ref, own_ref, send_ref, sum_ref):
         first, second = 0.0, 0.0
-        for half in range(2):
-            rows = slice(half * ROW, (half + 1) * ROW)
+        y = position()[0]
+        for half, out_ref in ((y, own_ref), (1 - y, send_ref)):
+            rows = pl.ds(pl.multiple_of(half * ROW, ROW), ROW)
             normal, inv = normal_of(x_ref[rows, :].astype(F32))
             grad = 0.0
             for part in range(3):
@@ -909,17 +961,17 @@
             first = first + jnp.sum(grad * normal, 0, keepdims=True)
             second = second + jnp.sum(grad, 0, keepdims=True)
             total = h_ref[rows, :] + norm_back(grad, normal, inv, vec_ref[0:1, :])
-            out_ref[half] = total.astype(BF)
+            out_ref[...] = total.astype(BF)
         sum_ref[0:1, :] = first
         sum_ref[1:2, :] = second
 
-    outs = [shape_of((2, ROW, D)), shape_of((2, D), F32)]
+    outs = [shape_of((ROW, D)), shape_of((ROW, D)), shape_of((2, D), F32)]
     args = (grads, weight, resident, vec, hidden_grad)
-    return call("back_first", kernel, outs, args, long=True)
-
-
-def down_back(act, weight, dtype, hidden=None, late=None):
-    extra = tuple(v for v in (hidden, late) if v is not None)
+    return call("back_first", kernel, outs, args)
+
+
+def down_back(act, weight, dtype, hidden=None):
+    extra = () if hidden is None else (hidden,)
 
     def kernel(a_ref, w_ref, *refs):
         out_ref = refs[-1]
@@ -929,7 +981,18 @@
                 total = total + refs[0][:, n : n + 256]
             out_ref[:, n : n + 256] = total.astype(dtype)
 
-    return call("down_back", kernel, [shape_of((2 * ROW, D), dtype)], (act, weight, *extra))[0]
+    outs = [shape_of((2 * ROW, D), dtype)]
+    return call("down_back", kernel, outs, (act, weight, *extra))[0]
+
+
+def result_of(own, other):
+    def kernel(a_ref, b_ref, own_ref, send_ref):
+        y = position()[0]
+        for half, out_ref in ((y, own_ref), (1 - y, send_ref)):
+            rows = pl.ds(pl.multiple_of(half * ROW, ROW), ROW)
+            out_ref[...] = (a_ref[rows, :] + b_ref[rows, :].astype(F32)).astype(BF)
+
+    return call("result_of", kernel, [shape_of((ROW, D))] * 2, (own, other))
 
 
 def interleave(own, other):
@@ -1038,7 +1101,7 @@
 
     normed, qkv = chain(project, resident, vec, qkv_weight)
     up_two = up_g.two()
-    mixed = chain(lambda v: attention_forward(v, *lengths), qkv)
+    mixed, logs = chain(lambda v: attention_forward(v, *lengths), qkv)
     normed_two, hidden = chain(attend, mixed, out_weight, resident, vec)
     ct_sent = swap(grad_result, 1)
     normed_sent = swap(normed_two, 1)
@@ -1089,11 +1152,10 @@
             out_in,
         )
     )
-    grads = chain(lambda a, b: attention_backward(a, b, *lengths), qkv, grad_mixed)
-    up_stwo = up_s.two()
+    grads = chain(lambda a, b, v: attention_backward(a, b, v, *lengths), qkv, grad_mixed, logs)
     attn_send, attn_keep = chain(attn_grad, normed, grads)
     attn_in = swap(attn_send, 1)
-    grad_rows, sums_one = chain(back_first, grads, qkv_weight, resident, vec, grad_hidden)
+    gx_own, gx_send, sums_one = chain(back_first, grads, qkv_weight, resident, vec, grad_hidden)
 
     def small_lines(one, two, shift):
         last = shift.reshape(chips, row_f // row_w, row_w).transpose(1, 0, 2)[:, :, None]
@@ -1102,26 +1164,18 @@
 
     sums = chain(small_lines, sums_one, sums_two, grad_shift)
     sums_in = swap(sums, 1)
-    down_x, down_y, down_one_own, down_two_own = down_s.last()
+    up_stwo = up_s.two()
     attn_parts = chain(
         lambda a, b, p, q: core_sum(a, b, p, q, attn_s.rel_z), attn_keep, attn_in, sums, sums_in
     )
-    attn_sone = attn_s.one(attn_parts)
-    later = swap(attn_parts[0][0, :16, :128], 1)
-    down_sent = swap(
-        chain(lambda a, w, v: down_back(a, w, BF, None, v), act_other, down_weight, later), 1
-    )
+    attn_sone = attn_s.one(attn_parts, *up_stwo)
+    down_sent = swap(chain(lambda a, w: down_back(a, w, BF), act_other, down_weight), 1)
     down_own = chain(lambda a, w, h: down_back(a, w, F32, h), act_own, down_weight, hidden)
-
     up_sz = up_s.over_z()
 
-    def result_of(own, other):
-        total = (own + other.astype(F32)).astype(BF).reshape(2, ROW, D)
-        return split_halves(total)
-
-    res_send, res_own = chain(result_of, down_own, down_sent)
-    gx_send, gx_own = chain(split_halves, grad_rows)
-    attn_stwo = attn_s.two(extras=(down_x, down_y))
+    down_sz = down_sz.reshape(4, half_f, D)
+    attn_stwo = attn_s.two(extras=(down_sz,))
+    res_own, res_send = chain(result_of, down_own, down_sent)
     sum_up = chain(up_s.total, up_sz)
     sum_up = sum_up.reshape(-1, FF // 2)
     out_rows = sum_up[2 * row_w :]
@@ -1129,15 +1183,16 @@
     up_rows = sum_up[: 2 * row_w].reshape(2, row_w, FF // 2)
     up_mine = lax.dynamic_index_in_dim(up_rows, c, 0, keepdims=False)
     up_theirs = swap(lax.dynamic_index_in_dim(up_rows, 1 - c, 0, keepdims=False), 1)
+    attn_sz = attn_s.over_z()
     gx_other = swap(after(gx_send, *attn_stwo), "y")
     out_other = swap(after(res_send, *attn_stwo), "y")
-    attn_sz = attn_s.over_z()
-
-    def sum_of_down(upper, from_x, lower, from_y):
+
+    def sum_of_down(lines, from_x, from_y):
+        upper, lower = lines[0], lines[2]
         from_x, from_y = (v[:, 3 * D + 128 :].reshape(half_f, D) for v in (from_x, from_y))
         return jnp.concatenate([plus(upper.astype(F32), from_x), plus(lower.astype(F32), from_y)], 0)
 
-    sum_down = chain(sum_of_down, down_one_own, attn_stwo[0], down_two_own, attn_stwo[1])
+    sum_down = chain(sum_of_down, down_sz, *attn_stwo)
 
     def home(own, other):
         return ordered(y, own[None], other[None], 0).reshape(MICRO, 1, 1, ROW, D)

time: 356 us -> 344 us (0.966)
  other arithmetic: 30 us -> 17.5 us
  waiting for transfers between devices: 97.5 us -> 92.6 us
  Pallas kernels: 119 us -> 123 us
    ppermute x13, waiting for transfers between devices: 59.5 us -> 30.6 us  [swap(): return lax.ppermute(block, 'pair', [(i, i ^ 1) for i in range(2)])]
    ppermute x30 -> x29, waiting for transfers between devices: 30.7 us -> 54.8 us  [swap(): return lax.ppermute(block, 'rows', [(i, i ^ way) for i in range(count)])]
    convert_element_type x9 -> x3, other arithmetic: 12.2 us -> 1.34 us  [plus(): return (left.astype(F32) + right.astype(F32)).astype(left.dtype)]
    pallas_call x1 -> x4, Pallas kernels: 15.9 us -> 21.1 us  [the longest x1 16 us: attention_forward(): pl.pallas_call(kernel, grid=(steps,), out_shape=[jax.ShapeDtypeStruct((2...]
    pallas_call x1, Pallas kernels: 19.5 us -> 14.6 us  [attention_backward(): pl.pallas_call(kernel, grid=(steps,), out_shape=jax.ShapeDtypeStruct((3,...]
    unnamed x124 -> x136, local copies, waits for them, and re-layouts: 24.9 us -> 28.6 us
    pallas_call x19 -> x20, Pallas kernels: 83.9 us -> 87.7 us  [call(): pl.pallas_call(kernel, out_shape=outs, in_specs=[VMEM] * len(args) if spe...]
    ppermute x30 -> x29, starting transfers between devices: 21 us -> 20.9 us  [swap(): return lax.ppermute(block, 'rows', [(i, i ^ way) for i in range(count)])]
  transfers between devices with their start and end apart: 47 -> 46, of which waited for: 21 -> 22; matrix products, arithmetic and copies ran while one was open for 14% -> 10% of each run, Pallas kernels for 32% -> 34%
where the time goes in v3:
time: 344 us; the launch traced here: 338 us
  Pallas kernels  123 us (36%)
  waiting for transfers between devices  92.6 us (27%)
  local copies, waits for them, and re-layouts  50 us (15%)
  starting transfers between devices  40.1 us (12%)
  other arithmetic  17.5 us (5%)
  between operations  14.9 us (4%)
    pallas_call x20, Pallas kernels, call(): pl.pallas_call(kernel, out_shape=outs, in_specs=[VMEM] * len(args) if spe...  87.7 us
    ppermute x29, waiting for transfers between devices, swap(): return lax.ppermute(block, 'rows', [(i, i ^ way) for i in range(count)])  54.8 us
    ppermute x13, waiting for transfers between devices, swap(): return lax.ppermute(block, 'pair', [(i, i ^ 1) for i in range(2)])  30.6 us
    unnamed x136, local copies, waits for them, and re-layouts  28.6 us
    ppermute x29, starting transfers between devices, swap(): return lax.ppermute(block, 'rows', [(i, i ^ way) for i in range(count)])  20.9 us
    ppermute x13, starting transfers between devices, swap(): return lax.ppermute(block, 'pair', [(i, i ^ 1) for i in range(2)])  18.7 us
    pallas_call x1, Pallas kernels, attention_forward(): pl.pallas_call(kernel, grid=(steps,), out_shape=[jax.ShapeDtypeStruct((2...  16 us
    pallas_call x1, Pallas kernels, attention_backward(): pl.pallas_call(kernel, grid=(steps,), out_shape=jax.ShapeDtypeStruct((3,...  14.6 us
  transfers between devices with their start and end apart: 46, of which 22 were waited for; matrix products, arithmetic and copies ran while one was open for 10% of the time, Pallas kernels for 34%

profile of v3, /device:TPU:0, one launch (start us, length us, event | category | flops | bytes accessed | tf_op | source)
XLA Modules:
  0.0 338.4 jit_solution(17213312803687566995)
XLA Ops:
  13.8 3.0 collective-permute-start.4
  18.3 2.6 collective-permute-start.2
  26.8 13.3 %collective-permute-done.4 = bf16[2,256,1024]{2,1,0:T(8,128)(2,1)S(1)} collective-permute-done((bf16[2,256,1024]{2,1,0:T(8,128)(2,1)}, bf16[2,256,1024]{2,1,0:T(8,128)(2,1)S(1)}, u32[]{:S(2)}, u32[]{:S(2)}) %collective-permute-start.4) | collective-permute-done | bytes 1048608 | tf_op jit(solution)/shard_map/ppermute | solution.py:32
  47.7 13.0 %collective-permute-done.5 = bf16[64,5248]{1,0:T(8,128)(2,1)S(1)} collective-permute-done((bf16[64,5248]{1,0:T(8,128)(2,1)S(1)}, bf16[64,5248]{1,0:T(8,128)(2,1)S(1)}, u32[]{:S(2)}, u32[]{:S(2)}) %collective-permute-start.5) | collective-permute-done | bytes 671776 | tf_op jit(solution)/shard_map/ppermute | solution.py:34
  69.8 5.3 %all-gather.5.cloned.1.call-done = bf16[256,2048]{1,0:T(8,128)(2,1)} async-done(((bf16[64,2048]{1,0:T(8,128)(2,1)}), bf16[256,2048]{1,0:T(8,128)(2,1)}) %all-gather.5.cloned.1.call-update) | async-done | bytes 1048592 | tf_op jit(solution)/shard_map/all_gather | solution.py:59
  75.2 2.3 fusion.7
  77.4 9.1 %collective-permute-done.11.refs_3_ = bf16[4,32,4224]{2,1,0:T(8,128)(2,1)S(1)} collective-permute-done((bf16[4,32,4224]{2,1,0:T(8,128)(2,1)S(1)}, bf16[4,32,4224]{2,1,0:T(8,128)(2,1)S(1)}, u32[]{:S(2)}, u32[]{:S(2)}) %collective-permute-start.11) | collective-permute-done | bytes 1081376 | tf_op jit(solution)/shard_map/ppermute | solution.py:34
  93.4 4.5 %unpack.1 = (bf16[16,2,32,3072]{3,2,1,0:T(8,128)(2,1)S(1)}, bf16[16,2,32,1024]{3,2,1,0:T(8,128)(2,1)S(1)}, f32[8,1024]{1,0:T(8,128)S(1)}) custom-call(bf16[4,32,4224]{2,1,0:T(8,128)(2,1)S(1)} %pad_maximum_fusion.1.refs_0_, bf16[4,32,4224]{2,1,0:T(8,128)(2,1)} %collective-permute-done.9.refs_1_, bf16[4,32,4224]{2,1,0:T(8,128)(2,1)S(1)} %pad_maximum_fusion.2.refs_2_, ...), custom_call_target="tpu_custom_call" | custom-call | flops 1048576 | bytes 1024 | tf_op jit(solution)/shard_map/unpack/pallas_call | solution.py:543
  99.2 3.9 %project.1 = (bf16[512,1024]{1,0:T(8,128)(2,1)S(1)}, bf16[512,3072]{1,0:T(8,128)(2,1)S(1)}) custom-call(bf16[512,1024]{1,0:T(8,128)(2,1)S(1)} %copy-done.3, f32[8,1024]{1,0:T(8,128)S(1)} %get-tuple-element.359.vec_ref, bf16[1024,3072]{1,0:T(8,128)(2,1)S(1)} %bitcast.96), custom_call_target="tpu_custom_call" | custom-call | flops 1048576 | bytes 1024 | tf_op jit(solution)/shard_map/project/pallas_call | solution.py:543
  112.4 16.0 %attention_forward.1 = (bf16[512,1024]{1,0:T(8,128)(2,1)S(1)}, f32[4,4,512]{2,1,0:T(4,128)S(1)}) custom-call(s32[2]{0:T(128)S(1)} %get-tuple-element.463.phone_ref, s32[2]{0:T(128)S(1)} %get-tuple-element.464.prompt_ref, s32[2]{0:T(128)S(1)} %fusion.5.target_ref, bf16[512,3072]{1,0:T(8,128)(2,1)S(1)} %get-tuple-element.349.q_ref.k_ref.v_ref, ...), custom_call_target="tpu_custom_call" | custom-call | flops 1048576 | bytes 1024 | tf_op jit(solution)/shard_map/attention_forward/pallas_call | solution.py:432
  128.4 2.7 attend.1
  139.3 7.9 %feed_first.1 = (bf16[512,2048]{1,0:T(8,128)(2,1)S(1)}, bf16[512,2048]{1,0:T(8,128)(2,1)S(1)}, bf16[1024,2048]{1,0:T(8,128)(2,1)S(1)}) custom-call(bf16[512,1024]{1,0:T(8,128)(2,1)} %get-tuple-element.339.n_ref.n0, f32[1,2048]{1,0:T(1,128)S(1)} %reshape.248.shift_ref, bf16[4,64,2048]{2,1,0:T(8,128)(2,1)} %constant_dynamic-update-slice_fusion.refs_0_, ...), custom_call_target="tpu_custom_call" | custom-call | flops 34359738368 | bytes 1024 | tf_op jit(solution)/shard_map/feed_first/pallas_call | solution.py:543
  147.3 6.3 %feed_second.1 = (bf16[512,2048]{1,0:T(8,128)(2,1)S(1)}, bf16[512,2048]{1,0:T(8,128)(2,1)S(1)}) custom-call(bf16[512,1024]{1,0:T(8,128)(2,1)} %collective-permute-done.20.n_ref.n1, bf16[1024,2048]{1,0:T(8,128)(2,1)S(1)} %get-tuple-element.320.w_ref, f32[1,2048]{1,0:T(1,128)S(1)} %reshape.248.shift_ref), custom_call_target="tpu_custom_call" | custom-call | flops 1048576 | bytes 1024 | tf_op jit(solution)/shard_map/feed_second/pallas_call | solution.py:543
  153.7 7.1 %down_grad.1 = (bf16[8,64,1024]{2,1,0:T(8,128)(2,1)S(1)}, bf16[8,64,1024]{2,1,0:T(8,128)(2,1)S(1)}, bf16[8,64,1024]{2,1,0:T(8,128)(2,1)S(1)}, bf16[8,64,1024]{2,1,0:T(8,128)(2,1)S(1)}) custom-call(bf16[512,2048]{1,0:T(8,128)(2,1)S(1)} %get-tuple-element.387.a0.a_ref, bf16[512,2048]{1,0:T(8,128)(2,1)S(1)} %get-tuple-element.385.a1.a_ref, ...), custom_call_target="tpu_custom_call" | custom-call | flops 1048576 | bytes 1024 | tf_op jit(solution)/shard_map/down_grad/pallas_call | solution.py:543
  162.5 13.6 %back_act.1 = (bf16[512,2048]{1,0:T(8,128)(2,1)S(1)}, bf16[512,2048]{1,0:T(8,128)(2,1)S(1)}, f32[1,2048]{1,0:T(1,128)S(1)}, bf16[2048,1024]{1,0:T(8,128)(2,1)S(1)}) custom-call(bf16[512,1024]{1,0:T(8,128)(2,1)} %maximum_select_fusion.1.c0.ct_ref, bf16[512,1024]{1,0:T(8,128)(2,1)} %collective-permute-done.19.c1, bf16[512,2048]{1,0:T(8,128)(2,1)S(1)} %get-tuple-element.307.s0, ...), custom_call_target="tpu_custom_call" | custom-call | flops 1048576 | bytes 1024 | tf_op jit(solution)/shard_map/back_act/pallas_call | solution.py:543
  176.2 2.4 back_up.2
  178.7 2.4 back_up.3.a_ref
  182.5 4.1 %back_norm.1 = (bf16[512,1024]{1,0:T(8,128)(2,1)S(1)}, bf16[512,1024]{1,0:T(8,128)(2,1)S(1)}, f32[512,1024]{1,0:T(8,128)S(1)}, f32[2,1024]{1,0:T(2,128)S(1)}) custom-call(f32[512,1024]{1,0:T(8,128)S(1)} %back_up.3.a_ref, bf16[512,1024]{1,0:T(8,128)(2,1)S(1)} %collective-permute-done.21.b_ref, f32[512,1024]{1,0:T(8,128)S(1)} %copy-done.13, ...), custom_call_target="tpu_custom_call" | custom-call | flops 1048576 | bytes 1024 | tf_op jit(solution)/shard_map/back_norm/pallas_call | solution.py:543
  187.9 2.3 out_grad.1
  198.9 8.3 %up_grad.1 = (bf16[4,80,2048]{2,1,0:T(8,128)(2,1)}, bf16[4,80,2048]{2,1,0:T(8,128)(2,1)S(1)}, bf16[4,80,2048]{2,1,0:T(8,128)(2,1)}, bf16[4,80,2048]{2,1,0:T(8,128)(2,1)S(1)}) custom-call(bf16[512,1024]{1,0:T(8,128)(2,1)} %get-tuple-element.339.n_ref.n0, bf16[512,1024]{1,0:T(8,128)(2,1)} %collective-permute-done.20.n_ref.n1, ...), custom_call_target="tpu_custom_call" | custom-call | flops 1048576 | bytes 1024 | tf_op jit(solution)/shard_map/up_grad/pallas_call | solution.py:543
  213.2 14.6 %attention_backward.1.g_ref = bf16[3,512,1024]{2,1,0:T(8,128)(2,1)S(1)} custom-call(s32[2]{0:T(128)S(1)} %get-tuple-element.463.phone_ref, s32[2]{0:T(128)S(1)} %get-tuple-element.464.prompt_ref, s32[2]{0:T(128)S(1)} %fusion.5.target_ref, bf16[512,3072]{1,0:T(8,128)(2,1)S(1)} %get-tuple-element.349.q_ref.k_ref.v_ref, ...), custom_call_target="tpu_custom_call" | custom-call | flops 1048576 | bytes 1024 | tf_op jit(solution)/shard_map/attention_backward/pallas_call | solution.py:511
  227.8 5.2 %attn_grad.1 = (bf16[16,32,3072]{2,1,0:T(8,128)(2,1)}, bf16[16,32,3072]{2,1,0:T(8,128)(2,1)S(1)}) custom-call(bf16[512,1024]{1,0:T(8,128)(2,1)S(1)} %copy-done.27, bf16[3,512,1024]{2,1,0:T(8,128)(2,1)S(1)} %attention_backward.1.g_ref), custom_call_target="tpu_custom_call" | custom-call | flops 1048576 | bytes 1024 | tf_op jit(solution)/shard_map/attn_grad/pallas_call | solution.py:543
  233.0 5.3 %back_first.1 = (bf16[256,1024]{1,0:T(8,128)(2,1)S(1)}, bf16[256,1024]{1,0:T(8,128)(2,1)}, f32[2,1024]{1,0:T(2,128)S(1)}) custom-call(bf16[3,512,1024]{2,1,0:T(8,128)(2,1)S(1)} %attention_backward.1.g_ref, bf16[1024,3072]{1,0:T(8,128)(2,1)S(1)} %bitcast.99, bf16[512,1024]{1,0:T(8,128)(2,1)S(1)} %copy-done.5, f32[8,1024]{1,0:T(8,128)S(1)} %get-tuple-element.359.vec_ref, ...), custom_call_target="tpu_custom_call" | custom-call | flops 1048576 | bytes 1024 | tf_op jit(solution)/shard_map/back_first/pallas_call | solution.py:543
  250.1 4.1 %core_sum.1 = (bf16[4,32,3200]{2,1,0:T(8,128)(2,1)}, bf16[4,32,3200]{2,1,0:T(8,128)(2,1)S(1)}, bf16[4,32,3200]{2,1,0:T(8,128)(2,1)}, bf16[4,32,3200]{2,1,0:T(8,128)(2,1)S(1)}) custom-call(bf16[16,32,3072]{2,1,0:T(8,128)(2,1)S(1)} %get-tuple-element.377.a_ref, bf16[16,32,3072]{2,1,0:T(8,128)(2,1)} %collective-permute-done.25.b_ref, ...), custom_call_target="tpu_custom_call" | custom-call | flops 1048576 | bytes 1024 | tf_op jit(solution)/shard_map/core_sum/pallas_call | solution.py:543
  255.1 7.6 %collective-permute-done.30.b_ref = bf16[2,80,2048]{2,1,0:T(8,128)(2,1)S(1)} collective-permute-done((bf16[2,80,2048]{2,1,0:T(8,128)(2,1)S(1)}, bf16[2,80,2048]{2,1,0:T(8,128)(2,1)S(1)}, u32[]{:S(2)}, u32[]{:S(2)}) %collective-permute-start.30) | collective-permute-done | bytes 655392 | tf_op jit(solution)/shard_map/ppermute | solution.py:34
  265.8 3.3 down_back.2
  269.2 2.3 down_back.3.a_ref
  272.8 9.6 %collective-permute-done.33.refs_5_.refs_7_ = bf16[4,32,3200]{2,1,0:T(8,128)(2,1)} collective-permute-done((bf16[4,32,3200]{2,1,0:T(8,128)(2,1)}, bf16[4,32,3200]{2,1,0:T(8,128)(2,1)}, u32[]{:S(2)}, u32[]{:S(2)}) %collective-permute-start.33) | collective-permute-done | bytes 819232 | tf_op jit(solution)/shard_map/ppermute | solution.py:34
  292.7 7.8 %collective-permute-done.34 = bf16[64,4224]{1,0:T(8,128)(2,1)S(1)} collective-permute-done((bf16[64,4224]{1,0:T(8,128)(2,1)S(1)}, bf16[64,4224]{1,0:T(8,128)(2,1)S(1)}, u32[]{:S(2)}, u32[]{:S(2)}) %collective-permute-start.34) | collective-permute-done | bytes 540704 | tf_op jit(solution)/shard_map/ppermute | solution.py:34
  312.2 12.0 %collective-permute-done.36 = bf16[256,1024]{1,0:T(8,128)(2,1)} collective-permute-done((bf16[256,1024]{1,0:T(8,128)(2,1)}, bf16[256,1024]{1,0:T(8,128)(2,1)}, u32[]{:S(2)}, u32[]{:S(2)}) %collective-permute-start.36) | collective-permute-done | bytes 524320 | tf_op jit(solution)/shard_map/ppermute | solution.py:32
  324.2 2.3 maximum_select_fusion.2
  326.6 2.7 fusion
  (296 shorter events, 116.7 us)
Async XLA Ops:
  7.2 68.0 %all-gather.5.cloned.1.call-start = ((), (), s32[]{:S(2)}) async-start(), calls=%async_computation.4 | async-start | bytes 1310720 | tf_op jit(solution)/shard_map/all_gather | solution.py:59
  13.8 26.3 %collective-permute-start.4 = (bf16[2,256,1024]{2,1,0:T(8,128)(2,1)}, bf16[2,256,1024]{2,1,0:T(8,128)(2,1)S(1)}, u32[]{:S(2)}, u32[]{:S(2)}) collective-permute-start(bf16[2,256,1024]{2,1,0:T(8,128)(2,1)} %pad_maximum_fusion.3), channel_id=1, source_target_pairs={{0,16},{16,0},{1,17},{17,1},{2,18},{18,2},{3,19},{19,3},{4,20},{20... | collective-permute-start | bytes 3145736 | tf_op jit(solution)/shard_map/ppermute | solution.py:32
  16.8 26.4 %collective-permute-start.1 = (bf16[1,32,4224]{2,1,0:T(8,128)(2,1)S(1)}, bf16[1,32,4224]{2,1,0:T(8,128)(2,1)S(1)}, u32[]{:S(2)}, u32[]{:S(2)}) collective-permute-start(bf16[1,32,4224]{2,1,0:T(8,128)(2,1)S(1)} %bitcast.106), channel_id=1, source_target_pairs={{0,4},{1,5},{2,6},{3,7},{4,0},{5,1},{6,2},{7,3},{8,12},{9,13},{10,... | collective-permute-start | bytes 811016 | tf_op jit(solution)/shard_map/ppermute | solution.py:34
  18.3 24.8 %collective-permute-start.2 = (bf16[1,32,4224]{2,1,0:T(8,128)(2,1)S(1)}, bf16[1,32,4224]{2,1,0:T(8,128)(2,1)S(1)}, u32[]{:S(2)}, u32[]{:S(2)}) collective-permute-start(bf16[1,32,4224]{2,1,0:T(8,128)(2,1)S(1)} %bitcast.107), channel_id=1, source_target_pairs={{0,8},{1,9},{2,10},{3,11},{4,12},{5,13},{6,14},{7,15},{8,0},{9,1},... | collective-permute-start | bytes 811016 | tf_op jit(solution)/shard_map/ppermute | solution.py:34
  20.9 22.2 %collective-permute-start.3 = (bf16[1,32,4224]{2,1,0:T(8,128)(2,1)S(1)}, bf16[1,32,4224]{2,1,0:T(8,128)(2,1)}, u32[]{:S(2)}, u32[]{:S(2)}) collective-permute-start(bf16[1,32,4224]{2,1,0:T(8,128)(2,1)S(1)} %bitcast.108), channel_id=1, source_target_pairs={{0,12},{1,13},{2,14},{3,15},{4,8},{5,9},{6,10},{7,11},{8,4},{9,5},... | collective-permute-start | bytes 811016 | tf_op jit(solution)/shard_map/ppermute | solution.py:34
  44.4 16.3 %collective-permute-start.5 = (bf16[64,5248]{1,0:T(8,128)(2,1)S(1)}, bf16[64,5248]{1,0:T(8,128)(2,1)S(1)}, u32[]{:S(2)}, u32[]{:S(2)}) collective-permute-start(bf16[64,5248]{1,0:T(8,128)(2,1)S(1)} %pad_maximum_fusion.4), channel_id=1, source_target_pairs={{0,2},{1,3},{2,0},{3,1},{4,6},{5,7},{6,4},{7,5},{8,10},{9,11},{10,... | collective-permute-start | bytes 2015240 | tf_op jit(solution)/shard_map/ppermute | solution.py:34
  47.7 87.0 %all-gather.7.cloned.1.call-start = ((), (), s32[]{:S(2)}) async-start(), calls=%async_computation.5 | async-start | bytes 2621440 | tf_op jit(solution)/shard_map/all_gather | solution.py:59
  62.8 23.7 %collective-permute-start.11 = (bf16[4,32,4224]{2,1,0:T(8,128)(2,1)S(1)}, bf16[4,32,4224]{2,1,0:T(8,128)(2,1)S(1)}, u32[]{:S(2)}, u32[]{:S(2)}) collective-permute-start(bf16[4,32,4224]{2,1,0:T(8,128)(2,1)S(1)} %pad_maximum_fusion.2.refs_2_), channel_id=1, source_target_pairs={{0,2},{1,3},{2,0},{3,1},{4,6},{5,7},{6,4},{7,5},{8,10},{9,11},{10,... | collective-permute-start | bytes 3244040 | tf_op jit(solution)/shard_map/ppermute | solution.py:34
  64.0 23.8 %collective-permute-start.9 = (bf16[4,32,4224]{2,1,0:T(8,128)(2,1)S(1)}, bf16[4,32,4224]{2,1,0:T(8,128)(2,1)}, u32[]{:S(2)}, u32[]{:S(2)}) collective-permute-start(bf16[4,32,4224]{2,1,0:T(8,128)(2,1)S(1)} %pad_maximum_fusion.1.refs_0_), channel_id=1, source_target_pairs={{0,16},{16,0},{1,17},{17,1},{2,18},{18,2},{3,19},{19,3},{4,20},{20... | collective-permute-start | bytes 3244040 | tf_op jit(solution)/shard_map/ppermute | solution.py:32
  67.4 20.8 %collective-permute-start.8 = (bf16[4,32,4224]{2,1,0:T(8,128)(2,1)S(1)}, bf16[4,32,4224]{2,1,0:T(8,128)(2,1)}, u32[]{:S(2)}, u32[]{:S(2)}) collective-permute-start(bf16[4,32,4224]{2,1,0:T(8,128)(2,1)S(1)} %pad_maximum_fusion.2.refs_2_), channel_id=1, source_target_pairs={{0,1},{1,0},{2,3},{3,2},{4,5},{5,4},{6,7},{7,6},{8,9},{9,8},{10,11... | collective-permute-start | bytes 3244040 | tf_op jit(solution)/shard_map/ppermute | solution.py:34
  67.5 20.7 %collective-permute-start.7 = (bf16[4,32,4224]{2,1,0:T(8,128)(2,1)S(1)}, bf16[4,32,4224]{2,1,0:T(8,128)(2,1)}, u32[]{:S(2)}, u32[]{:S(2)}) collective-permute-start(bf16[4,32,4224]{2,1,0:T(8,128)(2,1)S(1)} %pad_maximum_fusion.1.refs_0_), channel_id=1, source_target_pairs={{0,1},{1,0},{2,3},{3,2},{4,5},{5,4},{6,7},{7,6},{8,9},{9,8},{10,11... | collective-permute-start | bytes 3244040 | tf_op jit(solution)/shard_map/ppermute | solution.py:34
  87.9 195.6 %reduce-scatter.3.cloned.1.call-start = ((), (), s32[]{:S(2)}) async-start(), calls=%async_computation.2 | async-start | bytes 2621440 | tf_op jit(solution)/shard_map/reduce_scatter | solution.py:63
  107.6 27.0 %collective-permute-start.16 = (bf16[4,64,2048]{2,1,0:T(8,128)(2,1)}, bf16[4,64,2048]{2,1,0:T(8,128)(2,1)}, u32[]{:S(2)}, u32[]{:S(2)}) collective-permute-start(bf16[4,64,2048]{2,1,0:T(8,128)(2,1)} %constant_dynamic-update-slice_fusion.2.refs_2_), channel_id=1, source_target_pairs={{0,2},{1,3},{2,0},{3,1},{4,6},{5,7},{6,4},{7,5},{8,10},{9,11},{10,... | collective-permute-start | bytes 3145736 | tf_op jit(solution)/shard_map/ppermute | solution.py:34
  110.4 24.2 %collective-permute-start.15 = (bf16[4,64,2048]{2,1,0:T(8,128)(2,1)}, bf16[4,64,2048]{2,1,0:T(8,128)(2,1)}, u32[]{:S(2)}, u32[]{:S(2)}) collective-permute-start(bf16[4,64,2048]{2,1,0:T(8,128)(2,1)} %constant_dynamic-update-slice_fusion.refs_0_), channel_id=1, source_target_pairs={{0,16},{16,0},{1,17},{17,1},{2,18},{18,2},{3,19},{19,3},{4,20},{20... | collective-permute-start | bytes 3145736 | tf_op jit(solution)/shard_map/ppermute | solution.py:32
  112.0 41.7 %collective-permute-start.19 = (bf16[512,1024]{1,0:T(8,128)(2,1)}, bf16[512,1024]{1,0:T(8,128)(2,1)}, u32[]{:S(2)}, u32[]{:S(2)}) collective-permute-start(bf16[512,1024]{1,0:T(8,128)(2,1)} %maximum_select_fusion.1.c0.ct_ref), channel_id=1, source_target_pairs={{0,1},{1,0},{2,3},{3,2},{4,5},{5,4},{6,7},{7,6},{8,9},{9,8},{10,11... | collective-permute-start | bytes 3145736 | tf_op jit(solution)/shard_map/ppermute | solution.py:34
  136.4 25.6 %collective-permute-start.17 = (bf16[8,64,1024]{2,1,0:T(8,128)(2,1)S(1)}, bf16[8,64,1024]{2,1,0:T(8,128)(2,1)S(1)}, u32[]{:S(2)}, u32[]{:S(2)}) collective-permute-start(bf16[8,64,1024]{2,1,0:T(8,128)(2,1)S(1)} %bitcast.104), channel_id=1, source_target_pairs={{0,16},{16,0},{1,17},{17,1},{2,18},{18,2},{3,19},{19,3},{4,20},{20... | collective-permute-start | bytes 3145736 | tf_op jit(solution)/shard_map/ppermute | solution.py:32
  137.9 24.6 %collective-permute-start.18 = (bf16[8,64,1024]{2,1,0:T(8,128)(2,1)S(1)}, bf16[8,64,1024]{2,1,0:T(8,128)(2,1)S(1)}, u32[]{:S(2)}, u32[]{:S(2)}) collective-permute-start(bf16[8,64,1024]{2,1,0:T(8,128)(2,1)S(1)} %bitcast.102), channel_id=1, source_target_pairs={{0,2},{1,3},{2,0},{3,1},{4,6},{5,7},{6,4},{7,5},{8,10},{9,11},{10,... | collective-permute-start | bytes 3145736 | tf_op jit(solution)/shard_map/ppermute | solution.py:34
  160.8 30.9 %collective-permute-start.23 = (bf16[8,64,1024]{2,1,0:T(8,128)(2,1)S(1)}, bf16[8,64,1024]{2,1,0:T(8,128)(2,1)S(1)}, u32[]{:S(2)}, u32[]{:S(2)}) collective-permute-start(bf16[8,64,1024]{2,1,0:T(8,128)(2,1)S(1)} %get-tuple-element.301), channel_id=1, source_target_pairs={{0,16},{16,0},{1,17},{17,1},{2,18},{18,2},{3,19},{19,3},{4,20},{20... | collective-permute-start | bytes 3145736 | tf_op jit(solution)/shard_map/ppermute | solution.py:32
  161.7 30.0 %collective-permute-start.24 = (bf16[8,64,1024]{2,1,0:T(8,128)(2,1)S(1)}, bf16[8,64,1024]{2,1,0:T(8,128)(2,1)S(1)}, u32[]{:S(2)}, u32[]{:S(2)}) collective-permute-start(bf16[8,64,1024]{2,1,0:T(8,128)(2,1)S(1)} %get-tuple-element.303), channel_id=1, source_target_pairs={{0,2},{1,3},{2,0},{3,1},{4,6},{5,7},{6,4},{7,5},{8,10},{9,11},{10,... | collective-permute-start | bytes 3145736 | tf_op jit(solution)/shard_map/ppermute | solution.py:34
  209.3 31.4 %collective-permute-start.27 = (bf16[4,80,2048]{2,1,0:T(8,128)(2,1)}, bf16[4,80,2048]{2,1,0:T(8,128)(2,1)}, u32[]{:S(2)}, u32[]{:S(2)}) collective-permute-start(bf16[4,80,2048]{2,1,0:T(8,128)(2,1)} %get-tuple-element.345), channel_id=1, source_target_pairs={{0,16},{16,0},{1,17},{17,1},{2,18},{18,2},{3,19},{19,3},{4,20},{20... | collective-permute-start | bytes 3932168 | tf_op jit(solution)/shard_map/ppermute | solution.py:32
  210.3 30.9 %collective-permute-start.28 = (bf16[4,80,2048]{2,1,0:T(8,128)(2,1)}, bf16[4,80,2048]{2,1,0:T(8,128)(2,1)}, u32[]{:S(2)}, u32[]{:S(2)}) collective-permute-start(bf16[4,80,2048]{2,1,0:T(8,128)(2,1)} %get-tuple-element.347), channel_id=1, source_target_pairs={{0,2},{1,3},{2,0},{3,1},{4,6},{5,7},{6,4},{7,5},{8,10},{9,11},{10,... | collective-permute-start | bytes 3932168 | tf_op jit(solution)/shard_map/ppermute | solution.py:34
  211.7 92.2 %reduce-scatter.5.cloned.1.call-start = ((), (), s32[]{:S(2)}) async-start(), calls=%async_computation.3 | async-start | bytes 1638400 | tf_op jit(solution)/shard_map/reduce_scatter | solution.py:63
  233.0 17.1 %collective-permute-start.25 = (bf16[16,32,3072]{2,1,0:T(8,128)(2,1)}, bf16[16,32,3072]{2,1,0:T(8,128)(2,1)}, u32[]{:S(2)}, u32[]{:S(2)}) collective-permute-start(bf16[16,32,3072]{2,1,0:T(8,128)(2,1)} %get-tuple-element.355), channel_id=1, source_target_pairs={{0,1},{1,0},{2,3},{3,2},{4,5},{5,4},{6,7},{7,6},{8,9},{9,8},{10,11... | collective-permute-start | bytes 9437192 | tf_op jit(solution)/shard_map/ppermute | solution.py:34
  246.0 16.7 %collective-permute-start.30 = (bf16[2,80,2048]{2,1,0:T(8,128)(2,1)S(1)}, bf16[2,80,2048]{2,1,0:T(8,128)(2,1)S(1)}, u32[]{:S(2)}, u32[]{:S(2)}) collective-permute-start(bf16[2,80,2048]{2,1,0:T(8,128)(2,1)S(1)} %get-tuple-element.373), channel_id=1, source_target_pairs={{0,2},{1,3},{2,0},{3,1},{4,6},{5,7},{6,4},{7,5},{8,10},{9,11},{10,... | collective-permute-start | bytes 1966088 | tf_op jit(solution)/shard_map/ppermute | solution.py:34
  263.0 19.3 %collective-permute-start.33 = (bf16[4,32,3200]{2,1,0:T(8,128)(2,1)}, bf16[4,32,3200]{2,1,0:T(8,128)(2,1)}, u32[]{:S(2)}, u32[]{:S(2)}) collective-permute-start(bf16[4,32,3200]{2,1,0:T(8,128)(2,1)} %get-tuple-element.391), channel_id=1, source_target_pairs={{0,2},{1,3},{2,0},{3,1},{4,6},{5,7},{6,4},{7,5},{8,10},{9,11},{10,... | collective-permute-start | bytes 2457608 | tf_op jit(solution)/shard_map/ppermute | solution.py:34
  264.4 19.0 %collective-permute-start.32 = (bf16[4,32,3200]{2,1,0:T(8,128)(2,1)}, bf16[4,32,3200]{2,1,0:T(8,128)(2,1)}, u32[]{:S(2)}, u32[]{:S(2)}) collective-permute-start(bf16[4,32,3200]{2,1,0:T(8,128)(2,1)} %get-tuple-element.390), channel_id=1, source_target_pairs={{0,16},{16,0},{1,17},{17,1},{2,18},{18,2},{3,19},{19,3},{4,20},{20... | collective-permute-start | bytes 2457608 | tf_op jit(solution)/shard_map/ppermute | solution.py:32
  269.1 21.8 %collective-permute-start.29 = (bf16[512,1024]{1,0:T(8,128)(2,1)}, bf16[512,1024]{1,0:T(8,128)(2,1)S(1)}, u32[]{:S(2)}, u32[]{:S(2)}) collective-permute-start(bf16[512,1024]{1,0:T(8,128)(2,1)} %down_back.2), channel_id=1, source_target_pairs={{0,1},{1,0},{2,3},{3,2},{4,5},{5,4},{6,7},{7,6},{8,9},{9,8},{10,11... | collective-permute-start | bytes 3145736 | tf_op jit(solution)/shard_map/ppermute | solution.py:34
  301.9 24.7 %collective-permute-start.38 = (bf16[256,1024]{1,0:T(8,128)(2,1)}, bf16[256,1024]{1,0:T(8,128)(2,1)}, u32[]{:S(2)}, u32[]{:S(2)}) collective-permute-start(bf16[256,1024]{1,0:T(8,128)(2,1)} %get-tuple-element.424), channel_id=1, source_target_pairs={{0,16},{16,0},{1,17},{17,1},{2,18},{18,2},{3,19},{19,3},{4,20},{20... | collective-permute-start | bytes 1572872 | tf_op jit(solution)/shard_map/ppermute | solution.py:32
  303.6 20.6 %collective-permute-start.36 = (bf16[256,1024]{1,0:T(8,128)(2,1)}, bf16[256,1024]{1,0:T(8,128)(2,1)}, u32[]{:S(2)}, u32[]{:S(2)}) collective-permute-start(bf16[256,1024]{1,0:T(8,128)(2,1)} %get-tuple-element.411), channel_id=1, source_target_pairs={{0,16},{16,0},{1,17},{17,1},{2,18},{18,2},{3,19},{19,3},{4,20},{20... | collective-permute-start | bytes 1572872 | tf_op jit(solution)/shard_map/ppermute | solution.py:32
  305.2 24.1 %collective-permute-start.40 = (bf16[32,3200]{1,0:T(8,128)(2,1)S(1)}, bf16[32,3200]{1,0:T(8,128)(2,1)S(1)}, u32[]{:S(2)}, u32[]{:S(2)}) collective-permute-start(bf16[32,3200]{1,0:T(8,128)(2,1)S(1)} %get-tuple-element.454), channel_id=1, source_target_pairs={{0,8},{1,9},{2,10},{3,11},{4,12},{5,13},{6,14},{7,15},{8,0},{9,1},... | collective-permute-start | bytes 614408 | tf_op jit(solution)/shard_map/ppermute | solution.py:34
  307.2 22.1 %collective-permute-start.41 = (bf16[32,3200]{1,0:T(8,128)(2,1)S(1)}, bf16[32,3200]{1,0:T(8,128)(2,1)S(1)}, u32[]{:S(2)}, u32[]{:S(2)}) collective-permute-start(bf16[32,3200]{1,0:T(8,128)(2,1)S(1)} %get-tuple-element.453), channel_id=1, source_target_pairs={{0,12},{1,13},{2,14},{3,15},{4,8},{5,9},{6,10},{7,11},{8,4},{9,5},... | collective-permute-start | bytes 614408 | tf_op jit(solution)/shard_map/ppermute | solution.py:34
  311.1 18.2 %collective-permute-start.39 = (bf16[32,3200]{1,0:T(8,128)(2,1)S(1)}, bf16[32,3200]{1,0:T(8,128)(2,1)S(1)}, u32[]{:S(2)}, u32[]{:S(2)}) collective-permute-start(bf16[32,3200]{1,0:T(8,128)(2,1)S(1)} %get-tuple-element.448), channel_id=1, source_target_pairs={{0,4},{1,5},{2,6},{3,7},{4,0},{5,1},{6,2},{7,3},{8,12},{9,13},{10,... | collective-permute-start | bytes 614408 | tf_op jit(solution)/shard_map/ppermute | solution.py:34
  (82 other events, 589.1 us)
Sparse Core Ops, SparseCore 0:
  47.8 27.2 all-gather.4
  88.0 46.6 all-gather.6
  211.8 43.1 reduce-scatter.2
  272.9 30.8 reduce-scatter.4

commit v4 on v3

--- a/solution.py
+++ b/solution.py
@@ -63,6 +63,30 @@
     return lax.psum_scatter(column, "rows", scatter_dimension=0, axis_index_groups=z_groups())
 
 
+def join_planes(left, left_in, right, right_in):
+    half, rows, cols = left.shape
+
+    def kernel(a_ref, b_ref, c_ref, d_ref, left_ref, right_ref):
+        left_ref[0] = a_ref[0]
+        left_ref[1] = b_ref[0]
+        right_ref[0] = c_ref[0]
+        right_ref[1] = d_ref[0]
+
+    part = pl.BlockSpec((1, rows, cols), lambda i: (i, 0, 0))
+    both = pl.BlockSpec((2, None, rows, cols), lambda i: (0, i, 0, 0))
+    made = pl.pallas_call(
+        kernel,
+        grid=(half,),
+        out_shape=[jax.ShapeDtypeStruct((2, half, rows, cols), BF)] * 2,
+        in_specs=[part] * 4,
+        out_specs=[both] * 2,
+        compiler_params=pltpu.CompilerParams(vmem_limit_bytes=16 << 20),
+        cost_estimate=pl.CostEstimate(flops=1 << 20, bytes_accessed=1 << 10, transcendentals=0),
+        name="join_planes",
+    )(left, left_in, right, right_in)
+    return [v.reshape(2 * half, rows, cols) for v in made]
+
+
 class Gather:
     def __init__(self, chain, by_permutes):
         self.chain = chain
@@ -106,7 +130,7 @@
             left, right = halves
             left_x, right_y = sides
             if not extras:
-                return jnp.concatenate([left, left_x], 0), jnp.concatenate([right, right_y], 0)
+                return join_planes(left, left_x, right, right_y)
             main = [v[:, :cols].reshape(block) for v in (left, left_x, right, right_y)]
             more = [v[:, cols:].reshape(extras) for v in (left, left_x, right, right_y)]
             return (
@@ -773,38 +797,27 @@
     size = wide // chips
     arrays = [p[0] for p in pieces]
     half = size // 2
-    wave = chips // 2
 
     def kernel(c0, c1, s0, s1, *refs):
-        ins, (g0, g1, sum_ref, w_ref, sems) = refs[: len(arrays)], refs[len(arrays) :]
+        ins, (g0, g1, sum_ref, w_ref) = refs[: len(arrays)], refs[len(arrays) :]
         where = position()
-
-        def copy_of(n, i):
-            name = pieces[n][1][i]
-            row = pl.multiple_of(chip_slot(name, where, False) * size + (n // 2) * half, half)
-            return pltpu.make_async_copy(
-                ins[n].at[i], w_ref.at[pl.ds(row, half), :], sems.at[n * wave + i]
-            )
-
-        waves = [[], []]
-        for n in range(4):
-            for i, (jy, _, _) in enumerate(pieces[n][1]):
-                waves[jy].append(copy_of(n, i))
-        for copy in waves[0] + waves[1]:
-            copy.start()
-        for jy in range(2):
-            for copy in waves[jy]:
-                copy.wait()
-            for j in range(0, wave * size, 256):
-                start = pl.multiple_of((where[0] ^ jy) * (wave * size) + j, 256)
-                at = pl.ds(start, 256)
-                sums = 0.0
-                for ct, slope, out in ((c0, s0, g0), (c1, s1, g1)):
-                    grad = bdot(ct[...], w_ref[at, :], NT) * slope[:, at].astype(F32)
-                    grad = grad.astype(BF)
-                    sums = sums + jnp.sum(grad.astype(F32), 0, keepdims=True)
-                    out[:, at] = grad
-                sum_ref[:, at] = sums
+        for z in range(depth()):
+            for jy in range(2):
+                for n, (_, names) in enumerate(pieces):
+                    for i, name in enumerate(names):
+                        if name[:2] == (jy, z):
+                            slot = chip_slot(name, where, False)
+                            row = pl.multiple_of(slot * size + (n // 2) * half, half)
+                            w_ref[pl.ds(row, half), :] = ins[n][i]
+        for j in range(chips // 2):
+            at = slice(j * 2 * size, (j + 1) * 2 * size)
+            sums = 0.0
+            for ct, slope, out in ((c0, s0, g0), (c1, s1, g1)):
+                grad = bdot(ct[...], w_ref[at, :], NT) * slope[:, at].astype(F32)
+                grad = grad.astype(BF)
+                sums = sums + jnp.sum(grad.astype(F32), 0, keepdims=True)
+                out[:, at] = grad
+            sum_ref[:, at] = sums
 
     part = shape_of((2 * ROW, wide))
     return call(
@@ -812,8 +825,6 @@
         kernel,
         [part, part, shape_of((1, wide), F32), shape_of((wide, D))],
         (*cts, *slopes, *arrays),
-        [VMEM] * 4 + [ANY] * 4,
-        [pltpu.SemaphoreType.DMA((4 * wave,))],
     )
 
 
@@ -995,6 +1006,38 @@
     return call("result_of", kernel, [shape_of((ROW, D))] * 2, (own, other))
 
 
+def home(out_own, out_other, grad_own, grad_other):
+    lines = ROW // 2
+
+    def kernel(a_ref, b_ref, c_ref, d_ref, out_ref, grad_ref):
+        mine = pl.program_id(1) == position()[0]
+
+        @pl.when(mine)
+        def _():
+            out_ref[0] = a_ref[...]
+            grad_ref[0] = c_ref[...].astype(F32)
+
+        @pl.when(jnp.logical_not(mine))
+        def _():
+            out_ref[0] = b_ref[...]
+            grad_ref[0] = d_ref[...].astype(F32)
+
+    part = pl.BlockSpec((lines, D), lambda i, m: (i, 0))
+    return pl.pallas_call(
+        kernel,
+        grid=(2, MICRO),
+        out_shape=[
+            jax.ShapeDtypeStruct((MICRO, ROW, D), BF),
+            jax.ShapeDtypeStruct((MICRO, ROW, D), F32),
+        ],
+        in_specs=[part] * 4,
+        out_specs=[pl.BlockSpec((1, lines, D), lambda i, m: (m, i, 0))] * 2,
+        compiler_params=pltpu.CompilerParams(vmem_limit_bytes=16 << 20),
+        cost_estimate=pl.CostEstimate(flops=1 << 20, bytes_accessed=1 << 10, transcendentals=0),
+        name="home",
+    )(out_own, out_other, grad_own, grad_other)
+
+
 def interleave(own, other):
     rows, wide = own.shape
     size = wide // (4 * depth())
@@ -1194,12 +1237,9 @@
 
     sum_down = chain(sum_of_down, down_sz, *attn_stwo)
 
-    def home(own, other):
-        return ordered(y, own[None], other[None], 0).reshape(MICRO, 1, 1, ROW, D)
-
     up_final = chain(interleave, up_mine, up_theirs)
-    out_stack = chain(home, res_own, out_other)
-    grad_stack = chain(lambda own, other: home(own, other).astype(F32), gx_own, gx_other)
+    out_stack, grad_stack = chain(home, res_own, out_other, gx_own, gx_other)
+    out_stack, grad_stack = (v.reshape(MICRO, 1, 1, ROW, D) for v in (out_stack, grad_stack))
     sum_attn = attn_s.total(attn_sz)
     small_sum = sum_attn[:, 3 * D : 3 * D + lines].T.reshape(-1)
     edges = [i * row_w for i in range(5)]

time: 344 us -> 331 us (0.962)
  local copies, waits for them, and re-layouts: 50 us -> 43.9 us
  other arithmetic: 17.5 us -> 12.1 us
    pallas_call x20, Pallas kernels: 87.7 us -> 80.9 us  [call(): pl.pallas_call(kernel, out_shape=outs, in_specs=[VMEM] * len(args) if spe...]
    pallas_call x0 -> x2, Pallas kernels: none -> 3.58 us  [the longest x1 2.17 us: home(): pl.pallas_call(kernel, grid=(2, MICRO), out_shape=[jax.ShapeDtypeStruct((...]
    unnamed x136 -> x132, local copies, waits for them, and re-layouts: 28.6 us -> 26.1 us
  transfers between devices with their start and end apart: 46 -> 46, of which waited for: 22 -> 26; matrix products, arithmetic and copies ran while one was open for 10% -> 7% of each run, Pallas kernels for 34% -> 34%
where the time goes in v4:
time: 331 us; the launch traced here: 325 us
  Pallas kernels  121 us (37%)
  waiting for transfers between devices  93.5 us (28%)
  local copies, waits for them, and re-layouts  43.9 us (13%)
  starting transfers between devices  40.1 us (12%)
  between operations  14.9 us (5%)
  other arithmetic  12.1 us (4%)
    pallas_call x20, Pallas kernels, call(): pl.pallas_call(kernel, out_shape=outs, in_specs=[VMEM] * len(args) if spe...  80.9 us
    ppermute x29, waiting for transfers between devices, swap(): return lax.ppermute(block, 'rows', [(i, i ^ way) for i in range(count)])  55.7 us
    ppermute x13, waiting for transfers between devices, swap(): return lax.ppermute(block, 'pair', [(i, i ^ 1) for i in range(2)])  31.6 us
    unnamed x132, local copies, waits for them, and re-layouts  26.1 us
    ppermute x29, starting transfers between devices, swap(): return lax.ppermute(block, 'rows', [(i, i ^ way) for i in range(count)])  20.8 us
    ppermute x13, starting transfers between devices, swap(): return lax.ppermute(block, 'pair', [(i, i ^ 1) for i in range(2)])  18.9 us
    pallas_call x1, Pallas kernels, attention_forward(): pl.pallas_call(kernel, grid=(steps,), out_shape=[jax.ShapeDtypeStruct((2...  15.9 us
    pallas_call x1, Pallas kernels, attention_backward(): pl.pallas_call(kernel, grid=(steps,), out_shape=jax.ShapeDtypeStruct((3,...  15 us
  transfers between devices with their start and end apart: 46, of which 26 were waited for; matrix products, arithmetic and copies ran while one was open for 7% of the time, Pallas kernels for 34%

profile of v4, /device:TPU:0, one launch (start us, length us, event | category | flops | bytes accessed | tf_op | source)
XLA Modules:
  0.0 324.9 jit_solution(10322443046114574314)
XLA Ops:
  13.8 3.0 collective-permute-start.4
  18.4 2.6 collective-permute-start.2
  25.9 14.3 %collective-permute-done.4 = bf16[2,256,1024]{2,1,0:T(8,128)(2,1)S(1)} collective-permute-done((bf16[2,256,1024]{2,1,0:T(8,128)(2,1)}, bf16[2,256,1024]{2,1,0:T(8,128)(2,1)S(1)}, u32[]{:S(2)}, u32[]{:S(2)}) %collective-permute-start.4) | collective-permute-done | bytes 1048608 | tf_op jit(solution)/shard_map/ppermute | solution.py:32
  47.8 13.0 %collective-permute-done.5 = bf16[64,5248]{1,0:T(8,128)(2,1)S(1)} collective-permute-done((bf16[64,5248]{1,0:T(8,128)(2,1)S(1)}, bf16[64,5248]{1,0:T(8,128)(2,1)S(1)}, u32[]{:S(2)}, u32[]{:S(2)}) %collective-permute-start.5) | collective-permute-done | bytes 671776 | tf_op jit(solution)/shard_map/ppermute | solution.py:34
  69.3 5.9 %all-gather.5.cloned.1.call-done = bf16[256,2048]{1,0:T(8,128)(2,1)} async-done(((bf16[64,2048]{1,0:T(8,128)(2,1)}), bf16[256,2048]{1,0:T(8,128)(2,1)}) %all-gather.5.cloned.1.call-update) | async-done | bytes 1048592 | tf_op jit(solution)/shard_map/all_gather | solution.py:59
  77.5 9.1 %collective-permute-done.11.refs_3_ = bf16[4,32,4224]{2,1,0:T(8,128)(2,1)S(1)} collective-permute-done((bf16[4,32,4224]{2,1,0:T(8,128)(2,1)S(1)}, bf16[4,32,4224]{2,1,0:T(8,128)(2,1)S(1)}, u32[]{:S(2)}, u32[]{:S(2)}) %collective-permute-start.11) | collective-permute-done | bytes 1081376 | tf_op jit(solution)/shard_map/ppermute | solution.py:34
  93.3 4.2 %unpack.1 = (bf16[16,2,32,3072]{3,2,1,0:T(8,128)(2,1)S(1)}, bf16[16,2,32,1024]{3,2,1,0:T(8,128)(2,1)S(1)}, f32[8,1024]{1,0:T(8,128)S(1)}) custom-call(bf16[4,32,4224]{2,1,0:T(8,128)(2,1)S(1)} %pad_maximum_fusion.1.refs_0_, bf16[4,32,4224]{2,1,0:T(8,128)(2,1)} %collective-permute-done.9.refs_1_, bf16[4,32,4224]{2,1,0:T(8,128)(2,1)S(1)} %pad_maximum_fusion.2.refs_2_, ...), custom_call_target="tpu_custom_call" | custom-call | flops 1048576 | bytes 1024 | tf_op jit(solution)/shard_map/unpack/pallas_call | solution.py:567
  98.9 3.9 %project.1 = (bf16[512,1024]{1,0:T(8,128)(2,1)S(1)}, bf16[512,3072]{1,0:T(8,128)(2,1)S(1)}) custom-call(bf16[512,1024]{1,0:T(8,128)(2,1)S(1)} %copy-done.3, f32[8,1024]{1,0:T(8,128)S(1)} %get-tuple-element.365.vec_ref, bf16[1024,3072]{1,0:T(8,128)(2,1)S(1)} %bitcast.100), custom_call_target="tpu_custom_call" | custom-call | flops 1048576 | bytes 1024 | tf_op jit(solution)/shard_map/project/pallas_call | solution.py:567
  110.1 15.9 %attention_forward.1 = (bf16[512,1024]{1,0:T(8,128)(2,1)S(1)}, f32[4,4,512]{2,1,0:T(4,128)S(1)}) custom-call(s32[2]{0:T(128)S(1)} %get-tuple-element.504.phone_ref, s32[2]{0:T(128)S(1)} %get-tuple-element.505.prompt_ref, s32[2]{0:T(128)S(1)} %fusion.4.target_ref, bf16[512,3072]{1,0:T(8,128)(2,1)S(1)} %get-tuple-element.355.q_ref.k_ref.v_ref, ...), custom_call_target="tpu_custom_call" | custom-call | flops 1048576 | bytes 1024 | tf_op jit(solution)/shard_map/attention_forward/pallas_call | solution.py:456
  126.1 2.7 attend.1
  136.1 7.9 %feed_first.1 = (bf16[512,2048]{1,0:T(8,128)(2,1)S(1)}, bf16[512,2048]{1,0:T(8,128)(2,1)S(1)}, bf16[1024,2048]{1,0:T(8,128)(2,1)S(1)}) custom-call(bf16[512,1024]{1,0:T(8,128)(2,1)} %get-tuple-element.345.n_ref.n0, f32[1,2048]{1,0:T(1,128)S(1)} %reshape.138.shift_ref, bf16[4,64,2048]{2,1,0:T(8,128)(2,1)} %bitcast.25.refs_0_, ...), custom_call_target="tpu_custom_call" | custom-call | flops 34359738368 | bytes 1024 | tf_op jit(solution)/shard_map/feed_first/pallas_call | solution.py:567
  144.1 6.3 %feed_second.1 = (bf16[512,2048]{1,0:T(8,128)(2,1)S(1)}, bf16[512,2048]{1,0:T(8,128)(2,1)S(1)}) custom-call(bf16[512,1024]{1,0:T(8,128)(2,1)} %collective-permute-done.20.n_ref.n1, bf16[1024,2048]{1,0:T(8,128)(2,1)S(1)} %get-tuple-element.326.w_ref, f32[1,2048]{1,0:T(1,128)S(1)} %reshape.138.shift_ref), custom_call_target="tpu_custom_call" | custom-call | flops 1048576 | bytes 1024 | tf_op jit(solution)/shard_map/feed_second/pallas_call | solution.py:567
  150.5 7.1 %down_grad.1 = (bf16[8,64,1024]{2,1,0:T(8,128)(2,1)S(1)}, bf16[8,64,1024]{2,1,0:T(8,128)(2,1)S(1)}, bf16[8,64,1024]{2,1,0:T(8,128)(2,1)S(1)}, bf16[8,64,1024]{2,1,0:T(8,128)(2,1)S(1)}) custom-call(bf16[512,2048]{1,0:T(8,128)(2,1)S(1)} %get-tuple-element.393.a0.a_ref, bf16[512,2048]{1,0:T(8,128)(2,1)S(1)} %get-tuple-element.391.a1.a_ref, ...), custom_call_target="tpu_custom_call" | custom-call | flops 1048576 | bytes 1024 | tf_op jit(solution)/shard_map/down_grad/pallas_call | solution.py:567
  159.9 6.9 %back_act.1 = (bf16[512,2048]{1,0:T(8,128)(2,1)S(1)}, bf16[512,2048]{1,0:T(8,128)(2,1)S(1)}, f32[1,2048]{1,0:T(1,128)S(1)}, bf16[2048,1024]{1,0:T(8,128)(2,1)S(1)}) custom-call(bf16[512,1024]{1,0:T(8,128)(2,1)} %maximum_select_fusion.1.c0.ct_ref, bf16[512,1024]{1,0:T(8,128)(2,1)} %collective-permute-done.19.c1, bf16[512,2048]{1,0:T(8,128)(2,1)S(1)} %get-tuple-element.313.s0, ...), custom_call_target="tpu_custom_call" | custom-call | flops 1048576 | bytes 1024 | tf_op jit(solution)/shard_map/back_act/pallas_call | solution.py:567
  166.8 2.4 back_up.2
  169.4 2.4 back_up.3.a_ref
  173.1 4.3 %back_norm.1 = (bf16[512,1024]{1,0:T(8,128)(2,1)S(1)}, bf16[512,1024]{1,0:T(8,128)(2,1)S(1)}, f32[512,1024]{1,0:T(8,128)S(1)}, f32[2,1024]{1,0:T(2,128)S(1)}) custom-call(f32[512,1024]{1,0:T(8,128)S(1)} %back_up.3.a_ref, bf16[512,1024]{1,0:T(8,128)(2,1)S(1)} %collective-permute-done.21.b_ref, f32[512,1024]{1,0:T(8,128)S(1)} %copy-done.13, ...), custom_call_target="tpu_custom_call" | custom-call | flops 1048576 | bytes 1024 | tf_op jit(solution)/shard_map/back_norm/pallas_call | solution.py:567
  178.7 2.3 out_grad.1
  189.6 8.3 %up_grad.1 = (bf16[4,80,2048]{2,1,0:T(8,128)(2,1)}, bf16[4,80,2048]{2,1,0:T(8,128)(2,1)S(1)}, bf16[4,80,2048]{2,1,0:T(8,128)(2,1)}, bf16[4,80,2048]{2,1,0:T(8,128)(2,1)S(1)}) custom-call(bf16[512,1024]{1,0:T(8,128)(2,1)} %get-tuple-element.345.n_ref.n0, bf16[512,1024]{1,0:T(8,128)(2,1)} %collective-permute-done.20.n_ref.n1, ...), custom_call_target="tpu_custom_call" | custom-call | flops 1048576 | bytes 1024 | tf_op jit(solution)/shard_map/up_grad/pallas_call | solution.py:567
  203.2 15.0 %attention_backward.1.g_ref = bf16[3,512,1024]{2,1,0:T(8,128)(2,1)S(1)} custom-call(s32[2]{0:T(128)S(1)} %get-tuple-element.504.phone_ref, s32[2]{0:T(128)S(1)} %get-tuple-element.505.prompt_ref, s32[2]{0:T(128)S(1)} %fusion.4.target_ref, bf16[512,3072]{1,0:T(8,128)(2,1)S(1)} %get-tuple-element.355.q_ref.k_ref.v_ref, ...), custom_call_target="tpu_custom_call" | custom-call | flops 1048576 | bytes 1024 | tf_op jit(solution)/shard_map/attention_backward/pallas_call | solution.py:535
  218.3 5.2 %attn_grad.1 = (bf16[16,32,3072]{2,1,0:T(8,128)(2,1)}, bf16[16,32,3072]{2,1,0:T(8,128)(2,1)S(1)}) custom-call(bf16[512,1024]{1,0:T(8,128)(2,1)S(1)} %copy-done.27, bf16[3,512,1024]{2,1,0:T(8,128)(2,1)S(1)} %attention_backward.1.g_ref), custom_call_target="tpu_custom_call" | custom-call | flops 1048576 | bytes 1024 | tf_op jit(solution)/shard_map/attn_grad/pallas_call | solution.py:567
  223.5 5.3 %back_first.1 = (bf16[256,1024]{1,0:T(8,128)(2,1)S(1)}, bf16[256,1024]{1,0:T(8,128)(2,1)}, f32[2,1024]{1,0:T(2,128)S(1)}) custom-call(bf16[3,512,1024]{2,1,0:T(8,128)(2,1)S(1)} %attention_backward.1.g_ref, bf16[1024,3072]{1,0:T(8,128)(2,1)S(1)} %bitcast.103, bf16[512,1024]{1,0:T(8,128)(2,1)S(1)} %copy-done.5, f32[8,1024]{1,0:T(8,128)S(1)} %get-tuple-element.365.vec_ref, ...), custom_call_target="tpu_custom_call" | custom-call | flops 1048576 | bytes 1024 | tf_op jit(solution)/shard_map/back_first/pallas_call | solution.py:567
  240.5 4.1 %core_sum.1 = (bf16[4,32,3200]{2,1,0:T(8,128)(2,1)}, bf16[4,32,3200]{2,1,0:T(8,128)(2,1)S(1)}, bf16[4,32,3200]{2,1,0:T(8,128)(2,1)}, bf16[4,32,3200]{2,1,0:T(8,128)(2,1)S(1)}) custom-call(bf16[16,32,3072]{2,1,0:T(8,128)(2,1)S(1)} %get-tuple-element.383.a_ref, bf16[16,32,3072]{2,1,0:T(8,128)(2,1)} %collective-permute-done.25.b_ref, ...), custom_call_target="tpu_custom_call" | custom-call | flops 1048576 | bytes 1024 | tf_op jit(solution)/shard_map/core_sum/pallas_call | solution.py:567
  245.5 7.7 %collective-permute-done.30.b_ref = bf16[2,80,2048]{2,1,0:T(8,128)(2,1)S(1)} collective-permute-done((bf16[2,80,2048]{2,1,0:T(8,128)(2,1)S(1)}, bf16[2,80,2048]{2,1,0:T(8,128)(2,1)S(1)}, u32[]{:S(2)}, u32[]{:S(2)}) %collective-permute-start.30) | collective-permute-done | bytes 655392 | tf_op jit(solution)/shard_map/ppermute | solution.py:34
  256.5 3.3 %down_back.2 = bf16[512,1024]{1,0:T(8,128)(2,1)} custom-call(bf16[512,2048]{1,0:T(8,128)(2,1)S(1)} %copy-done.11, bf16[2048,1024]{1,0:T(8,128)(2,1)S(1)} %copy-done.7), custom_call_target="tpu_custom_call" | custom-call | flops 1048576 | bytes 1024 | tf_op jit(solution)/shard_map/down_back/pallas_call | solution.py:567
  259.8 2.3 down_back.3.a_ref
  263.4 9.5 %collective-permute-done.33.refs_5_.refs_7_ = bf16[4,32,3200]{2,1,0:T(8,128)(2,1)} collective-permute-done((bf16[4,32,3200]{2,1,0:T(8,128)(2,1)}, bf16[4,32,3200]{2,1,0:T(8,128)(2,1)}, u32[]{:S(2)}, u32[]{:S(2)}) %collective-permute-start.33) | collective-permute-done | bytes 819232 | tf_op jit(solution)/shard_map/ppermute | solution.py:34
  283.1 7.7 %collective-permute-done.34 = bf16[64,4224]{1,0:T(8,128)(2,1)S(1)} collective-permute-done((bf16[64,4224]{1,0:T(8,128)(2,1)S(1)}, bf16[64,4224]{1,0:T(8,128)(2,1)S(1)}, u32[]{:S(2)}, u32[]{:S(2)}) %collective-permute-start.34) | collective-permute-done | bytes 540704 | tf_op jit(solution)/shard_map/ppermute | solution.py:34
  296.7 2.5 collective-permute-start.40
  303.2 3.5 %collective-permute-done.37.d_ref = bf16[256,1024]{1,0:T(8,128)(2,1)S(1)} collective-permute-done((bf16[256,1024]{1,0:T(8,128)(2,1)}, bf16[256,1024]{1,0:T(8,128)(2,1)S(1)}, u32[]{:S(2)}, u32[]{:S(2)}) %collective-permute-start.37) | collective-permute-done | bytes 524320 | tf_op jit(solution)/shard_map/ppermute | solution.py:32
  306.7 6.9 %collective-permute-done.36.b_ref = bf16[256,1024]{1,0:T(8,128)(2,1)S(1)} collective-permute-done((bf16[256,1024]{1,0:T(8,128)(2,1)}, bf16[256,1024]{1,0:T(8,128)(2,1)S(1)}, u32[]{:S(2)}, u32[]{:S(2)}) %collective-permute-start.36) | collective-permute-done | bytes 524320 | tf_op jit(solution)/shard_map/ppermute | solution.py:32
  313.7 2.2 home.1
  (290 shorter events, 112.4 us)
Async XLA Ops:
  7.2 68.0 %all-gather.5.cloned.1.call-start = ((), (), s32[]{:S(2)}) async-start(), calls=%async_computation.4 | async-start | bytes 1310720 | tf_op jit(solution)/shard_map/all_gather | solution.py:59
  13.8 26.3 %collective-permute-start.4 = (bf16[2,256,1024]{2,1,0:T(8,128)(2,1)}, bf16[2,256,1024]{2,1,0:T(8,128)(2,1)S(1)}, u32[]{:S(2)}, u32[]{:S(2)}) collective-permute-start(bf16[2,256,1024]{2,1,0:T(8,128)(2,1)} %pad_maximum_fusion.3), channel_id=1, source_target_pairs={{0,16},{16,0},{1,17},{17,1},{2,18},{18,2},{3,19},{19,3},{4,20},{20... | collective-permute-start | bytes 3145736 | tf_op jit(solution)/shard_map/ppermute | solution.py:32
  16.8 26.4 %collective-permute-start.1 = (bf16[1,32,4224]{2,1,0:T(8,128)(2,1)S(1)}, bf16[1,32,4224]{2,1,0:T(8,128)(2,1)S(1)}, u32[]{:S(2)}, u32[]{:S(2)}) collective-permute-start(bf16[1,32,4224]{2,1,0:T(8,128)(2,1)S(1)} %bitcast.110), channel_id=1, source_target_pairs={{0,4},{1,5},{2,6},{3,7},{4,0},{5,1},{6,2},{7,3},{8,12},{9,13},{10,... | collective-permute-start | bytes 811016 | tf_op jit(solution)/shard_map/ppermute | solution.py:34
  18.4 24.9 %collective-permute-start.2 = (bf16[1,32,4224]{2,1,0:T(8,128)(2,1)S(1)}, bf16[1,32,4224]{2,1,0:T(8,128)(2,1)S(1)}, u32[]{:S(2)}, u32[]{:S(2)}) collective-permute-start(bf16[1,32,4224]{2,1,0:T(8,128)(2,1)S(1)} %bitcast.111), channel_id=1, source_target_pairs={{0,8},{1,9},{2,10},{3,11},{4,12},{5,13},{6,14},{7,15},{8,0},{9,1},... | collective-permute-start | bytes 811016 | tf_op jit(solution)/shard_map/ppermute | solution.py:34
  20.9 22.3 %collective-permute-start.3 = (bf16[1,32,4224]{2,1,0:T(8,128)(2,1)S(1)}, bf16[1,32,4224]{2,1,0:T(8,128)(2,1)}, u32[]{:S(2)}, u32[]{:S(2)}) collective-permute-start(bf16[1,32,4224]{2,1,0:T(8,128)(2,1)S(1)} %bitcast.112), channel_id=1, source_target_pairs={{0,12},{1,13},{2,14},{3,15},{4,8},{5,9},{6,10},{7,11},{8,4},{9,5},... | collective-permute-start | bytes 811016 | tf_op jit(solution)/shard_map/ppermute | solution.py:34
  44.4 16.3 %collective-permute-start.5 = (bf16[64,5248]{1,0:T(8,128)(2,1)S(1)}, bf16[64,5248]{1,0:T(8,128)(2,1)S(1)}, u32[]{:S(2)}, u32[]{:S(2)}) collective-permute-start(bf16[64,5248]{1,0:T(8,128)(2,1)S(1)} %pad_maximum_fusion.4), channel_id=1, source_target_pairs={{0,2},{1,3},{2,0},{3,1},{4,6},{5,7},{6,4},{7,5},{8,10},{9,11},{10,... | collective-permute-start | bytes 2015240 | tf_op jit(solution)/shard_map/ppermute | solution.py:34
  46.2 15.7 %collective-permute-start.6 = (bf16[64,5248]{1,0:T(8,128)(2,1)S(1)}, bf16[64,5248]{1,0:T(8,128)(2,1)S(1)}, u32[]{:S(2)}, u32[]{:S(2)}) collective-permute-start(bf16[64,5248]{1,0:T(8,128)(2,1)S(1)} %pad_maximum_fusion.5), channel_id=1, source_target_pairs={{0,16},{16,0},{1,17},{17,1},{2,18},{18,2},{3,19},{19,3},{4,20},{20... | collective-permute-start | bytes 2015240 | tf_op jit(solution)/shard_map/ppermute | solution.py:32
  47.8 82.8 %all-gather.7.cloned.1.call-start = ((), (), s32[]{:S(2)}) async-start(), calls=%async_computation.5 | async-start | bytes 2621440 | tf_op jit(solution)/shard_map/all_gather | solution.py:59
  62.9 23.7 %collective-permute-start.11 = (bf16[4,32,4224]{2,1,0:T(8,128)(2,1)S(1)}, bf16[4,32,4224]{2,1,0:T(8,128)(2,1)S(1)}, u32[]{:S(2)}, u32[]{:S(2)}) collective-permute-start(bf16[4,32,4224]{2,1,0:T(8,128)(2,1)S(1)} %pad_maximum_fusion.2.refs_2_), channel_id=1, source_target_pairs={{0,2},{1,3},{2,0},{3,1},{4,6},{5,7},{6,4},{7,5},{8,10},{9,11},{10,... | collective-permute-start | bytes 3244040 | tf_op jit(solution)/shard_map/ppermute | solution.py:34
  64.1 23.8 %collective-permute-start.9 = (bf16[4,32,4224]{2,1,0:T(8,128)(2,1)S(1)}, bf16[4,32,4224]{2,1,0:T(8,128)(2,1)}, u32[]{:S(2)}, u32[]{:S(2)}) collective-permute-start(bf16[4,32,4224]{2,1,0:T(8,128)(2,1)S(1)} %pad_maximum_fusion.1.refs_0_), channel_id=1, source_target_pairs={{0,16},{16,0},{1,17},{17,1},{2,18},{18,2},{3,19},{19,3},{4,20},{20... | collective-permute-start | bytes 3244040 | tf_op jit(solution)/shard_map/ppermute | solution.py:32
  75.2 198.7 %reduce-scatter.3.cloned.1.call-start = ((), (), s32[]{:S(2)}) async-start(), calls=%async_computation.2 | async-start | bytes 2621440 | tf_op jit(solution)/shard_map/reduce_scatter | solution.py:63
  107.1 24.5 %collective-permute-start.15 = (bf16[4,64,2048]{2,1,0:T(8,128)(2,1)}, bf16[4,64,2048]{2,1,0:T(8,128)(2,1)}, u32[]{:S(2)}, u32[]{:S(2)}) collective-permute-start(bf16[4,64,2048]{2,1,0:T(8,128)(2,1)} %bitcast.25.refs_0_), channel_id=1, source_target_pairs={{0,16},{16,0},{1,17},{17,1},{2,18},{18,2},{3,19},{19,3},{4,20},{20... | collective-permute-start | bytes 3145736 | tf_op jit(solution)/shard_map/ppermute | solution.py:32
  108.4 24.2 %collective-permute-start.16 = (bf16[4,64,2048]{2,1,0:T(8,128)(2,1)}, bf16[4,64,2048]{2,1,0:T(8,128)(2,1)}, u32[]{:S(2)}, u32[]{:S(2)}) collective-permute-start(bf16[4,64,2048]{2,1,0:T(8,128)(2,1)} %bitcast.26.refs_2_), channel_id=1, source_target_pairs={{0,2},{1,3},{2,0},{3,1},{4,6},{5,7},{6,4},{7,5},{8,10},{9,11},{10,... | collective-permute-start | bytes 3145736 | tf_op jit(solution)/shard_map/ppermute | solution.py:34
  109.7 40.8 %collective-permute-start.19 = (bf16[512,1024]{1,0:T(8,128)(2,1)}, bf16[512,1024]{1,0:T(8,128)(2,1)}, u32[]{:S(2)}, u32[]{:S(2)}) collective-permute-start(bf16[512,1024]{1,0:T(8,128)(2,1)} %maximum_select_fusion.1.c0.ct_ref), channel_id=1, source_target_pairs={{0,1},{1,0},{2,3},{3,2},{4,5},{5,4},{6,7},{7,6},{8,9},{9,8},{10,11... | collective-permute-start | bytes 3145736 | tf_op jit(solution)/shard_map/ppermute | solution.py:34
  134.3 25.6 %collective-permute-start.17 = (bf16[8,64,1024]{2,1,0:T(8,128)(2,1)S(1)}, bf16[8,64,1024]{2,1,0:T(8,128)(2,1)S(1)}, u32[]{:S(2)}, u32[]{:S(2)}) collective-permute-start(bf16[8,64,1024]{2,1,0:T(8,128)(2,1)S(1)} %bitcast.108), channel_id=1, source_target_pairs={{0,16},{16,0},{1,17},{17,1},{2,18},{18,2},{3,19},{19,3},{4,20},{20... | collective-permute-start | bytes 3145736 | tf_op jit(solution)/shard_map/ppermute | solution.py:32
  135.1 24.9 %collective-permute-start.18 = (bf16[8,64,1024]{2,1,0:T(8,128)(2,1)S(1)}, bf16[8,64,1024]{2,1,0:T(8,128)(2,1)S(1)}, u32[]{:S(2)}, u32[]{:S(2)}) collective-permute-start(bf16[8,64,1024]{2,1,0:T(8,128)(2,1)S(1)} %bitcast.106), channel_id=1, source_target_pairs={{0,2},{1,3},{2,0},{3,1},{4,6},{5,7},{6,4},{7,5},{8,10},{9,11},{10,... | collective-permute-start | bytes 3145736 | tf_op jit(solution)/shard_map/ppermute | solution.py:34
  157.6 24.9 %collective-permute-start.23 = (bf16[8,64,1024]{2,1,0:T(8,128)(2,1)S(1)}, bf16[8,64,1024]{2,1,0:T(8,128)(2,1)S(1)}, u32[]{:S(2)}, u32[]{:S(2)}) collective-permute-start(bf16[8,64,1024]{2,1,0:T(8,128)(2,1)S(1)} %get-tuple-element.307), channel_id=1, source_target_pairs={{0,16},{16,0},{1,17},{17,1},{2,18},{18,2},{3,19},{19,3},{4,20},{20... | collective-permute-start | bytes 3145736 | tf_op jit(solution)/shard_map/ppermute | solution.py:32
  159.2 23.4 %collective-permute-start.24 = (bf16[8,64,1024]{2,1,0:T(8,128)(2,1)S(1)}, bf16[8,64,1024]{2,1,0:T(8,128)(2,1)S(1)}, u32[]{:S(2)}, u32[]{:S(2)}) collective-permute-start(bf16[8,64,1024]{2,1,0:T(8,128)(2,1)S(1)} %get-tuple-element.309), channel_id=1, source_target_pairs={{0,2},{1,3},{2,0},{3,1},{4,6},{5,7},{6,4},{7,5},{8,10},{9,11},{10,... | collective-permute-start | bytes 3145736 | tf_op jit(solution)/shard_map/ppermute | solution.py:34
  200.0 31.4 %collective-permute-start.27 = (bf16[4,80,2048]{2,1,0:T(8,128)(2,1)}, bf16[4,80,2048]{2,1,0:T(8,128)(2,1)}, u32[]{:S(2)}, u32[]{:S(2)}) collective-permute-start(bf16[4,80,2048]{2,1,0:T(8,128)(2,1)} %get-tuple-element.351), channel_id=1, source_target_pairs={{0,16},{16,0},{1,17},{17,1},{2,18},{18,2},{3,19},{19,3},{4,20},{20... | collective-permute-start | bytes 3932168 | tf_op jit(solution)/shard_map/ppermute | solution.py:32
  200.7 31.1 %collective-permute-start.28 = (bf16[4,80,2048]{2,1,0:T(8,128)(2,1)}, bf16[4,80,2048]{2,1,0:T(8,128)(2,1)}, u32[]{:S(2)}, u32[]{:S(2)}) collective-permute-start(bf16[4,80,2048]{2,1,0:T(8,128)(2,1)} %get-tuple-element.353), channel_id=1, source_target_pairs={{0,2},{1,3},{2,0},{3,1},{4,6},{5,7},{6,4},{7,5},{8,10},{9,11},{10,... | collective-permute-start | bytes 3932168 | tf_op jit(solution)/shard_map/ppermute | solution.py:34
  201.8 92.7 %reduce-scatter.5.cloned.1.call-start = ((), (), s32[]{:S(2)}) async-start(), calls=%async_computation.3 | async-start | bytes 1638400 | tf_op jit(solution)/shard_map/reduce_scatter | solution.py:63
  223.5 17.0 %collective-permute-start.25 = (bf16[16,32,3072]{2,1,0:T(8,128)(2,1)}, bf16[16,32,3072]{2,1,0:T(8,128)(2,1)}, u32[]{:S(2)}, u32[]{:S(2)}) collective-permute-start(bf16[16,32,3072]{2,1,0:T(8,128)(2,1)} %get-tuple-element.361), channel_id=1, source_target_pairs={{0,1},{1,0},{2,3},{3,2},{4,5},{5,4},{6,7},{7,6},{8,9},{9,8},{10,11... | collective-permute-start | bytes 9437192 | tf_op jit(solution)/shard_map/ppermute | solution.py:34
  236.6 16.6 %collective-permute-start.30 = (bf16[2,80,2048]{2,1,0:T(8,128)(2,1)S(1)}, bf16[2,80,2048]{2,1,0:T(8,128)(2,1)S(1)}, u32[]{:S(2)}, u32[]{:S(2)}) collective-permute-start(bf16[2,80,2048]{2,1,0:T(8,128)(2,1)S(1)} %get-tuple-element.379), channel_id=1, source_target_pairs={{0,2},{1,3},{2,0},{3,1},{4,6},{5,7},{6,4},{7,5},{8,10},{9,11},{10,... | collective-permute-start | bytes 1966088 | tf_op jit(solution)/shard_map/ppermute | solution.py:34
  237.7 16.1 %collective-permute-start.31 = (bf16[2,80,2048]{2,1,0:T(8,128)(2,1)S(1)}, bf16[2,80,2048]{2,1,0:T(8,128)(2,1)S(1)}, u32[]{:S(2)}, u32[]{:S(2)}) collective-permute-start(bf16[2,80,2048]{2,1,0:T(8,128)(2,1)S(1)} %get-tuple-element.380), channel_id=1, source_target_pairs={{0,16},{16,0},{1,17},{17,1},{2,18},{18,2},{3,19},{19,3},{4,20},{20... | collective-permute-start | bytes 1966088 | tf_op jit(solution)/shard_map/ppermute | solution.py:32
  253.9 19.0 %collective-permute-start.33 = (bf16[4,32,3200]{2,1,0:T(8,128)(2,1)}, bf16[4,32,3200]{2,1,0:T(8,128)(2,1)}, u32[]{:S(2)}, u32[]{:S(2)}) collective-permute-start(bf16[4,32,3200]{2,1,0:T(8,128)(2,1)} %get-tuple-element.397), channel_id=1, source_target_pairs={{0,2},{1,3},{2,0},{3,1},{4,6},{5,7},{6,4},{7,5},{8,10},{9,11},{10,... | collective-permute-start | bytes 2457608 | tf_op jit(solution)/shard_map/ppermute | solution.py:34
  255.0 18.9 %collective-permute-start.32 = (bf16[4,32,3200]{2,1,0:T(8,128)(2,1)}, bf16[4,32,3200]{2,1,0:T(8,128)(2,1)}, u32[]{:S(2)}, u32[]{:S(2)}) collective-permute-start(bf16[4,32,3200]{2,1,0:T(8,128)(2,1)} %get-tuple-element.396), channel_id=1, source_target_pairs={{0,16},{16,0},{1,17},{17,1},{2,18},{18,2},{3,19},{19,3},{4,20},{20... | collective-permute-start | bytes 2457608 | tf_op jit(solution)/shard_map/ppermute | solution.py:32
  259.8 21.5 %collective-permute-start.29 = (bf16[512,1024]{1,0:T(8,128)(2,1)}, bf16[512,1024]{1,0:T(8,128)(2,1)S(1)}, u32[]{:S(2)}, u32[]{:S(2)}) collective-permute-start(bf16[512,1024]{1,0:T(8,128)(2,1)} %down_back.2), channel_id=1, source_target_pairs={{0,1},{1,0},{2,3},{3,2},{4,5},{5,4},{6,7},{7,6},{8,9},{9,8},{10,11... | collective-permute-start | bytes 3145736 | tf_op jit(solution)/shard_map/ppermute | solution.py:34
  291.6 15.1 %collective-permute-start.37 = (bf16[256,1024]{1,0:T(8,128)(2,1)}, bf16[256,1024]{1,0:T(8,128)(2,1)S(1)}, u32[]{:S(2)}, u32[]{:S(2)}) collective-permute-start(bf16[256,1024]{1,0:T(8,128)(2,1)} %get-tuple-element.418), channel_id=1, source_target_pairs={{0,16},{16,0},{1,17},{17,1},{2,18},{18,2},{3,19},{19,3},{4,20},{20... | collective-permute-start | bytes 1572872 | tf_op jit(solution)/shard_map/ppermute | solution.py:32
  293.4 20.2 %collective-permute-start.36 = (bf16[256,1024]{1,0:T(8,128)(2,1)}, bf16[256,1024]{1,0:T(8,128)(2,1)S(1)}, u32[]{:S(2)}, u32[]{:S(2)}) collective-permute-start(bf16[256,1024]{1,0:T(8,128)(2,1)} %get-tuple-element.417), channel_id=1, source_target_pairs={{0,16},{16,0},{1,17},{17,1},{2,18},{18,2},{3,19},{19,3},{4,20},{20... | collective-permute-start | bytes 1572872 | tf_op jit(solution)/shard_map/ppermute | solution.py:32
  296.7 19.2 %collective-permute-start.40 = (bf16[32,3200]{1,0:T(8,128)(2,1)S(1)}, bf16[32,3200]{1,0:T(8,128)(2,1)S(1)}, u32[]{:S(2)}, u32[]{:S(2)}) collective-permute-start(bf16[32,3200]{1,0:T(8,128)(2,1)S(1)} %get-tuple-element.495), channel_id=1, source_target_pairs={{0,8},{1,9},{2,10},{3,11},{4,12},{5,13},{6,14},{7,15},{8,0},{9,1},... | collective-permute-start | bytes 614408 | tf_op jit(solution)/shard_map/ppermute | solution.py:34
  299.2 16.7 %collective-permute-start.41 = (bf16[32,3200]{1,0:T(8,128)(2,1)S(1)}, bf16[32,3200]{1,0:T(8,128)(2,1)S(1)}, u32[]{:S(2)}, u32[]{:S(2)}) collective-permute-start(bf16[32,3200]{1,0:T(8,128)(2,1)S(1)} %get-tuple-element.494), channel_id=1, source_target_pairs={{0,12},{1,13},{2,14},{3,15},{4,8},{5,9},{6,10},{7,11},{8,4},{9,5},... | collective-permute-start | bytes 614408 | tf_op jit(solution)/shard_map/ppermute | solution.py:34
  300.5 15.4 %collective-permute-start.39 = (bf16[32,3200]{1,0:T(8,128)(2,1)S(1)}, bf16[32,3200]{1,0:T(8,128)(2,1)S(1)}, u32[]{:S(2)}, u32[]{:S(2)}) collective-permute-start(bf16[32,3200]{1,0:T(8,128)(2,1)S(1)} %get-tuple-element.489), channel_id=1, source_target_pairs={{0,4},{1,5},{2,6},{3,7},{4,0},{5,1},{6,2},{7,3},{8,12},{9,13},{10,... | collective-permute-start | bytes 614408 | tf_op jit(solution)/shard_map/ppermute | solution.py:34
  (81 other events, 595.4 us)
Sparse Core Ops, SparseCore 0:
  47.9 27.2 all-gather.4
  77.4 45.4 all-gather.6
  201.9 44.3 reduce-scatter.2
  263.5 30.9 reduce-scatter.4

commit v5 on v4

--- a/solution.py
+++ b/solution.py
@@ -1205,9 +1205,9 @@
         last = ordered(c, last, jnp.zeros_like(last), 2).reshape(-1, D)
         return jnp.concatenate([one, two, last], 0)
 
+    up_stwo = up_s.two()
     sums = chain(small_lines, sums_one, sums_two, grad_shift)
     sums_in = swap(sums, 1)
-    up_stwo = up_s.two()
     attn_parts = chain(
         lambda a, b, p, q: core_sum(a, b, p, q, attn_s.rel_z), attn_keep, attn_in, sums, sums_in
     )

time: 331 us -> 330 us (level)
    ppermute x29, waiting for transfers between devices: 55.7 us -> 52.1 us  [swap(): return lax.ppermute(block, 'rows', [(i, i ^ way) for i in range(count)])]
    unnamed x132 -> x140, local copies, waits for them, and re-layouts: 26.1 us -> 25.2 us
  transfers between devices with their start and end apart: 46 -> 46, of which waited for: 26 -> 27; matrix products, arithmetic and copies ran while one was open for 7% -> 7% of each run, Pallas kernels for 34% -> 35%
where the time goes in v5:
time: 330 us; the launch traced here: 325 us
  Pallas kernels  123 us (37%)
  waiting for transfers between devices  92.5 us (28%)
  local copies, waits for them, and re-layouts  42.9 us (13%)
  starting transfers between devices  39.2 us (12%)
  between operations  14.9 us (5%)
  other arithmetic  12 us (4%)
    pallas_call x20, Pallas kernels, call(): pl.pallas_call(kernel, out_shape=outs, in_specs=[VMEM] * len(args) if spe...  81.4 us
    ppermute x29, waiting for transfers between devices, swap(): return lax.ppermute(block, 'rows', [(i, i ^ way) for i in range(count)])  52.1 us
    ppermute x13, waiting for transfers between devices, swap(): return lax.ppermute(block, 'pair', [(i, i ^ 1) for i in range(2)])  32.4 us
    unnamed x140, local copies, waits for them, and re-layouts  25.2 us
    ppermute x29, starting transfers between devices, swap(): return lax.ppermute(block, 'rows', [(i, i ^ way) for i in range(count)])  20.7 us
    ppermute x13, starting transfers between devices, swap(): return lax.ppermute(block, 'pair', [(i, i ^ 1) for i in range(2)])  18.1 us
    pallas_call x1, Pallas kernels, attention_forward(): pl.pallas_call(kernel, grid=(steps,), out_shape=[jax.ShapeDtypeStruct((2...  16 us
    pallas_call x1, Pallas kernels, attention_backward(): pl.pallas_call(kernel, grid=(steps,), out_shape=jax.ShapeDtypeStruct((3,...  15 us
  transfers between devices with their start and end apart: 46, of which 27 were waited for; matrix products, arithmetic and copies ran while one was open for 7% of the time, Pallas kernels for 35%

profile of v5, /device:TPU:0, one launch (start us, length us, event | category | flops | bytes accessed | tf_op | source)
XLA Modules:
  0.0 324.5 jit_solution(9667157436055515228)
XLA Ops:
  13.8 3.0 collective-permute-start.4
  18.4 2.6 collective-permute-start.2
  25.9 14.3 %collective-permute-done.4 = bf16[2,256,1024]{2,1,0:T(8,128)(2,1)S(1)} collective-permute-done((bf16[2,256,1024]{2,1,0:T(8,128)(2,1)}, bf16[2,256,1024]{2,1,0:T(8,128)(2,1)S(1)}, u32[]{:S(2)}, u32[]{:S(2)}) %collective-permute-start.4) | collective-permute-done | bytes 1048608 | tf_op jit(solution)/shard_map/ppermute | solution.py:32
  47.8 13.0 %collective-permute-done.5 = bf16[64,5248]{1,0:T(8,128)(2,1)S(1)} collective-permute-done((bf16[64,5248]{1,0:T(8,128)(2,1)S(1)}, bf16[64,5248]{1,0:T(8,128)(2,1)S(1)}, u32[]{:S(2)}, u32[]{:S(2)}) %collective-permute-start.5) | collective-permute-done | bytes 671776 | tf_op jit(solution)/shard_map/ppermute | solution.py:34
  69.3 5.9 %all-gather.5.cloned.1.call-done = bf16[256,2048]{1,0:T(8,128)(2,1)} async-done(((bf16[64,2048]{1,0:T(8,128)(2,1)}), bf16[256,2048]{1,0:T(8,128)(2,1)}) %all-gather.5.cloned.1.call-update) | async-done | bytes 1048592 | tf_op jit(solution)/shard_map/all_gather | solution.py:59
  77.5 9.1 %collective-permute-done.11.refs_3_ = bf16[4,32,4224]{2,1,0:T(8,128)(2,1)S(1)} collective-permute-done((bf16[4,32,4224]{2,1,0:T(8,128)(2,1)S(1)}, bf16[4,32,4224]{2,1,0:T(8,128)(2,1)S(1)}, u32[]{:S(2)}, u32[]{:S(2)}) %collective-permute-start.11) | collective-permute-done | bytes 1081376 | tf_op jit(solution)/shard_map/ppermute | solution.py:34
  93.3 4.2 %unpack.1 = (bf16[16,2,32,3072]{3,2,1,0:T(8,128)(2,1)S(1)}, bf16[16,2,32,1024]{3,2,1,0:T(8,128)(2,1)S(1)}, f32[8,1024]{1,0:T(8,128)S(1)}) custom-call(bf16[4,32,4224]{2,1,0:T(8,128)(2,1)S(1)} %pad_maximum_fusion.1.refs_0_, bf16[4,32,4224]{2,1,0:T(8,128)(2,1)} %collective-permute-done.9.refs_1_, bf16[4,32,4224]{2,1,0:T(8,128)(2,1)S(1)} %pad_maximum_fusion.2.refs_2_, ...), custom_call_target="tpu_custom_call" | custom-call | flops 1048576 | bytes 1024 | tf_op jit(solution)/shard_map/unpack/pallas_call | solution.py:567
  98.9 3.9 %project.1 = (bf16[512,1024]{1,0:T(8,128)(2,1)S(1)}, bf16[512,3072]{1,0:T(8,128)(2,1)S(1)}) custom-call(bf16[512,1024]{1,0:T(8,128)(2,1)S(1)} %copy-done.3, f32[8,1024]{1,0:T(8,128)S(1)} %get-tuple-element.365.vec_ref, bf16[1024,3072]{1,0:T(8,128)(2,1)S(1)} %bitcast.100), custom_call_target="tpu_custom_call" | custom-call | flops 1048576 | bytes 1024 | tf_op jit(solution)/shard_map/project/pallas_call | solution.py:567
  110.1 16.0 %attention_forward.1 = (bf16[512,1024]{1,0:T(8,128)(2,1)S(1)}, f32[4,4,512]{2,1,0:T(4,128)S(1)}) custom-call(s32[2]{0:T(128)S(1)} %get-tuple-element.504.phone_ref, s32[2]{0:T(128)S(1)} %get-tuple-element.505.prompt_ref, s32[2]{0:T(128)S(1)} %fusion.4.target_ref, bf16[512,3072]{1,0:T(8,128)(2,1)S(1)} %get-tuple-element.355.q_ref.k_ref.v_ref, ...), custom_call_target="tpu_custom_call" | custom-call | flops 1048576 | bytes 1024 | tf_op jit(solution)/shard_map/attention_forward/pallas_call | solution.py:456
  126.1 2.7 attend.1
  136.1 7.9 %feed_first.1 = (bf16[512,2048]{1,0:T(8,128)(2,1)S(1)}, bf16[512,2048]{1,0:T(8,128)(2,1)S(1)}, bf16[1024,2048]{1,0:T(8,128)(2,1)S(1)}) custom-call(bf16[512,1024]{1,0:T(8,128)(2,1)} %get-tuple-element.345.n_ref.n0, f32[1,2048]{1,0:T(1,128)S(1)} %reshape.138.shift_ref, bf16[4,64,2048]{2,1,0:T(8,128)(2,1)} %bitcast.25.refs_0_, ...), custom_call_target="tpu_custom_call" | custom-call | flops 34359738368 | bytes 1024 | tf_op jit(solution)/shard_map/feed_first/pallas_call | solution.py:567
  144.1 6.3 %feed_second.1 = (bf16[512,2048]{1,0:T(8,128)(2,1)S(1)}, bf16[512,2048]{1,0:T(8,128)(2,1)S(1)}) custom-call(bf16[512,1024]{1,0:T(8,128)(2,1)} %collective-permute-done.20.n_ref.n1, bf16[1024,2048]{1,0:T(8,128)(2,1)S(1)} %get-tuple-element.326.w_ref, f32[1,2048]{1,0:T(1,128)S(1)} %reshape.138.shift_ref), custom_call_target="tpu_custom_call" | custom-call | flops 1048576 | bytes 1024 | tf_op jit(solution)/shard_map/feed_second/pallas_call | solution.py:567
  150.5 7.1 %down_grad.1 = (bf16[8,64,1024]{2,1,0:T(8,128)(2,1)S(1)}, bf16[8,64,1024]{2,1,0:T(8,128)(2,1)S(1)}, bf16[8,64,1024]{2,1,0:T(8,128)(2,1)S(1)}, bf16[8,64,1024]{2,1,0:T(8,128)(2,1)S(1)}) custom-call(bf16[512,2048]{1,0:T(8,128)(2,1)S(1)} %get-tuple-element.393.a0.a_ref, bf16[512,2048]{1,0:T(8,128)(2,1)S(1)} %get-tuple-element.391.a1.a_ref, ...), custom_call_target="tpu_custom_call" | custom-call | flops 1048576 | bytes 1024 | tf_op jit(solution)/shard_map/down_grad/pallas_call | solution.py:567
  159.9 6.9 %back_act.1 = (bf16[512,2048]{1,0:T(8,128)(2,1)S(1)}, bf16[512,2048]{1,0:T(8,128)(2,1)S(1)}, f32[1,2048]{1,0:T(1,128)S(1)}, bf16[2048,1024]{1,0:T(8,128)(2,1)S(1)}) custom-call(bf16[512,1024]{1,0:T(8,128)(2,1)} %maximum_select_fusion.1.c0.ct_ref, bf16[512,1024]{1,0:T(8,128)(2,1)} %collective-permute-done.19.c1, bf16[512,2048]{1,0:T(8,128)(2,1)S(1)} %get-tuple-element.313.s0, ...), custom_call_target="tpu_custom_call" | custom-call | flops 1048576 | bytes 1024 | tf_op jit(solution)/shard_map/back_act/pallas_call | solution.py:567
  166.8 2.4 back_up.2
  169.4 2.4 back_up.3.a_ref
  173.1 4.3 %back_norm.1 = (bf16[512,1024]{1,0:T(8,128)(2,1)S(1)}, bf16[512,1024]{1,0:T(8,128)(2,1)S(1)}, f32[512,1024]{1,0:T(8,128)S(1)}, f32[2,1024]{1,0:T(2,128)S(1)}) custom-call(f32[512,1024]{1,0:T(8,128)S(1)} %back_up.3.a_ref, bf16[512,1024]{1,0:T(8,128)(2,1)S(1)} %collective-permute-done.21.b_ref, f32[512,1024]{1,0:T(8,128)S(1)} %copy-done.13, ...), custom_call_target="tpu_custom_call" | custom-call | flops 1048576 | bytes 1024 | tf_op jit(solution)/shard_map/back_norm/pallas_call | solution.py:567
  178.7 2.3 out_grad.1
  189.6 8.3 %up_grad.1 = (bf16[4,80,2048]{2,1,0:T(8,128)(2,1)}, bf16[4,80,2048]{2,1,0:T(8,128)(2,1)S(1)}, bf16[4,80,2048]{2,1,0:T(8,128)(2,1)}, bf16[4,80,2048]{2,1,0:T(8,128)(2,1)S(1)}) custom-call(bf16[512,1024]{1,0:T(8,128)(2,1)} %get-tuple-element.345.n_ref.n0, bf16[512,1024]{1,0:T(8,128)(2,1)} %collective-permute-done.20.n_ref.n1, ...), custom_call_target="tpu_custom_call" | custom-call | flops 1048576 | bytes 1024 | tf_op jit(solution)/shard_map/up_grad/pallas_call | solution.py:567
  203.3 15.0 %attention_backward.1.g_ref = bf16[3,512,1024]{2,1,0:T(8,128)(2,1)S(1)} custom-call(s32[2]{0:T(128)S(1)} %get-tuple-element.504.phone_ref, s32[2]{0:T(128)S(1)} %get-tuple-element.505.prompt_ref, s32[2]{0:T(128)S(1)} %fusion.4.target_ref, bf16[512,3072]{1,0:T(8,128)(2,1)S(1)} %get-tuple-element.355.q_ref.k_ref.v_ref, ...), custom_call_target="tpu_custom_call" | custom-call | flops 1048576 | bytes 1024 | tf_op jit(solution)/shard_map/attention_backward/pallas_call | solution.py:535
  218.3 5.2 %attn_grad.1 = (bf16[16,32,3072]{2,1,0:T(8,128)(2,1)}, bf16[16,32,3072]{2,1,0:T(8,128)(2,1)S(1)}) custom-call(bf16[512,1024]{1,0:T(8,128)(2,1)S(1)} %copy-done.27, bf16[3,512,1024]{2,1,0:T(8,128)(2,1)S(1)} %attention_backward.1.g_ref), custom_call_target="tpu_custom_call" | custom-call | flops 1048576 | bytes 1024 | tf_op jit(solution)/shard_map/attn_grad/pallas_call | solution.py:567
  223.6 5.4 %back_first.1 = (bf16[256,1024]{1,0:T(8,128)(2,1)S(1)}, bf16[256,1024]{1,0:T(8,128)(2,1)}, f32[2,1024]{1,0:T(2,128)S(1)}) custom-call(bf16[3,512,1024]{2,1,0:T(8,128)(2,1)S(1)} %attention_backward.1.g_ref, bf16[1024,3072]{1,0:T(8,128)(2,1)S(1)} %bitcast.103, bf16[512,1024]{1,0:T(8,128)(2,1)S(1)} %copy-done.5, f32[8,1024]{1,0:T(8,128)S(1)} %get-tuple-element.365.vec_ref, ...), custom_call_target="tpu_custom_call" | custom-call | flops 1048576 | bytes 1024 | tf_op jit(solution)/shard_map/back_first/pallas_call | solution.py:567
  231.8 2.9 add_halves.2
  241.9 4.5 %core_sum.1 = (bf16[4,32,3200]{2,1,0:T(8,128)(2,1)}, bf16[4,32,3200]{2,1,0:T(8,128)(2,1)S(1)}, bf16[4,32,3200]{2,1,0:T(8,128)(2,1)}, bf16[4,32,3200]{2,1,0:T(8,128)(2,1)S(1)}) custom-call(bf16[16,32,3072]{2,1,0:T(8,128)(2,1)S(1)} %get-tuple-element.383.a_ref, bf16[16,32,3072]{2,1,0:T(8,128)(2,1)} %collective-permute-done.25.b_ref, ...), custom_call_target="tpu_custom_call" | custom-call | flops 1048576 | bytes 1024 | tf_op jit(solution)/shard_map/core_sum/pallas_call | solution.py:567
  247.3 5.3 %collective-permute-done.30.b_ref = bf16[2,80,2048]{2,1,0:T(8,128)(2,1)} collective-permute-done((bf16[2,80,2048]{2,1,0:T(8,128)(2,1)}, bf16[2,80,2048]{2,1,0:T(8,128)(2,1)}, u32[]{:S(2)}, u32[]{:S(2)}) %collective-permute-start.30) | collective-permute-done | bytes 655392 | tf_op jit(solution)/shard_map/ppermute | solution.py:34
  255.8 3.3 %down_back.2 = bf16[512,1024]{1,0:T(8,128)(2,1)} custom-call(bf16[512,2048]{1,0:T(8,128)(2,1)S(1)} %copy-done.11, bf16[2048,1024]{1,0:T(8,128)(2,1)S(1)} %copy-done.7), custom_call_target="tpu_custom_call" | custom-call | flops 1048576 | bytes 1024 | tf_op jit(solution)/shard_map/down_back/pallas_call | solution.py:567
  259.1 2.3 down_back.3.a_ref
  263.8 8.4 %collective-permute-done.33.refs_5_.refs_7_ = bf16[4,32,3200]{2,1,0:T(8,128)(2,1)} collective-permute-done((bf16[4,32,3200]{2,1,0:T(8,128)(2,1)}, bf16[4,32,3200]{2,1,0:T(8,128)(2,1)}, u32[]{:S(2)}, u32[]{:S(2)}) %collective-permute-start.33) | collective-permute-done | bytes 819232 | tf_op jit(solution)/shard_map/ppermute | solution.py:34
  282.1 6.7 %collective-permute-done.34 = bf16[64,4224]{1,0:T(8,128)(2,1)S(1)} collective-permute-done((bf16[64,4224]{1,0:T(8,128)(2,1)S(1)}, bf16[64,4224]{1,0:T(8,128)(2,1)S(1)}, u32[]{:S(2)}, u32[]{:S(2)}) %collective-permute-start.34) | collective-permute-done | bytes 540704 | tf_op jit(solution)/shard_map/ppermute | solution.py:34
  288.8 2.4 collective-permute-done.35
  303.7 2.5 collective-permute-done.37.d_ref
  306.2 6.1 %collective-permute-done.36.b_ref = bf16[256,1024]{1,0:T(8,128)(2,1)S(1)} collective-permute-done((bf16[256,1024]{1,0:T(8,128)(2,1)}, bf16[256,1024]{1,0:T(8,128)(2,1)S(1)}, u32[]{:S(2)}, u32[]{:S(2)}) %collective-permute-start.36) | collective-permute-done | bytes 524320 | tf_op jit(solution)/shard_map/ppermute | solution.py:32
  (298 shorter events, 117.1 us)
Async XLA Ops:
  7.2 68.0 %all-gather.5.cloned.1.call-start = ((), (), s32[]{:S(2)}) async-start(), calls=%async_computation.4 | async-start | bytes 1310720 | tf_op jit(solution)/shard_map/all_gather | solution.py:59
  13.8 26.3 %collective-permute-start.4 = (bf16[2,256,1024]{2,1,0:T(8,128)(2,1)}, bf16[2,256,1024]{2,1,0:T(8,128)(2,1)S(1)}, u32[]{:S(2)}, u32[]{:S(2)}) collective-permute-start(bf16[2,256,1024]{2,1,0:T(8,128)(2,1)} %pad_maximum_fusion.3), channel_id=1, source_target_pairs={{0,16},{16,0},{1,17},{17,1},{2,18},{18,2},{3,19},{19,3},{4,20},{20... | collective-permute-start | bytes 3145736 | tf_op jit(solution)/shard_map/ppermute | solution.py:32
  16.8 26.4 %collective-permute-start.1 = (bf16[1,32,4224]{2,1,0:T(8,128)(2,1)S(1)}, bf16[1,32,4224]{2,1,0:T(8,128)(2,1)S(1)}, u32[]{:S(2)}, u32[]{:S(2)}) collective-permute-start(bf16[1,32,4224]{2,1,0:T(8,128)(2,1)S(1)} %bitcast.110), channel_id=1, source_target_pairs={{0,4},{1,5},{2,6},{3,7},{4,0},{5,1},{6,2},{7,3},{8,12},{9,13},{10,... | collective-permute-start | bytes 811016 | tf_op jit(solution)/shard_map/ppermute | solution.py:34
  18.4 24.9 %collective-permute-start.2 = (bf16[1,32,4224]{2,1,0:T(8,128)(2,1)S(1)}, bf16[1,32,4224]{2,1,0:T(8,128)(2,1)S(1)}, u32[]{:S(2)}, u32[]{:S(2)}) collective-permute-start(bf16[1,32,4224]{2,1,0:T(8,128)(2,1)S(1)} %bitcast.111), channel_id=1, source_target_pairs={{0,8},{1,9},{2,10},{3,11},{4,12},{5,13},{6,14},{7,15},{8,0},{9,1},... | collective-permute-start | bytes 811016 | tf_op jit(solution)/shard_map/ppermute | solution.py:34
  20.9 22.3 %collective-permute-start.3 = (bf16[1,32,4224]{2,1,0:T(8,128)(2,1)S(1)}, bf16[1,32,4224]{2,1,0:T(8,128)(2,1)}, u32[]{:S(2)}, u32[]{:S(2)}) collective-permute-start(bf16[1,32,4224]{2,1,0:T(8,128)(2,1)S(1)} %bitcast.112), channel_id=1, source_target_pairs={{0,12},{1,13},{2,14},{3,15},{4,8},{5,9},{6,10},{7,11},{8,4},{9,5},... | collective-permute-start | bytes 811016 | tf_op jit(solution)/shard_map/ppermute | solution.py:34
  44.4 16.3 %collective-permute-start.5 = (bf16[64,5248]{1,0:T(8,128)(2,1)S(1)}, bf16[64,5248]{1,0:T(8,128)(2,1)S(1)}, u32[]{:S(2)}, u32[]{:S(2)}) collective-permute-start(bf16[64,5248]{1,0:T(8,128)(2,1)S(1)} %pad_maximum_fusion.4), channel_id=1, source_target_pairs={{0,2},{1,3},{2,0},{3,1},{4,6},{5,7},{6,4},{7,5},{8,10},{9,11},{10,... | collective-permute-start | bytes 2015240 | tf_op jit(solution)/shard_map/ppermute | solution.py:34
  46.2 15.7 %collective-permute-start.6 = (bf16[64,5248]{1,0:T(8,128)(2,1)S(1)}, bf16[64,5248]{1,0:T(8,128)(2,1)S(1)}, u32[]{:S(2)}, u32[]{:S(2)}) collective-permute-start(bf16[64,5248]{1,0:T(8,128)(2,1)S(1)} %pad_maximum_fusion.5), channel_id=1, source_target_pairs={{0,16},{16,0},{1,17},{17,1},{2,18},{18,2},{3,19},{19,3},{4,20},{20... | collective-permute-start | bytes 2015240 | tf_op jit(solution)/shard_map/ppermute | solution.py:32
  47.8 82.8 %all-gather.7.cloned.1.call-start = ((), (), s32[]{:S(2)}) async-start(), calls=%async_computation.5 | async-start | bytes 2621440 | tf_op jit(solution)/shard_map/all_gather | solution.py:59
  62.9 23.7 %collective-permute-start.11 = (bf16[4,32,4224]{2,1,0:T(8,128)(2,1)S(1)}, bf16[4,32,4224]{2,1,0:T(8,128)(2,1)S(1)}, u32[]{:S(2)}, u32[]{:S(2)}) collective-permute-start(bf16[4,32,4224]{2,1,0:T(8,128)(2,1)S(1)} %pad_maximum_fusion.2.refs_2_), channel_id=1, source_target_pairs={{0,2},{1,3},{2,0},{3,1},{4,6},{5,7},{6,4},{7,5},{8,10},{9,11},{10,... | collective-permute-start | bytes 3244040 | tf_op jit(solution)/shard_map/ppermute | solution.py:34
  64.1 23.8 %collective-permute-start.9 = (bf16[4,32,4224]{2,1,0:T(8,128)(2,1)S(1)}, bf16[4,32,4224]{2,1,0:T(8,128)(2,1)}, u32[]{:S(2)}, u32[]{:S(2)}) collective-permute-start(bf16[4,32,4224]{2,1,0:T(8,128)(2,1)S(1)} %pad_maximum_fusion.1.refs_0_), channel_id=1, source_target_pairs={{0,16},{16,0},{1,17},{17,1},{2,18},{18,2},{3,19},{19,3},{4,20},{20... | collective-permute-start | bytes 3244040 | tf_op jit(solution)/shard_map/ppermute | solution.py:32
  75.2 197.4 %reduce-scatter.3.cloned.1.call-start = ((), (), s32[]{:S(2)}) async-start(), calls=%async_computation.2 | async-start | bytes 2621440 | tf_op jit(solution)/shard_map/reduce_scatter | solution.py:63
  107.1 24.5 %collective-permute-start.15 = (bf16[4,64,2048]{2,1,0:T(8,128)(2,1)}, bf16[4,64,2048]{2,1,0:T(8,128)(2,1)}, u32[]{:S(2)}, u32[]{:S(2)}) collective-permute-start(bf16[4,64,2048]{2,1,0:T(8,128)(2,1)} %bitcast.25.refs_0_), channel_id=1, source_target_pairs={{0,16},{16,0},{1,17},{17,1},{2,18},{18,2},{3,19},{19,3},{4,20},{20... | collective-permute-start | bytes 3145736 | tf_op jit(solution)/shard_map/ppermute | solution.py:32
  108.4 24.2 %collective-permute-start.16 = (bf16[4,64,2048]{2,1,0:T(8,128)(2,1)}, bf16[4,64,2048]{2,1,0:T(8,128)(2,1)}, u32[]{:S(2)}, u32[]{:S(2)}) collective-permute-start(bf16[4,64,2048]{2,1,0:T(8,128)(2,1)} %bitcast.26.refs_2_), channel_id=1, source_target_pairs={{0,2},{1,3},{2,0},{3,1},{4,6},{5,7},{6,4},{7,5},{8,10},{9,11},{10,... | collective-permute-start | bytes 3145736 | tf_op jit(solution)/shard_map/ppermute | solution.py:34
  109.7 40.8 %collective-permute-start.19 = (bf16[512,1024]{1,0:T(8,128)(2,1)}, bf16[512,1024]{1,0:T(8,128)(2,1)}, u32[]{:S(2)}, u32[]{:S(2)}) collective-permute-start(bf16[512,1024]{1,0:T(8,128)(2,1)} %maximum_select_fusion.1.c0.ct_ref), channel_id=1, source_target_pairs={{0,1},{1,0},{2,3},{3,2},{4,5},{5,4},{6,7},{7,6},{8,9},{9,8},{10,11... | collective-permute-start | bytes 3145736 | tf_op jit(solution)/shard_map/ppermute | solution.py:34
  134.3 25.6 %collective-permute-start.17 = (bf16[8,64,1024]{2,1,0:T(8,128)(2,1)S(1)}, bf16[8,64,1024]{2,1,0:T(8,128)(2,1)S(1)}, u32[]{:S(2)}, u32[]{:S(2)}) collective-permute-start(bf16[8,64,1024]{2,1,0:T(8,128)(2,1)S(1)} %bitcast.108), channel_id=1, source_target_pairs={{0,16},{16,0},{1,17},{17,1},{2,18},{18,2},{3,19},{19,3},{4,20},{20... | collective-permute-start | bytes 3145736 | tf_op jit(solution)/shard_map/ppermute | solution.py:32
  135.1 24.9 %collective-permute-start.18 = (bf16[8,64,1024]{2,1,0:T(8,128)(2,1)S(1)}, bf16[8,64,1024]{2,1,0:T(8,128)(2,1)S(1)}, u32[]{:S(2)}, u32[]{:S(2)}) collective-permute-start(bf16[8,64,1024]{2,1,0:T(8,128)(2,1)S(1)} %bitcast.106), channel_id=1, source_target_pairs={{0,2},{1,3},{2,0},{3,1},{4,6},{5,7},{6,4},{7,5},{8,10},{9,11},{10,... | collective-permute-start | bytes 3145736 | tf_op jit(solution)/shard_map/ppermute | solution.py:34
  157.6 25.0 %collective-permute-start.23 = (bf16[8,64,1024]{2,1,0:T(8,128)(2,1)S(1)}, bf16[8,64,1024]{2,1,0:T(8,128)(2,1)S(1)}, u32[]{:S(2)}, u32[]{:S(2)}) collective-permute-start(bf16[8,64,1024]{2,1,0:T(8,128)(2,1)S(1)} %get-tuple-element.307), channel_id=1, source_target_pairs={{0,16},{16,0},{1,17},{17,1},{2,18},{18,2},{3,19},{19,3},{4,20},{20... | collective-permute-start | bytes 3145736 | tf_op jit(solution)/shard_map/ppermute | solution.py:32
  159.2 23.4 %collective-permute-start.24 = (bf16[8,64,1024]{2,1,0:T(8,128)(2,1)S(1)}, bf16[8,64,1024]{2,1,0:T(8,128)(2,1)S(1)}, u32[]{:S(2)}, u32[]{:S(2)}) collective-permute-start(bf16[8,64,1024]{2,1,0:T(8,128)(2,1)S(1)} %get-tuple-element.309), channel_id=1, source_target_pairs={{0,2},{1,3},{2,0},{3,1},{4,6},{5,7},{6,4},{7,5},{8,10},{9,11},{10,... | collective-permute-start | bytes 3145736 | tf_op jit(solution)/shard_map/ppermute | solution.py:34
  200.0 31.4 %collective-permute-start.26 = (bf16[4,80,2048]{2,1,0:T(8,128)(2,1)}, bf16[4,80,2048]{2,1,0:T(8,128)(2,1)}, u32[]{:S(2)}, u32[]{:S(2)}) collective-permute-start(bf16[4,80,2048]{2,1,0:T(8,128)(2,1)} %get-tuple-element.351), channel_id=1, source_target_pairs={{0,16},{16,0},{1,17},{17,1},{2,18},{18,2},{3,19},{19,3},{4,20},{20... | collective-permute-start | bytes 3932168 | tf_op jit(solution)/shard_map/ppermute | solution.py:32
  200.7 31.1 %collective-permute-start.27 = (bf16[4,80,2048]{2,1,0:T(8,128)(2,1)}, bf16[4,80,2048]{2,1,0:T(8,128)(2,1)}, u32[]{:S(2)}, u32[]{:S(2)}) collective-permute-start(bf16[4,80,2048]{2,1,0:T(8,128)(2,1)} %get-tuple-element.353), channel_id=1, source_target_pairs={{0,2},{1,3},{2,0},{3,1},{4,6},{5,7},{6,4},{7,5},{8,10},{9,11},{10,... | collective-permute-start | bytes 3932168 | tf_op jit(solution)/shard_map/ppermute | solution.py:34
  201.8 93.5 %reduce-scatter.5.cloned.1.call-start = ((), (), s32[]{:S(2)}) async-start(), calls=%async_computation.3 | async-start | bytes 1638400 | tf_op jit(solution)/shard_map/reduce_scatter | solution.py:63
  223.5 18.3 %collective-permute-start.25 = (bf16[16,32,3072]{2,1,0:T(8,128)(2,1)}, bf16[16,32,3072]{2,1,0:T(8,128)(2,1)}, u32[]{:S(2)}, u32[]{:S(2)}) collective-permute-start(bf16[16,32,3072]{2,1,0:T(8,128)(2,1)} %get-tuple-element.361), channel_id=1, source_target_pairs={{0,1},{1,0},{2,3},{3,2},{4,5},{5,4},{6,7},{7,6},{8,9},{9,8},{10,11... | collective-permute-start | bytes 9437192 | tf_op jit(solution)/shard_map/ppermute | solution.py:34
  236.4 16.2 %collective-permute-start.30 = (bf16[2,80,2048]{2,1,0:T(8,128)(2,1)}, bf16[2,80,2048]{2,1,0:T(8,128)(2,1)}, u32[]{:S(2)}, u32[]{:S(2)}) collective-permute-start(bf16[2,80,2048]{2,1,0:T(8,128)(2,1)} %get-tuple-element.376), channel_id=1, source_target_pairs={{0,2},{1,3},{2,0},{3,1},{4,6},{5,7},{6,4},{7,5},{8,10},{9,11},{10,... | collective-permute-start | bytes 1966088 | tf_op jit(solution)/shard_map/ppermute | solution.py:34
  237.5 16.0 %collective-permute-start.31 = (bf16[2,80,2048]{2,1,0:T(8,128)(2,1)}, bf16[2,80,2048]{2,1,0:T(8,128)(2,1)}, u32[]{:S(2)}, u32[]{:S(2)}) collective-permute-start(bf16[2,80,2048]{2,1,0:T(8,128)(2,1)} %get-tuple-element.377), channel_id=1, source_target_pairs={{0,16},{16,0},{1,17},{17,1},{2,18},{18,2},{3,19},{19,3},{4,20},{20... | collective-permute-start | bytes 1966088 | tf_op jit(solution)/shard_map/ppermute | solution.py:32
  253.5 18.6 %collective-permute-start.33 = (bf16[4,32,3200]{2,1,0:T(8,128)(2,1)}, bf16[4,32,3200]{2,1,0:T(8,128)(2,1)}, u32[]{:S(2)}, u32[]{:S(2)}) collective-permute-start(bf16[4,32,3200]{2,1,0:T(8,128)(2,1)} %get-tuple-element.397), channel_id=1, source_target_pairs={{0,2},{1,3},{2,0},{3,1},{4,6},{5,7},{6,4},{7,5},{8,10},{9,11},{10,... | collective-permute-start | bytes 2457608 | tf_op jit(solution)/shard_map/ppermute | solution.py:34
  254.4 18.2 %collective-permute-start.32 = (bf16[4,32,3200]{2,1,0:T(8,128)(2,1)}, bf16[4,32,3200]{2,1,0:T(8,128)(2,1)}, u32[]{:S(2)}, u32[]{:S(2)}) collective-permute-start(bf16[4,32,3200]{2,1,0:T(8,128)(2,1)} %get-tuple-element.396), channel_id=1, source_target_pairs={{0,16},{16,0},{1,17},{17,1},{2,18},{18,2},{3,19},{19,3},{4,20},{20... | collective-permute-start | bytes 2457608 | tf_op jit(solution)/shard_map/ppermute | solution.py:32
  259.1 21.3 %collective-permute-start.29 = (bf16[512,1024]{1,0:T(8,128)(2,1)}, bf16[512,1024]{1,0:T(8,128)(2,1)S(1)}, u32[]{:S(2)}, u32[]{:S(2)}) collective-permute-start(bf16[512,1024]{1,0:T(8,128)(2,1)} %down_back.2), channel_id=1, source_target_pairs={{0,1},{1,0},{2,3},{3,2},{4,5},{5,4},{6,7},{7,6},{8,9},{9,8},{10,11... | collective-permute-start | bytes 3145736 | tf_op jit(solution)/shard_map/ppermute | solution.py:34
  291.2 15.1 %collective-permute-start.37 = (bf16[256,1024]{1,0:T(8,128)(2,1)}, bf16[256,1024]{1,0:T(8,128)(2,1)S(1)}, u32[]{:S(2)}, u32[]{:S(2)}) collective-permute-start(bf16[256,1024]{1,0:T(8,128)(2,1)} %get-tuple-element.418), channel_id=1, source_target_pairs={{0,16},{16,0},{1,17},{17,1},{2,18},{18,2},{3,19},{19,3},{4,20},{20... | collective-permute-start | bytes 1572872 | tf_op jit(solution)/shard_map/ppermute | solution.py:32
  292.5 19.9 %collective-permute-start.36 = (bf16[256,1024]{1,0:T(8,128)(2,1)}, bf16[256,1024]{1,0:T(8,128)(2,1)S(1)}, u32[]{:S(2)}, u32[]{:S(2)}) collective-permute-start(bf16[256,1024]{1,0:T(8,128)(2,1)} %get-tuple-element.417), channel_id=1, source_target_pairs={{0,16},{16,0},{1,17},{17,1},{2,18},{18,2},{3,19},{19,3},{4,20},{20... | collective-permute-start | bytes 1572872 | tf_op jit(solution)/shard_map/ppermute | solution.py:32
  297.5 17.0 %collective-permute-start.40 = (bf16[32,3200]{1,0:T(8,128)(2,1)S(1)}, bf16[32,3200]{1,0:T(8,128)(2,1)S(1)}, u32[]{:S(2)}, u32[]{:S(2)}) collective-permute-start(bf16[32,3200]{1,0:T(8,128)(2,1)S(1)} %get-tuple-element.495), channel_id=1, source_target_pairs={{0,8},{1,9},{2,10},{3,11},{4,12},{5,13},{6,14},{7,15},{8,0},{9,1},... | collective-permute-start | bytes 614408 | tf_op jit(solution)/shard_map/ppermute | solution.py:34
  298.8 15.7 %collective-permute-start.41 = (bf16[32,3200]{1,0:T(8,128)(2,1)S(1)}, bf16[32,3200]{1,0:T(8,128)(2,1)S(1)}, u32[]{:S(2)}, u32[]{:S(2)}) collective-permute-start(bf16[32,3200]{1,0:T(8,128)(2,1)S(1)} %get-tuple-element.494), channel_id=1, source_target_pairs={{0,12},{1,13},{2,14},{3,15},{4,8},{5,9},{6,10},{7,11},{8,4},{9,5},... | collective-permute-start | bytes 614408 | tf_op jit(solution)/shard_map/ppermute | solution.py:34
  299.8 15.6 %collective-permute-start.39 = (bf16[32,3200]{1,0:T(8,128)(2,1)S(1)}, bf16[32,3200]{1,0:T(8,128)(2,1)S(1)}, u32[]{:S(2)}, u32[]{:S(2)}) collective-permute-start(bf16[32,3200]{1,0:T(8,128)(2,1)S(1)} %get-tuple-element.489), channel_id=1, source_target_pairs={{0,4},{1,5},{2,6},{3,7},{4,0},{5,1},{6,2},{7,3},{8,12},{9,13},{10,... | collective-permute-start | bytes 614408 | tf_op jit(solution)/shard_map/ppermute | solution.py:34
  (85 other events, 604.9 us)
Sparse Core Ops, SparseCore 0:
  47.9 27.2 all-gather.4
  77.4 45.4 all-gather.6
  201.9 44.4 reduce-scatter.2
  263.9 31.4 reduce-scatter.4
